TPU v7x, 32 devices: a whole 2x2x4 slice. The times are simulated.
32 devices in a mesh: bucket: 4 (over y, x), batch: 8 (over z, core).
Axes of the slice: x: 2, y: 2, z: 4, core: 2. Of those that a mesh axis runs over, the one named last changes fastest.
Arguments:
- images: float32 [8, 4, 5, 256, 256], P('batch', 'bucket'), may hold values from -6 to 6
- timesteps: int32 [8, 4, 5], P('batch', 'bucket'), may hold values from 0 to 999, as said below
- counts: int32 [8, 4], P('batch', 'bucket'), may hold values from 3 to 5, as said below
- source: int32 [8, 4], P('batch', 'bucket'), may hold values from 0 to 3, as said below
- cotangent: float32 [8, 4, 4, 256, 256], P('batch', 'bucket'), may hold values from -6 to 6
- first_gain: float32 [256], replicated, may hold values from 0.25 to 1.75
- first_shift: float32 [256], replicated, may hold values from -1.8 to 1.8
- first_conv: float32 [3, 3, 256, 256], replicated, may hold values from -0.125 to 0.125
- embed_weight: float32 [512, 256], replicated, may hold values from -0.25 to 0.25
- embed_bias: float32 [256], replicated, may hold values from -1.8 to 1.8
- second_gain: float32 [256], replicated, may hold values from 0.25 to 1.75
- second_shift: float32 [256], replicated, may hold values from -1.8 to 1.8
- second_conv: float32 [3, 3, 256, 256], replicated, may hold values from -0.125 to 0.125
- second_bias: float32 [256], replicated, may hold values from -1.8 to 1.8
- attend_gain: float32 [256], replicated, may hold values from 0.25 to 1.75
- attend_shift: float32 [256], replicated, may hold values from -1.8 to 1.8
- triple_weight: float32 [256, 768], replicated, may hold values from -0.375 to 0.375
- query_bias: float32 [256], replicated, may hold values from -1.8 to 1.8
- value_bias: float32 [256], replicated, may hold values from -1.8 to 1.8
- output_weight: float32 [256, 256], replicated, may hold values from -1.5 to 1.5
- output_bias: float32 [256], replicated, may hold values from -1.8 to 1.8
Outputs:
- output: float32 [8, 4, 4, 256, 256], P('batch', 'bucket')
- image_gradient: float32 [8, 4, 5, 256, 256], P('batch', 'bucket')
- first_gain_gradient: float32 [256], replicated
- first_shift_gradient: float32 [256], replicated
- first_conv_gradient: float32 [3, 3, 256, 256], replicated
- embed_weight_gradient: float32 [512, 256], replicated
- embed_bias_gradient: float32 [256], replicated
- second_gain_gradient: float32 [256], replicated
- second_shift_gradient: float32 [256], replicated
- second_conv_gradient: float32 [3, 3, 256, 256], replicated
- second_bias_gradient: float32 [256], replicated
- attend_gain_gradient: float32 [256], replicated
- attend_shift_gradient: float32 [256], replicated
- triple_weight_gradient: float32 [256, 768], replicated
- query_bias_gradient: float32 [256], replicated
- value_bias_gradient: float32 [256], replicated
- output_weight_gradient: float32 [256, 256], replicated
- output_bias_gradient: float32 [256], replicated
Inputs may be any that keep to these rules, and one draw needn't show every extreme that they name: Each device holds 4 images, one fewer, or one more; in each batch column the counts add up to 4 times 4, as many devices hold one more as hold one fewer, and at least a third of the column's devices, rounded up, hold one more. `source`: A device holding one image fewer than 4 names a device of its batch column that holds one more, each of those named by exactly one device; every other device names its own bucket index. Images of bucket index b have timesteps from the integer part of b * 250 up to, but excluding, that of (b + 1) * 250.
All inputs are finite; a program needn't handle non-finite values.
Results may differ from a plain program's by a relative error of at most 0.014.
The roundings to bfloat16 on the way count: a program that leaves them out, or rounds other values in their place, can miss the bound.
Values sent between devices are 32-bit elements; how exact they have to be, the bound alone decides.
No kernel may reach another device: no remote copies, remote signals or barrier semaphores. Data moves between devices by JAX's collectives and lax.ppermute only.
A program may use at most 128 MiB of HBM per device.

v0:
```python
import math

import jax
import jax.numpy as jnp
from jax import lax
from jax.experimental import pallas as pl
from jax.experimental.pallas import tpu as pltpu
from jax.sharding import PartitionSpec as P

TEMB = 512
GROUPS = 32
SIDE = 16
WORK = 4
TOK = SIDE * SIDE
C = 256
PAD = TOK + 2 * SIDE
EPSILON = 1e-06
COUNT = float(TOK * (C // GROUPS))
CHUNK = 64
F32 = jnp.float32
BF16 = jnp.bfloat16
VMEM_LIMIT = 56 * 1024 * 1024
NT = (((1,), (1,)), ((), ()))
TN = (((0,), (0,)), ((), ()))

R_OUT_BIAS, R_QUERY_BIAS, R_VALUE_BIAS, R_ATT_GAIN, R_ATT_SHIFT, R_SEC_BIAS = 0, 1, 2, 3, 4, 5
R_SEC_GAIN, R_SEC_SHIFT, R_EMB_BIAS, R_FIRST_GAIN, R_FIRST_SHIFT = 6, 7, 8, 9, 10
SUMS = 16


def dot(a, b, dims=(((1,), (0,)), ((), ()))):
    return lax.dot_general(a, b, dims, preferred_element_type=F32)


def sigmoid(v):
    return 0.5 * jnp.tanh(0.5 * v) + 0.5


def group_matrix():
    row = lax.broadcasted_iota(jnp.int32, (C, C), 0) // (C // GROUPS)
    col = lax.broadcasted_iota(jnp.int32, (C, C), 1) // (C // GROUPS)
    return (row == col).astype(F32).astype(BF16)


def group_mean(sums, same):
    high = sums.astype(BF16).astype(F32)
    rest = sums - high
    mid = rest.astype(BF16).astype(F32)
    low = rest - mid
    total = dot(jnp.concatenate([high, mid, low], axis=0).astype(BF16), same)
    return (total[0:8] + total[8:16] + total[16:24]) * (1.0 / COUNT)


def over_chunks(count, body):
    steps = TOK // CHUNK

    def step(i, carry):
        body(i // steps, pl.multiple_of((i % steps) * CHUNK, CHUNK))
        return carry

    lax.fori_loop(0, count * steps, step, 0)


def fold(v):
    return jnp.sum(v.reshape(v.shape[0] // 8, 8, v.shape[1]), axis=0)


def column_sums(count, parts, body, hold):
    hold[0 : parts * count] = jnp.zeros((parts * count, 8, C), F32)

    def step(image, row):
        for part, v in enumerate(body(image, row)):
            hold[part * count + image] += fold(v)

    over_chunks(count, step)
    return gather_sums(count, parts, hold)


def gather_sums(count, parts, hold):
    out = []
    for part in range(parts):
        rows = [jnp.sum(hold[part * count + i], axis=0, keepdims=True) for i in range(count)]
        out.append(jnp.concatenate(rows + [jnp.zeros((8 - count, C), F32)], axis=0))
    return out


def edge_masks():
    column = lax.broadcasted_iota(jnp.int32, (CHUNK, C), 0) % SIDE
    return column == 0, column == SIDE - 1


def store_shifted(ref, image, row, v, backward):
    first, last = edge_masks()
    before = jnp.where(first, 0.0, pltpu.roll(v, 1, 0)).astype(BF16)
    after = jnp.where(last, 0.0, pltpu.roll(v, CHUNK - 1, 0)).astype(BF16)
    rows = pl.ds(row + SIDE, CHUNK)
    left, right = (after, before) if backward else (before, after)
    ref[image, rows, 0:C] = left
    ref[image, rows, C : 2 * C] = v.astype(BF16)
    ref[image, rows, 2 * C : 3 * C] = right


def clear_borders(ref, count):
    for i in range(count):
        ref[i, 0:SIDE, :] = jnp.zeros((SIDE, 3 * C), BF16)
        ref[i, PAD - SIDE : PAD, :] = jnp.zeros((SIDE, 3 * C), BF16)


def window(ref, count, di):
    return ref[0:count, SIDE * di : SIDE * di + TOK, :].reshape(count * TOK, 3 * C)


def norm_stats(count, ref, hold, same):
    (sums,) = column_sums(count, 1, lambda i, r: (ref[i, pl.ds(r, CHUNK), :],), hold)
    return sums_to_stats(count, sums, ref, hold, same)


def sums_to_stats(count, sums, ref, hold, same):
    mean = group_mean(sums, same)
    hold_mean = hold.at[hold.shape[0] - 1]
    hold_mean[...] = mean

    def squares(i, r):
        d = ref[i, pl.ds(r, CHUNK), :] - hold_mean[pl.ds(i, 1), :]
        return (d * d,)

    (second,) = column_sums(count, 1, squares, hold)
    return mean, lax.rsqrt(group_mean(second, same) + EPSILON)


def front(
    count, x, cot, times, w, out, dmid, out1, act1, act2, stats, sums, g_triple, g_out,
    shifted, hold, mid, normed, triple, mixed, dmixed, dtriple, dnormed, same_ref, accumulate,
):
    same = same_ref[...]

    def vec(name):
        return w[name][...]

    mean, scale = norm_stats(count, x, hold, same)
    for i in range(count):
        stats[i, 0:1, :] = mean[i : i + 1]
        stats[i, 1:2, :] = scale[i : i + 1]
    clear_borders(shifted, count)
    gain, shift = vec("first_gain"), vec("first_shift")

    def first(i, r):
        rows = pl.ds(r, CHUNK)
        pre = (x[i, rows, :] - stats[i, 0:1, :]) * stats[i, 1:2, :] * gain + shift
        act = pre * sigmoid(pre)
        act1[i, rows, :] = act.astype(BF16)
        store_shifted(shifted, i, r, act, False)

    over_chunks(count, first)

    half = TEMB // 2
    lane = lax.broadcasted_iota(jnp.int32, (8, half), 1).astype(F32)
    row = lax.broadcasted_iota(jnp.int32, (8, half), 0)
    frequency = jnp.exp(lane * (-math.log(10000.0) / (half - 1)))
    clock = jnp.zeros((8, half), F32)
    for i in range(count):
        clock = jnp.where(row == i, times[i], clock)
    angles = clock * frequency
    waves = jnp.concatenate([jnp.sin(angles), jnp.cos(angles)], axis=1)
    waves = waves * sigmoid(waves)
    stepped = lax.dot_general(
        waves, w["embed_weight"][...], (((1,), (0,)), ((), ())),
        precision=lax.Precision.HIGHEST, preferred_element_type=F32,
    ) + vec("embed_bias")

    kernel = w["first_conv"]
    conv = None
    for di in range(3):
        part = dot(window(shifted, count, di), kernel[di].reshape(3 * C, C).astype(BF16))
        conv = part if conv is None else conv + part
    for i in range(count):
        out1[i] = conv[i * TOK : (i + 1) * TOK] + stepped[i : i + 1]

    mean, scale = norm_stats(count, out1, hold, same)
    for i in range(count):
        stats[i, 2:3, :] = mean[i : i + 1]
        stats[i, 3:4, :] = scale[i : i + 1]
    gain2, shift2 = vec("second_gain"), vec("second_shift")

    def second(i, r):
        rows = pl.ds(r, CHUNK)
        pre = (out1[i, rows, :] - stats[i, 2:3, :]) * stats[i, 3:4, :] * gain2 + shift2
        act = pre * sigmoid(pre)
        act2[i, rows, :] = act.astype(BF16)
        store_shifted(shifted, i, r, act, False)

    over_chunks(count, second)
    kernel = w["second_conv"]
    conv = None
    for di in range(3):
        part = dot(window(shifted, count, di), kernel[di].reshape(3 * C, C).astype(BF16))
        conv = part if conv is None else conv + part
    bias = vec("second_bias")
    for i in range(count):
        mid[i] = conv[i * TOK : (i + 1) * TOK] + x[i] + bias

    mean, scale = norm_stats(count, mid, hold, same)
    for i in range(count):
        stats[i, 4:5, :] = mean[i : i + 1]
        stats[i, 5:6, :] = scale[i : i + 1]
    gain3, shift3 = vec("attend_gain"), vec("attend_shift")

    def third(i, r):
        rows = pl.ds(r, CHUNK)
        pre = (mid[i, rows, :] - stats[i, 4:5, :]) * stats[i, 5:6, :] * gain3 + shift3
        normed[i, rows, :] = pre.astype(BF16)

    over_chunks(count, third)
    flat = normed[0:count].reshape(count * TOK, C)
    w_triple = w["triple_weight"][...].astype(BF16)
    w_out = w["output_weight"][...].astype(BF16)
    for part, name in enumerate(("query_bias", None, "value_bias")):
        v = dot(flat, w_triple[:, part * C : (part + 1) * C])
        if name is not None:
            v = v + vec(name)
        triple[0:count, :, part * C : (part + 1) * C] = v.astype(BF16).reshape(count, TOK, C)

    cot_low = cot[0:count].reshape(count * TOK, C).astype(BF16)
    dmixed[0:count] = dot(cot_low, w_out, NT).astype(BF16).reshape(count, TOK, C)

    factor = 1.0 / math.sqrt(C)
    query_sum = jnp.zeros((1, C), F32)
    value_sum = jnp.zeros((1, C), F32)
    for i in range(count):
        q = triple[i, :, 0:C]
        k = triple[i, :, C : 2 * C]
        v = triple[i, :, 2 * C : 3 * C]
        dm = dmixed[i]
        s = dot(q, k, NT) * factor
        e = jnp.exp(s - jnp.max(s, axis=1, keepdims=True))
        p = e * (1.0 / jnp.sum(e, axis=1, keepdims=True))
        p_low = p.astype(BF16)
        mixed[i] = dot(p_low, v).astype(BF16)
        dp = dot(dm, v, NT)
        ds = (p * (dp - jnp.sum(p * dp, axis=1, keepdims=True))).astype(BF16)
        dq = dot(ds, k) * factor
        dk = dot(ds, q, TN) * factor
        dv = dot(p_low, dm, TN)
        query_sum = query_sum + jnp.sum(dq, axis=0, keepdims=True)
        value_sum = value_sum + jnp.sum(dv, axis=0, keepdims=True)
        dtriple[i, :, 0:C] = dq.astype(BF16)
        dtriple[i, :, C : 2 * C] = dk.astype(BF16)
        dtriple[i, :, 2 * C : 3 * C] = dv.astype(BF16)

    flat_mixed = mixed[0:count].reshape(count * TOK, C)
    projected = dot(flat_mixed, w_out)
    bias = vec("output_bias")
    for i in range(count):
        out[i] = mid[i] + projected[i * TOK : (i + 1) * TOK] + bias
    flat_d = dtriple[0:count].reshape(count * TOK, 3 * C)
    gw_out = dot(flat_mixed, cot_low, TN)
    gw_triple = dot(flat, flat_d, TN)
    if accumulate is None:
        g_out[...] = gw_out
        g_triple[...] = gw_triple
    else:
        accumulate(gw_out, gw_triple)
    dn = dot(flat_d, w_triple, NT)
    dnormed[0:count] = dn.reshape(count, TOK, C)

    def sums3(i, r):
        rows = pl.ds(r, CHUNK)
        d = dnormed[i, rows, :]
        unit = (mid[i, rows, :] - stats[i, 4:5, :]) * stats[i, 5:6, :]
        return d, d * unit, cot[i, rows, :]

    sum_d, sum_du, sum_cot = column_sums(count, 3, sums3, hold)
    first_mean = group_mean(sum_d * gain3, same)
    second_mean = group_mean(sum_du * gain3, same)
    hold[hold.shape[0] - 1] = first_mean
    hold[hold.shape[0] - 2] = second_mean

    def inner3(i, r):
        rows = pl.ds(r, CHUNK)
        d = dnormed[i, rows, :] * gain3
        scaled = stats[i, 5:6, :]
        unit = (mid[i, rows, :] - stats[i, 4:5, :]) * scaled
        m1 = hold[hold.shape[0] - 1, pl.ds(i, 1), :]
        m2 = hold[hold.shape[0] - 2, pl.ds(i, 1), :]
        g = (d - m1 - unit * m2) * scaled + cot[i, rows, :]
        dmid[i, rows, :] = g
        return (g,)

    (sum_mid,) = column_sums(count, 1, inner3, hold)
    pieces = [
        jnp.sum(sum_cot, axis=0, keepdims=True), query_sum, value_sum,
        jnp.sum(sum_du, axis=0, keepdims=True), jnp.sum(sum_d, axis=0, keepdims=True),
        jnp.sum(sum_mid, axis=0, keepdims=True),
    ]
    return pieces


WEIGHTS = (
    "first_gain", "first_shift", "first_conv", "embed_weight", "embed_bias", "second_gain", "second_shift",
    "second_conv", "second_bias", "attend_gain", "attend_shift", "triple_weight", "query_bias", "value_bias",
    "output_weight", "output_bias",
)


def front_scratch(count):
    return [
        pltpu.VMEM((count, PAD, 3 * C), BF16),
        pltpu.VMEM((16, 8, C), F32),
        pltpu.VMEM((count, TOK, C), F32),
        pltpu.VMEM((count, TOK, C), BF16),
        pltpu.VMEM((count, TOK, 3 * C), BF16),
        pltpu.VMEM((count, TOK, C), BF16),
        pltpu.VMEM((count, TOK, C), BF16),
        pltpu.VMEM((count, TOK, 3 * C), BF16),
        pltpu.VMEM((count, TOK, C), F32),
        pltpu.VMEM((C, C), BF16),
    ]


def store_sums(sums, pieces, before=None):
    sums[...] = jnp.zeros((SUMS, C), F32) if before is None else before[...]
    for r, piece in enumerate(pieces):
        sums[r : r + 1, :] += piece


def kernel_one(times, x, cot, *rest):
    w = dict(zip(WEIGHTS, rest[:16]))
    out, dmid, out1, act1, act2, stats, sums, g_triple, g_out = rest[16:25]
    scratch = rest[25:]
    scratch[-1][...] = group_matrix()
    moments = [times[0, 0, i].astype(F32) for i in range(WORK - 1)]
    pieces = front(
        WORK - 1, x, cot, moments, w, out, dmid, out1, act1, act2, stats, sums, g_triple, g_out, *scratch, None
    )
    store_sums(sums, pieces)


def owner_codes(mesh_shape):
    b, t = lax.axis_index("bucket"), lax.axis_index("batch")
    x, y = b % 2, (b // 2) % 2
    core, z = t % 2, (t // 2) % 2
    return core, x * 4 + y * 2 + z, z * 4 + x * 2 + y


def scatter_unit(dst, unit, value, codes):
    core, even, odd = codes
    for block in range(16):
        half, low = divmod(block, 8)
        mine = jnp.where(core == half, 0, 1)
        code = even if half == 0 else odd
        dst[mine * 8 + (low ^ code), unit] = value[16 * block : 16 * block + 16]


def kernel_two(times, extra, counts, x, cot, *rest):
    w = dict(zip(WEIGHTS, rest[:16]))
    (mid_in, act2_in, sums_in, gt_in, go_in, _o, _a, _d, _s) = rest[16:25]
    out, dmid, out1, act1, act2, stats, sums, blocks = rest[25:33]
    scratch = rest[33:43]
    full_act, full_shift = rest[43:]
    same = scratch[-1]
    same[...] = group_matrix()
    moment = jnp.where(counts[0, 0] >= WORK, times[0, 0, WORK - 1].astype(F32), extra[0, 0])
    codes = owner_codes(None)

    def accumulate(gw_out, gw_triple):
        scatter_unit(blocks, 12, gw_out + go_in[...], codes)
        total = gw_triple + gt_in[...]
        for part in range(3):
            scatter_unit(blocks, 9 + part, total[:, part * C : (part + 1) * C], codes)

    pieces = front(
        1, x, cot, [moment], w, out, dmid, out1, act1, act2, stats, sums, None, None, *scratch, accumulate
    )
    store_sums(sums, pieces, sums_in)

    clear_borders(full_shift, WORK)

    def early(i, r):
        store_shifted(full_shift, i, r, mid_in[i, pl.ds(r, CHUNK), :], True)

    def late(i, r):
        store_shifted(full_shift, i + WORK - 1, r, dmid[i, pl.ds(r, CHUNK), :], True)

    over_chunks(WORK - 1, early)
    over_chunks(1, late)
    full_act[0 : WORK - 1] = act2_in[...]
    full_act[WORK - 1] = act2[0]
    act = full_act[...].reshape(WORK * TOK, C)
    for di in range(3):
        g = dot(act, window(full_shift, WORK, 2 - di), TN)
        for dj in range(3):
            scatter_unit(blocks, di * 3 + dj, g[:, dj * C : (dj + 1) * C], codes)


def swish_norm_backward(dact, values, base, stats, row, gain, shift, hold, same, dpre, write):
    def sums_of(i, r):
        rows = pl.ds(r, CHUNK)
        unit = (base[i, rows, :] - stats[i, row : row + 1, :]) * stats[i, row + 1 : row + 2, :]
        pre = unit * gain + shift
        s = sigmoid(pre)
        d = dact[i, rows, :] * (s * (1.0 + pre * (1.0 - s)))
        dpre[i, rows, :] = d
        return d, d * unit

    sum_d, sum_du = column_sums(WORK, 2, sums_of, hold)
    first_mean = group_mean(sum_d * gain, same)
    second_mean = group_mean(sum_du * gain, same)
    hold[hold.shape[0] - 1] = first_mean
    hold[hold.shape[0] - 2] = second_mean

    def inner(i, r):
        rows = pl.ds(r, CHUNK)
        scaled = stats[i, row + 1 : row + 2, :]
        unit = (base[i, rows, :] - stats[i, row : row + 1, :]) * scaled
        m1 = hold[hold.shape[0] - 1, pl.ds(i, 1), :]
        m2 = hold[hold.shape[0] - 2, pl.ds(i, 1), :]
        return write(i, r, (dpre[i, rows, :] * gain - m1 - unit * m2) * scaled)

    sums = column_sums(WORK, 1, inner, hold)[0]
    return sum_d, sum_du, sums


def conv_backward(shifted, kernel, dact):
    total = None
    for di in range(3):
        win = window(shifted, WORK, 2 - di)
        for dj in range(3):
            part = dot(win[:, dj * C : (dj + 1) * C], kernel[di, dj].astype(BF16), NT)
            total = part if total is None else total + part
    dact[...] = total.reshape(WORK, TOK, C)


def kernel_three(times, extra, counts, dmid, out1, act1, stats, sums_in, kernel, gain_ref, shift_ref, blocks, low, sums, rows_out,
                 shifted, hold, dact, dpre, same_ref):
    same_ref[...] = group_matrix()
    same = same_ref[...]
    codes = owner_codes(None)
    clear_borders(shifted, WORK)

    def load(i, r):
        store_shifted(shifted, i, r, dmid[i, pl.ds(r, CHUNK), :], True)

    over_chunks(WORK, load)
    conv_backward(shifted, kernel, dact)

    def write(i, r, g):
        low[i, pl.ds(r, CHUNK), :] = g.astype(BF16)
        store_shifted(shifted, i, r, g, True)
        return (g,)

    sum_d, sum_du, sum_first = swish_norm_backward(
        dact, None, out1, stats, 2, gain_ref[...], shift_ref[...], hold, same, dpre, write
    )
    act = act1[...].reshape(WORK * TOK, C)
    for di in range(3):
        g = dot(act, window(shifted, WORK, 2 - di), TN)
        for dj in range(3):
            scatter_unit(blocks, di * 3 + dj, g[:, dj * C : (dj + 1) * C], codes)
    sums[...] = sums_in[...]
    sums[R_SEC_GAIN : R_SEC_GAIN + 1, :] = jnp.sum(sum_du, axis=0, keepdims=True)
    sums[R_SEC_SHIFT : R_SEC_SHIFT + 1, :] = jnp.sum(sum_d, axis=0, keepdims=True)
    sums[R_EMB_BIAS : R_EMB_BIAS + 1, :] = jnp.sum(sum_first, axis=0, keepdims=True)
    lane = lax.broadcasted_iota(jnp.int32, (1, C), 1)
    moment = jnp.where(counts[0, 0] >= WORK, times[0, 0, WORK - 1].astype(F32), extra[0, 0])
    clock = jnp.where(lane == WORK - 1, moment, 0.0)
    for i in range(WORK - 1):
        clock = jnp.where(lane == i, times[0, 0, i].astype(F32), clock)
    rows_out[...] = sum_first
    rows_out[WORK : WORK + 1, :] = clock


def kernel_four(counts, x, spare, dmid, low, stats, sums_in, kernel, gain_ref, shift_ref, grad, back, sums,
                base, shifted, hold, dact, dpre, same_ref):
    same_ref[...] = group_matrix()
    same = same_ref[...]
    clear_borders(shifted, WORK)
    base[0 : WORK - 1] = x[...]
    base[WORK - 1] = spare[...]

    def load(i, r):
        store_shifted(shifted, i, r, low[i, pl.ds(r, CHUNK), :].astype(F32), True)

    over_chunks(WORK, load)
    conv_backward(shifted, kernel, dact)

    def write(i, r, g):
        rows = pl.ds(r, CHUNK)
        dpre[i, rows, :] = g + dmid[i, rows, :]
        return (g,)

    sum_d, sum_du, _ = swish_norm_backward(
        dact, None, base, stats, 0, gain_ref[...], shift_ref[...], hold, same, dpre, write
    )
    grad[0 : WORK - 1] = dpre[0 : WORK - 1]
    keeps = counts[0, 0] >= WORK
    grad[WORK - 1] = jnp.where(keeps, dpre[WORK - 1], 0.0)
    back[...] = jnp.where(keeps, 0.0, dpre[WORK - 1])
    sums[...] = sums_in[...]
    sums[R_FIRST_GAIN : R_FIRST_GAIN + 1, :] = jnp.sum(sum_du, axis=0, keepdims=True)
    sums[R_FIRST_SHIFT : R_FIRST_SHIFT + 1, :] = jnp.sum(sum_d, axis=0, keepdims=True)


def whole(shape):
    return pl.BlockSpec(shape, lambda *_: (0,) * len(shape), memory_space=pltpu.VMEM)


def part(shape, first):
    return pl.BlockSpec(shape, lambda *_: (first,) + (0,) * (len(shape) - 1), memory_space=pltpu.VMEM)


SMEM = pl.BlockSpec(memory_space=pltpu.SMEM)
ANY = pl.BlockSpec(memory_space=pl.ANY)


def params():
    return pltpu.CompilerParams(vmem_limit_bytes=VMEM_LIMIT)


def shape(dims, dtype=F32):
    return jax.ShapeDtypeStruct(dims, dtype)


def weight_specs(w):
    return [whole(w[name].shape) for name in WEIGHTS]


def call_one(timesteps, images, cot, w):
    n = WORK - 1
    return pl.pallas_call(
        kernel_one,
        name="front_of_own_images",
        in_specs=[SMEM, part((n, TOK, C), 0), part((n, TOK, C), 0)] + weight_specs(w),
        out_specs=[part((n, TOK, C), 0)] * 5 + [part((n, 8, C), 0), whole((SUMS, C)), whole((C, 3 * C)), whole((C, C))],
        out_shape=[
            shape((WORK, TOK, C)), shape((WORK, TOK, C)), shape((WORK, TOK, C)),
            shape((WORK, TOK, C), BF16), shape((WORK, TOK, C), BF16),
            shape((WORK, 8, C)), shape((SUMS, C)), shape((C, 3 * C)), shape((C, C)),
        ],
        scratch_shapes=front_scratch(n),
        grid=(1,),
        compiler_params=params(),
    )(timesteps, images, cot, *[w[name] for name in WEIGHTS])


def call_two(timesteps, extra, counts, last, cot, w, early):
    out, dmid, out1, act1, act2, stats, sums, g_triple, g_out = early
    n = WORK - 1
    one = part((1, TOK, C), n)
    first = 5 + 16
    return pl.pallas_call(
        kernel_two,
        name="front_of_last_image",
        in_specs=[SMEM, SMEM, SMEM, whole((1, TOK, C)), one]
        + weight_specs(w)
        + [part((n, TOK, C), 0), part((n, TOK, C), 0), whole((SUMS, C)), whole((C, 3 * C)), whole((C, C)), ANY, ANY, ANY, ANY],
        out_specs=[one] * 5 + [part((1, 8, C), n), whole((SUMS, C)), whole((16, 13, 16, C))],
        out_shape=[
            shape((WORK, TOK, C)), shape((WORK, TOK, C)), shape((WORK, TOK, C)),
            shape((WORK, TOK, C), BF16), shape((WORK, TOK, C), BF16),
            shape((WORK, 8, C)), shape((SUMS, C)), shape((16, 13, 16, C)),
        ],
        scratch_shapes=front_scratch(1) + [pltpu.VMEM((WORK, TOK, C), BF16), pltpu.VMEM((WORK, PAD, 3 * C), BF16)],
        input_output_aliases={first + 5: 0, first: 1, first + 6: 2, first + 7: 3, first + 1: 4, first + 8: 5},
        grid=(1,),
        compiler_params=params(),
    )(timesteps, extra, counts, last, cot, *[w[name] for name in WEIGHTS], dmid, act2, sums, g_triple, g_out, out, out1, act1, stats)


def back_scratch():
    return [
        pltpu.VMEM((WORK, PAD, 3 * C), BF16),
        pltpu.VMEM((16, 8, C), F32),
        pltpu.VMEM((WORK, TOK, C), F32),
        pltpu.VMEM((WORK, TOK, C), F32),
        pltpu.VMEM((C, C), BF16),
    ]


def call_three(timesteps, extra, counts, dmid, out1, act1, stats, sums, w):
    full = (WORK, TOK, C)
    return pl.pallas_call(
        kernel_three,
        name="back_to_first_out",
        in_specs=[SMEM, SMEM, SMEM, whole(full), whole(full), whole(full), whole((WORK, 8, C)), whole((SUMS, C)),
                  whole((3, 3, C, C)), whole((1, C)), whole((1, C))],
        out_specs=[whole((16, 9, 16, C)), whole(full), whole((SUMS, C)), whole((8, C))],
        out_shape=[shape((16, 9, 16, C)), shape(full, BF16), shape((SUMS, C)), shape((8, C))],
        scratch_shapes=back_scratch(),
        grid=(1,),
        compiler_params=params(),
    )(timesteps, extra, counts, dmid, out1, act1, stats, sums, w["second_conv"], w["second_gain"], w["second_shift"])


def call_four(counts, images, last, dmid, low, stats, sums, w):
    full = (WORK, TOK, C)
    return pl.pallas_call(
        kernel_four,
        name="back_to_images",
        in_specs=[SMEM, part((WORK - 1, TOK, C), 0), whole((TOK, C)), whole(full), whole(full), whole((WORK, 8, C)),
                  whole((SUMS, C)), whole((3, 3, C, C)), whole((1, C)), whole((1, C))],
        out_specs=[part(full, 0), whole((TOK, C)), whole((SUMS, C))],
        out_shape=[shape((WORK + 1, TOK, C)), shape((TOK, C)), shape((SUMS, C))],
        scratch_shapes=[pltpu.VMEM(full, F32)] + back_scratch(),
        grid=(1,),
        compiler_params=params(),
    )(counts, images, last, dmid, low, stats, sums, w["first_conv"], w["first_gain"], w["first_shift"])


def assemble_kernel(units, *refs):
    own, other = refs[0], refs[1]
    outs = refs[2:]
    core, even, odd = owner_codes(None)
    for half in range(2):
        src = own if half == 0 else other
        holder = core if half == 0 else 1 - core
        code = jnp.where(holder == 0, even, odd)
        for low in range(8):
            block = holder * 8 + (low ^ code)
            rows = pl.ds(pl.multiple_of(block * 16, 16), 16)
            for unit in range(9):
                outs[0][unit, rows, :] = src[low, unit]
            if units == 13:
                for p in range(3):
                    outs[1][rows, p * C : (p + 1) * C] = src[low, 9 + p]
                outs[2][rows, :] = src[low, 12]


def assemble(units, own, other):
    out_shape = [shape((9, C, C))]
    if units == 13:
        out_shape += [shape((C, 3 * C)), shape((C, C))]
    return pl.pallas_call(
        lambda *refs: assemble_kernel(units, *refs),
        name="assemble",
        in_specs=[whole(own.shape), whole(other.shape)],
        out_specs=[whole(s.shape) for s in out_shape],
        out_shape=out_shape,
        grid=(1,),
        compiler_params=params(),
    )(own, other)


def embed_kernel(devices, own, other, out, rows):
    core, even, odd = owner_codes(None)
    half_count = devices // 2
    for half in range(2):
        src = own if half == 0 else other
        holder = core if half == 0 else 1 - core
        code = jnp.where(holder == 0, even, odd)
        code = code * (half_count // 8) + high_code()
        for rel in range(half_count):
            place = holder * half_count + (rel ^ code)
            rows[pl.ds(pl.multiple_of(place * 8, 8), 8), :] = src[rel]
    everything = rows[...]
    half = TEMB // 2
    index = lax.broadcasted_iota(jnp.int32, (8 * devices, half), 0) % 8
    moments = jnp.zeros((8 * devices, half), F32)
    lane = lax.broadcasted_iota(jnp.int32, (8 * devices, C), 1)
    blocks = everything.reshape(devices, 8, C)
    clock_rows = jnp.broadcast_to(blocks[:, WORK : WORK + 1, :], (devices, 8, C)).reshape(8 * devices, C)
    moments = jnp.sum(jnp.where(lane == index, clock_rows, 0.0), axis=1, keepdims=True)
    frequency = jnp.exp(lax.broadcasted_iota(jnp.int32, (8 * devices, half), 1).astype(F32) * (-math.log(10000.0) / (half - 1)))
    angles = moments * frequency
    waves = jnp.concatenate([jnp.sin(angles), jnp.cos(angles)], axis=1)
    waves = waves * sigmoid(waves)
    keep = lax.broadcasted_iota(jnp.int32, (8 * devices, C), 0) % 8 < WORK
    grads = jnp.where(keep, everything, 0.0)
    out[...] = lax.dot_general(waves, grads, TN, precision=lax.Precision.HIGHEST, preferred_element_type=F32)


def high_code():
    b, t = lax.axis_index("bucket"), lax.axis_index("batch")
    nb = lax.axis_size("bucket")
    return (t // 4) * (nb // 4) + b // 4


def embed_gradient(devices, own, other):
    return pl.pallas_call(
        lambda *refs: embed_kernel(devices, *refs),
        name="embed_gradient",
        in_specs=[whole(own.shape), whole(other.shape)],
        out_specs=whole((TEMB, C)),
        out_shape=shape((TEMB, C)),
        scratch_shapes=[pltpu.VMEM((devices * 8, C), F32)],
        grid=(1,),
        compiler_params=params(),
    )(own, other)


AXES = ("bucket", "batch")


def solution(mesh):
    n_bucket, n_batch = mesh.shape["bucket"], mesh.shape["batch"]
    devices = n_bucket * n_batch

    def flips(fn):
        pairs = []
        for b in range(n_bucket):
            for t in range(n_batch):
                nb, nt = fn(b, t)
                pairs.append((b * n_batch + t, nb * n_batch + nt))
        return pairs

    def by_core(even, odd):
        def fn(b, t):
            kind, bit = even if t % 2 == 0 else odd
            return (b ^ bit, t) if kind == "b" else (b, t ^ bit)

        return flips(fn)

    x, y, z = ("b", 1), ("b", 2), ("t", 2)
    core_perm = flips(lambda b, t: (b, t ^ 1))
    stages = [by_core(x, z), by_core(y, x), by_core(z, y)]
    rest = []
    bit = 4
    while bit < n_bucket:
        rest.append(("b", bit))
        bit *= 2
    bit = 4
    while bit < n_batch:
        rest.append(("t", bit))
        bit *= 2
    rest_perms = [by_core(s, s) for s in rest]
    bucket_perms = [flips(lambda b, t, k=k: (b ^ k, t)) for k in range(1, n_bucket)]

    def send(v, perm):
        return lax.ppermute(v, AXES, perm)

    def reduce_blocks(blocks, units):
        v = blocks.reshape(2, 2, 2, 2, units * 16, C)
        r, k = send(v[1], core_perm), v[0]
        for perm in stages:
            out = k[1] + r[1]
            k = k[0] + r[0]
            r = send(out, perm)
        return k + r

    def shards(images, timesteps, counts, source, cotangent, *weights):
        w = dict(zip(WEIGHTS, weights))
        w = {k: v.reshape(1, C) if v.ndim == 1 else v for k, v in w.items()}
        slots = images[0, 0]
        cot = cotangent[0, 0]
        me = lax.axis_index("bucket")
        keeps = counts[0, 0] >= WORK
        own_offset = jnp.where(keeps, 0, source[0, 0] ^ me)

        spare = slots[WORK]
        note = jnp.concatenate(
            [timesteps[0, 0, WORK][None].astype(F32), own_offset[None].astype(F32), jnp.zeros((126,), F32)]
        ).reshape(1, 128)
        arrived = [send(spare, p) for p in bucket_perms]
        notes = [send(note, p) for p in bucket_perms]

        early = call_one(timesteps, slots, cot, w)

        taken, moment = slots[WORK - 1], note[0, 0]
        for k in range(1, n_bucket):
            taken = jnp.where(own_offset == k, arrived[k - 1], taken)
            moment = jnp.where(own_offset == k, notes[k - 1][0, 0], moment)
        extra = jnp.broadcast_to(moment, (1, 128))

        out, dmid, out1, act1, act2, stats, sums, blocks2 = call_two(timesteps, extra, counts, taken[None], cot, w, early)
        blocks1, low, sums, rows = call_three(timesteps, extra, counts, dmid, out1, act1, stats, sums, w)
        grad, back, sums = call_four(counts, slots, taken, dmid, low, stats, sums, w)

        m2 = reduce_blocks(blocks2, 13)
        for perm in rest_perms:
            m2 = m2 + send(m2, perm)
        for perm in stages[::-1]:
            m2 = jnp.stack([m2, send(m2, perm)])
        other2 = send(m2, core_perm)
        dims = (8, 13, 16, C)
        g_second, g_triple, g_out = assemble(13, m2.reshape(dims), other2.reshape(dims))

        m1 = reduce_blocks(blocks1, 9)
        n1 = 9 * 16
        carry = m1
        rows = rows[None]
        for perm in rest_perms:
            packed = jnp.concatenate([carry, sums, rows.reshape(-1, C)], axis=0)
            got = send(packed, perm)
            carry = carry + got[:n1]
            sums = sums + got[n1 : n1 + SUMS]
            rows = jnp.concatenate([rows, got[n1 + SUMS :].reshape(rows.shape)], axis=0)
        carry = carry[None]
        for perm in stages[::-1]:
            size = carry.shape[0] * n1
            packed = jnp.concatenate([carry.reshape(size, C), sums, rows.reshape(-1, C)], axis=0)
            got = send(packed, perm)
            carry = jnp.concatenate([carry, got[:size].reshape(carry.shape)], axis=0)
            sums = sums + got[size : size + SUMS]
            rows = jnp.concatenate([rows, got[size + SUMS :].reshape(rows.shape)], axis=0)
        other1, other_sums, other_rows = send(carry, core_perm), send(sums, core_perm), send(rows, core_perm)
        dims = (8, 9, 16, C)
        (g_first,) = assemble(9, carry.reshape(dims), other1.reshape(dims))
        sums = sums + other_sums
        g_embed = embed_gradient(devices, rows, other_rows)

        if n_bucket == 4:
            core = lax.axis_index("batch") % 2
            bit_a = jnp.where(core == 0, 1, 2)
            bit_b = 3 - bit_a
            first_hop, second_hop = by_core(x, y), by_core(y, x)
            offset_a = jnp.where(core == 0, notes[0][0, 1], notes[1][0, 1]).astype(jnp.int32)
            hop = send(jnp.where((own_offset & bit_a) != 0, back, 0.0), first_hop)
            onward = (offset_a & bit_a) != 0
            turn = jnp.where(onward & ((offset_a & bit_b) != 0), hop, jnp.where(own_offset == bit_b, back, 0.0))
            got = send(turn, second_hop)
            last = jnp.where(onward & ((offset_a & bit_b) == 0), hop, got)
        else:
            last = jnp.zeros_like(back)
            for k in range(1, n_bucket):
                last = last + send(jnp.where(own_offset == k, back, 0.0), bucket_perms[k - 1])
        grad = lax.dynamic_update_slice(grad, last[None], (WORK, 0, 0))

        def vec(r):
            return sums[r]

        return (
            out[None, None], grad[None, None],
            vec(R_FIRST_GAIN), vec(R_FIRST_SHIFT), g_first.reshape(3, 3, C, C), g_embed, vec(R_EMB_BIAS),
            vec(R_SEC_GAIN), vec(R_SEC_SHIFT), g_second.reshape(3, 3, C, C), vec(R_SEC_BIAS),
            vec(R_ATT_GAIN), vec(R_ATT_SHIFT), g_triple, vec(R_QUERY_BIAS), vec(R_VALUE_BIAS),
            g_out, vec(R_OUT_BIAS),
        )

    placed = (
        P("batch", "bucket", None, None, None), P("batch", "bucket", None), P("batch", "bucket"),
        P("batch", "bucket"), P("batch", "bucket", None, None, None),
    ) + (P(),) * 16
    return jax.shard_map(
        shards,
        mesh=mesh,
        in_specs=placed,
        out_specs=(P("batch", "bucket", None, None, None),) * 2 + (P(),) * 16,
        check_vma=False,
    )
```

profile of v0, /device:TPU:0, one launch (start us, length us, event | category | flops | bytes accessed | tf_op | source)
XLA Modules:
  0.0 178.1 jit_solution(163529888755538046)
XLA Ops:
  1.6 3.0 %collective-permute-start.5 = (f32[256,256]{1,0:T(8,128)S(1)}, f32[256,256]{1,0:T(8,128)S(1)}, u32[]{:S(2)}, u32[]{:S(2)}) collective-permute-start(f32[256,256]{1,0:T(8,128)S(1)} %slice_bitcast_fusion.4), channel_id=1, source_target_pairs={{0,8},{1,9},{2,10},{3,11},{4,12},{5,13},{6,14},{7,15},{8,0},{9,1},... | collective-permute-start | bytes 786440 | tf_op jit(solution)/shard_map/ppermute | solution.py:728
  4.6 1.5 collective-permute-start.4
  9.5 2.0 %collective-permute-start.2 = (f32[1,128]{1,0:T(1,128)S(1)}, f32[1,128]{1,0:T(1,128)S(1)}, u32[]{:S(2)}, u32[]{:S(2)}) collective-permute-start(f32[1,128]{1,0:T(1,128)S(1)} %maximum_bitcast_fusion.3), channel_id=1, source_target_pairs={{0,8},{1,9},{2,10},{3,11},{4,12},{5,13},{6,14},{7,15},{8,0},{9,1},... | collective-permute-start | bytes 1544 | tf_op jit(solution)/shard_map/ppermute | solution.py:728
  11.4 1.5 collective-permute-start.1
  12.9 17.0 %front_of_own_images.1 = (f32[4,256,256]{2,1,0:T(8,128)}, f32[4,256,256]{2,1,0:T(8,128)}, f32[4,256,256]{2,1,0:T(8,128)}, bf16[4,256,256]{2,1,0:T(8,128)(2,1)}, ...) custom-call(s32[1,1,5]{2,1,0:T(1,128)} %times.5, ...), custom_call_target="tpu_custom_call" | custom-call | tf_op jit(solution)/shard_map/front_of_own_images/pallas_call | solution.py:529
  32.5 2.0 %collective-permute-done = f32[1,128]{1,0:T(1,128)S(1)} collective-permute-done((f32[1,128]{1,0:T(1,128)S(1)}, f32[1,128]{1,0:T(1,128)S(1)}, u32[]{:S(2)}, u32[]{:S(2)}) %collective-permute-start) | collective-permute-done | bytes 544 | tf_op jit(solution)/shard_map/ppermute | solution.py:728
  34.6 1.7 fusion.7.spare
  36.8 12.5 %front_of_last_image.1 = (f32[4,256,256]{2,1,0:T(8,128)}, f32[4,256,256]{2,1,0:T(8,128)}, f32[4,256,256]{2,1,0:T(8,128)}, bf16[4,256,256]{2,1,0:T(8,128)(2,1)}, ...) custom-call(s32[1,1,5]{2,1,0:T(1,128)} %times.5, ...), custom_call_target="tpu_custom_call", output_to_operand_aliasing={{0}: (26, {}), {1}: (21, {}), {2}: (27, {}), {3}: (28, {}),... | custom-call | tf_op jit(solution)/shard_map/front_of_last_image/pallas_call | solution.py:550
  49.3 11.6 %back_to_first_out.1 = (f32[16,9,16,256]{3,2,1,0:T(8,128)}, bf16[4,256,256]{2,1,0:T(8,128)(2,1)}, f32[16,256]{1,0:T(8,128)}, f32[8,256]{1,0:T(8,128)}) custom-call(s32[1,1,5]{2,1,0:T(1,128)} %times.5, f32[1,128]{1,0:T(1,128)} %broadcast_in_dim.31.extra, s32[1,1]{1,0:T(1,128)S(6)} %copy.56.counts, f32[4,256,256]{2,1,0:T(8,128)} %get-tuple-element.54.dmid, ...), custom_call_target="tpu_custom_call" | custom-call | tf_op jit(solution)/shard_map/back_to_first_out/pallas_call | solution.py:581
  65.9 9.3 %collective-permute-done.9 = f32[2,2,144,256]{3,2,1,0:T(8,128)S(1)} collective-permute-done((f32[2,2,144,256]{3,2,1,0:T(8,128)S(1)}, f32[2,2,144,256]{3,2,1,0:T(8,128)S(1)}, u32[]{:S(2)}, u32[]{:S(2)}) %collective-permute-start.9) | collective-permute-done | bytes 589856 | tf_op jit(solution)/shard_map/ppermute | solution.py:728
  76.0 6.1 %collective-permute-done.10 = f32[2,144,256]{2,1,0:T(8,128)S(1)} collective-permute-done((f32[2,144,256]{2,1,0:T(8,128)S(1)}, f32[2,144,256]{2,1,0:T(8,128)S(1)}, u32[]{:S(2)}, u32[]{:S(2)}) %collective-permute-start.10) | collective-permute-done | bytes 294944 | tf_op jit(solution)/shard_map/ppermute | solution.py:728
  82.1 1.6 collective-permute-start.11
  86.0 7.2 %back_to_images.1 = (f32[5,256,256]{2,1,0:T(8,128)}, f32[256,256]{1,0:T(8,128)}, f32[16,256]{1,0:T(8,128)}) custom-call(s32[1,1]{1,0:T(1,128)S(6)} %copy.56.counts, f32[5,256,256]{2,1,0:T(8,128)} %bitcast.155, f32[256,256]{1,0:T(8,128)} %fusion.7.spare, f32[4,256,256]{2,1,0:T(8,128)} %get-tuple-element.54.dmid, bf16[4,256,256]{2,1,0:T(8,128)(2,1)} %get-tuple-element.59.low, ...), custom_call_target="tpu_custom_call" | custom-call | tf_op jit(solution)/shard_map/back_to_images/pallas_call | solution.py:596
  94.0 2.7 %collective-permute-start.12 = (f32[168,256]{1,0:T(8,128)S(1)}, f32[168,256]{1,0:T(8,128)S(1)}, u32[]{:S(2)}, u32[]{:S(2)}) collective-permute-start(f32[168,256]{1,0:T(8,128)S(1)} %pad_maximum_fusion.10), channel_id=1, source_target_pairs={{0,4},{1,5},{2,6},{3,7},{4,0},{5,1},{6,2},{7,3},{8,12},{9,13},{10,... | collective-permute-start | bytes 516104 | tf_op jit(solution)/shard_map/ppermute | solution.py:728
  96.6 1.6 collective-permute-start.6
  98.2 4.5 %collective-permute-done.12 = f32[168,256]{1,0:T(8,128)S(1)} collective-permute-done((f32[168,256]{1,0:T(8,128)S(1)}, f32[168,256]{1,0:T(8,128)S(1)}, u32[]{:S(2)}, u32[]{:S(2)}) %collective-permute-start.12) | collective-permute-done | bytes 172064 | tf_op jit(solution)/shard_map/ppermute | solution.py:728
  102.9 1.6 collective-permute-start.21
  104.5 6.6 %collective-permute-done.21 = f32[2,208,256]{2,1,0:T(8,128)S(1)} collective-permute-done((f32[2,208,256]{2,1,0:T(8,128)S(1)}, f32[2,208,256]{2,1,0:T(8,128)S(1)}, u32[]{:S(2)}, u32[]{:S(2)}) %collective-permute-start.21) | collective-permute-done | bytes 426016 | tf_op jit(solution)/shard_map/ppermute | solution.py:728
  111.2 2.1 %collective-permute-start.13 = (f32[176,256]{1,0:T(8,128)S(1)}, f32[176,256]{1,0:T(8,128)S(1)}, u32[]{:S(2)}, u32[]{:S(2)}) collective-permute-start(f32[176,256]{1,0:T(8,128)S(1)} %pad_maximum_fusion.9), channel_id=1, source_target_pairs={{0,2},{1,17},{2,0},{3,19},{4,6},{5,21},{6,4},{7,23},{8,10},{9,25},... | collective-permute-start | bytes 540680 | tf_op jit(solution)/shard_map/ppermute | solution.py:728
  113.3 3.7 %collective-permute-done.22 = f32[208,256]{1,0:T(8,128)S(1)} collective-permute-done((f32[208,256]{1,0:T(8,128)S(1)}, f32[208,256]{1,0:T(8,128)S(1)}, u32[]{:S(2)}, u32[]{:S(2)}) %collective-permute-start.22) | collective-permute-done | bytes 213024 | tf_op jit(solution)/shard_map/ppermute | solution.py:728
  118.4 2.1 %collective-permute-done.13 = f32[176,256]{1,0:T(8,128)S(1)} collective-permute-done((f32[176,256]{1,0:T(8,128)S(1)}, f32[176,256]{1,0:T(8,128)S(1)}, u32[]{:S(2)}, u32[]{:S(2)}) %collective-permute-start.13) | collective-permute-done | bytes 180256 | tf_op jit(solution)/shard_map/ppermute | solution.py:728
  120.5 6.0 %collective-permute-done.23 = f32[208,256]{1,0:T(8,128)S(1)} collective-permute-done((f32[208,256]{1,0:T(8,128)S(1)}, f32[208,256]{1,0:T(8,128)S(1)}, u32[]{:S(2)}, u32[]{:S(2)}) %collective-permute-start.23) | collective-permute-done | bytes 213024 | tf_op jit(solution)/shard_map/ppermute | solution.py:728
  126.6 5.8 %collective-permute-done.24 = f32[208,256]{1,0:T(8,128)S(1)} collective-permute-done((f32[208,256]{1,0:T(8,128)S(1)}, f32[208,256]{1,0:T(8,128)S(1)}, u32[]{:S(2)}, u32[]{:S(2)}) %collective-permute-start.24) | collective-permute-done | bytes 213024 | tf_op jit(solution)/shard_map/ppermute | solution.py:728
  132.5 1.6 collective-permute-start.25
  134.8 1.6 collective-permute-start.7
  136.4 4.3 %collective-permute-done.25 = f32[2,208,256]{2,1,0:T(8,128)S(1)} collective-permute-done((f32[2,208,256]{2,1,0:T(8,128)S(1)}, f32[2,208,256]{2,1,0:T(8,128)S(1)}, u32[]{:S(2)}, u32[]{:S(2)}) %collective-permute-start.25) | collective-permute-done | bytes 426016 | tf_op jit(solution)/shard_map/ppermute | solution.py:728
  141.6 2.8 %collective-permute-done.14 = f32[336,256]{1,0:T(8,128)S(1)} collective-permute-done((f32[336,256]{1,0:T(8,128)S(1)}, f32[336,256]{1,0:T(8,128)S(1)}, u32[]{:S(2)}, u32[]{:S(2)}) %collective-permute-start.14) | collective-permute-done | bytes 344096 | tf_op jit(solution)/shard_map/ppermute | solution.py:728
  145.3 8.3 %collective-permute-done.26 = f32[2,2,208,256]{3,2,1,0:T(8,128)S(1)} collective-permute-done((f32[2,2,208,256]{3,2,1,0:T(8,128)S(1)}, f32[2,2,208,256]{3,2,1,0:T(8,128)S(1)}, u32[]{:S(2)}, u32[]{:S(2)}) %collective-permute-start.26) | collective-permute-done | bytes 852000 | tf_op jit(solution)/shard_map/ppermute | solution.py:728
  154.7 6.1 %collective-permute-done.15 = f32[656,256]{1,0:T(8,128)S(1)} collective-permute-done((f32[656,256]{1,0:T(8,128)S(1)}, f32[656,256]{1,0:T(8,128)S(1)}, u32[]{:S(2)}, u32[]{:S(2)}) %collective-permute-start.15) | collective-permute-done | bytes 671776 | tf_op jit(solution)/shard_map/ppermute | solution.py:728
  165.1 3.5 %embed_gradient.1 = f32[512,256]{1,0:T(8,128)} custom-call(f32[16,8,256]{2,1,0:T(8,128)} %copy-done.7, f32[16,8,256]{2,1,0:T(8,128)} %copy-done.8), custom_call_target="tpu_custom_call" | custom-call | tf_op jit(solution)/shard_map/embed_gradient/pallas_call | solution.py:678
  169.7 3.2 %assemble.2 = f32[9,256,256]{2,1,0:T(8,128)} custom-call(f32[8,9,16,256]{3,2,1,0:T(8,128)} %pad_maximum_fusion.1.refs_0_, f32[8,9,16,256]{3,2,1,0:T(8,128)} %bitcast.179), custom_call_target="tpu_custom_call" | custom-call | tf_op jit(solution)/shard_map/assemble/pallas_call | solution.py:632
  174.1 4.0 %assemble.3 = (f32[9,256,256]{2,1,0:T(8,128)}, f32[256,768]{1,0:T(8,128)}, f32[256,256]{1,0:T(8,128)}) custom-call(f32[8,13,16,256]{3,2,1,0:T(8,128)} %bitcast.156, f32[8,13,16,256]{3,2,1,0:T(8,128)} %bitcast.175), custom_call_target="tpu_custom_call" | custom-call | tf_op jit(solution)/shard_map/assemble/pallas_call | solution.py:632
  (106 shorter events, 23.3 us)
Async XLA Ops:
  1.6 32.9 %collective-permute-start.5 = (f32[256,256]{1,0:T(8,128)S(1)}, f32[256,256]{1,0:T(8,128)S(1)}, u32[]{:S(2)}, u32[]{:S(2)}) collective-permute-start(f32[256,256]{1,0:T(8,128)S(1)} %slice_bitcast_fusion.4), channel_id=1, source_target_pairs={{0,8},{1,9},{2,10},{3,11},{4,12},{5,13},{6,14},{7,15},{8,0},{9,1},... | collective-permute-start | bytes 786440 | tf_op jit(solution)/shard_map/ppermute | solution.py:728
  4.6 29.9 %collective-permute-start.4 = (f32[256,256]{1,0:T(8,128)S(1)}, f32[256,256]{1,0:T(8,128)S(1)}, u32[]{:S(2)}, u32[]{:S(2)}) collective-permute-start(f32[256,256]{1,0:T(8,128)S(1)} %slice_bitcast_fusion.4), channel_id=1, source_target_pairs={{0,16},{1,17},{2,18},{3,19},{4,20},{5,21},{6,22},{7,23},{8,24},{9,... | collective-permute-start | bytes 786440 | tf_op jit(solution)/shard_map/ppermute | solution.py:728
  6.2 28.4 %collective-permute-start.3 = (f32[256,256]{1,0:T(8,128)S(1)}, f32[256,256]{1,0:T(8,128)S(1)}, u32[]{:S(2)}, u32[]{:S(2)}) collective-permute-start(f32[256,256]{1,0:T(8,128)S(1)} %slice_bitcast_fusion.4), channel_id=1, source_target_pairs={{0,24},{1,25},{2,26},{3,27},{4,28},{5,29},{6,30},{7,31},{8,16},{9,... | collective-permute-start | bytes 786440 | tf_op jit(solution)/shard_map/ppermute | solution.py:728
  9.5 20.5 %collective-permute-start.2 = (f32[1,128]{1,0:T(1,128)S(1)}, f32[1,128]{1,0:T(1,128)S(1)}, u32[]{:S(2)}, u32[]{:S(2)}) collective-permute-start(f32[1,128]{1,0:T(1,128)S(1)} %maximum_bitcast_fusion.3), channel_id=1, source_target_pairs={{0,8},{1,9},{2,10},{3,11},{4,12},{5,13},{6,14},{7,15},{8,0},{9,1},... | collective-permute-start | bytes 1544 | tf_op jit(solution)/shard_map/ppermute | solution.py:728
  11.4 19.2 %collective-permute-start.1 = (f32[1,128]{1,0:T(1,128)S(1)}, f32[1,128]{1,0:T(1,128)S(1)}, u32[]{:S(2)}, u32[]{:S(2)}) collective-permute-start(f32[1,128]{1,0:T(1,128)S(1)} %maximum_bitcast_fusion.3), channel_id=1, source_target_pairs={{0,16},{1,17},{2,18},{3,19},{4,20},{5,21},{6,22},{7,23},{8,24},{9,... | collective-permute-start | bytes 1544 | tf_op jit(solution)/shard_map/ppermute | solution.py:728
  30.0 4.5 %collective-permute-start = (f32[1,128]{1,0:T(1,128)S(1)}, f32[1,128]{1,0:T(1,128)S(1)}, u32[]{:S(2)}, u32[]{:S(2)}) collective-permute-start(f32[1,128]{1,0:T(1,128)S(1)} %maximum_bitcast_fusion.3), channel_id=1, source_target_pairs={{0,24},{1,25},{2,26},{3,27},{4,28},{5,29},{6,30},{7,31},{8,16},{9,... | collective-permute-start | bytes 1544 | tf_op jit(solution)/shard_map/ppermute | solution.py:728
  49.3 13.0 %copy-start.1 = (f32[16,13,16,256]{3,2,1,0:T(8,128)S(1)}, f32[16,13,16,256]{3,2,1,0:T(8,128)}, u32[]{:S(2)}) copy-start(f32[16,13,16,256]{3,2,1,0:T(8,128)} %get-tuple-element.66) | copy-start | bytes 10223620
  62.2 2.9 %collective-permute-start.8 = (f32[2,2,2,144,256]{4,3,2,1,0:T(8,128)S(1)}, f32[2,2,2,144,256]{4,3,2,1,0:T(8,128)S(1)}, u32[]{:S(2)}, u32[]{:S(2)}) collective-permute-start(f32[2,2,2,144,256]{4,3,2,1,0:T(8,128)S(1)} %bitcast.177), channel_id=1, source_target_pairs={{0,1},{1,0},{2,3},{3,2},{4,5},{5,4},{6,7},{7,6},{8,9},{9,8},{10,11... | collective-permute-start | bytes 3538952 | tf_op jit(solution)/shard_map/ppermute | solution.py:728
  62.4 21.3 %collective-permute-start.19 = (f32[2,2,2,208,256]{4,3,2,1,0:T(8,128)S(1)}, f32[2,2,2,208,256]{4,3,2,1,0:T(8,128)S(1)}, u32[]{:S(2)}, u32[]{:S(2)}) collective-permute-start(f32[2,2,2,208,256]{4,3,2,1,0:T(8,128)S(1)} %bitcast.176), channel_id=1, source_target_pairs={{0,1},{1,0},{2,3},{3,2},{4,5},{5,4},{6,7},{7,6},{8,9},{9,8},{10,11... | collective-permute-start | bytes 5111816 | tf_op jit(solution)/shard_map/ppermute | solution.py:728
  65.3 9.9 %collective-permute-start.9 = (f32[2,2,144,256]{3,2,1,0:T(8,128)S(1)}, f32[2,2,144,256]{3,2,1,0:T(8,128)S(1)}, u32[]{:S(2)}, u32[]{:S(2)}) collective-permute-start(f32[2,2,144,256]{3,2,1,0:T(8,128)S(1)} %get-tuple-element.81), channel_id=1, source_target_pairs={{0,8},{1,3},{2,10},{3,1},{4,12},{5,7},{6,14},{7,5},{8,0},{9,11},{1... | collective-permute-start | bytes 1769480 | tf_op jit(solution)/shard_map/ppermute | solution.py:728
  75.3 6.8 %collective-permute-start.10 = (f32[2,144,256]{2,1,0:T(8,128)S(1)}, f32[2,144,256]{2,1,0:T(8,128)S(1)}, u32[]{:S(2)}, u32[]{:S(2)}) collective-permute-start(f32[2,144,256]{2,1,0:T(8,128)S(1)} %get-tuple-element.79), channel_id=1, source_target_pairs={{0,16},{1,9},{2,18},{3,11},{4,20},{5,13},{6,22},{7,15},{8,24},{9,1... | collective-permute-start | bytes 884744 | tf_op jit(solution)/shard_map/ppermute | solution.py:728
  82.1 11.1 %collective-permute-start.11 = (f32[144,256]{1,0:T(8,128)S(1)}, f32[144,256]{1,0:T(8,128)S(1)}, u32[]{:S(2)}, u32[]{:S(2)}) collective-permute-start(f32[144,256]{1,0:T(8,128)S(1)} %fusion.11), channel_id=1, source_target_pairs={{0,2},{1,17},{2,0},{3,19},{4,6},{5,21},{6,4},{7,23},{8,10},{9,25},... | collective-permute-start | bytes 442376 | tf_op jit(solution)/shard_map/ppermute | solution.py:728
  84.0 18.7 %collective-permute-start.20 = (f32[2,2,208,256]{3,2,1,0:T(8,128)S(1)}, f32[2,2,208,256]{3,2,1,0:T(8,128)S(1)}, u32[]{:S(2)}, u32[]{:S(2)}) collective-permute-start(f32[2,2,208,256]{3,2,1,0:T(8,128)S(1)} %get-tuple-element.77), channel_id=1, source_target_pairs={{0,8},{1,3},{2,10},{3,1},{4,12},{5,7},{6,14},{7,5},{8,0},{9,11},{1... | collective-permute-start | bytes 2555912 | tf_op jit(solution)/shard_map/ppermute | solution.py:728
  85.9 7.3 %copy-start.6 = (f32[8,256]{1,0:T(8,128)S(1)}, f32[8,256]{1,0:T(8,128)}, u32[]{:S(2)}) copy-start(f32[8,256]{1,0:T(8,128)} %get-tuple-element.65) | copy-start | bytes 24580
  93.2 9.6 %copy-start.9 = (f32[16,256]{1,0:T(8,128)S(1)}, f32[16,256]{1,0:T(8,128)}, u32[]{:S(2)}) copy-start(f32[16,256]{1,0:T(8,128)} %get-tuple-element.63) | copy-start | bytes 49156
  94.0 8.8 %collective-permute-start.12 = (f32[168,256]{1,0:T(8,128)S(1)}, f32[168,256]{1,0:T(8,128)S(1)}, u32[]{:S(2)}, u32[]{:S(2)}) collective-permute-start(f32[168,256]{1,0:T(8,128)S(1)} %pad_maximum_fusion.10), channel_id=1, source_target_pairs={{0,4},{1,5},{2,6},{3,7},{4,0},{5,1},{6,2},{7,3},{8,12},{9,13},{10,... | collective-permute-start | bytes 516104 | tf_op jit(solution)/shard_map/ppermute | solution.py:728
  96.6 38.1 %collective-permute-start.6 = (f32[256,256]{1,0:T(8,128)S(1)}, f32[256,256]{1,0:T(8,128)S(1)}, u32[]{:S(2)}, u32[]{:S(2)}) collective-permute-start(f32[256,256]{1,0:T(8,128)S(1)} %broadcast_select_fusion), channel_id=1, source_target_pairs={{0,8},{1,17},{2,10},{3,19},{4,12},{5,21},{6,14},{7,23},{8,0},{9,25... | collective-permute-start | bytes 786440 | tf_op jit(solution)/shard_map/ppermute | solution.py:728
  102.9 8.2 %collective-permute-start.21 = (f32[2,208,256]{2,1,0:T(8,128)S(1)}, f32[2,208,256]{2,1,0:T(8,128)S(1)}, u32[]{:S(2)}, u32[]{:S(2)}) collective-permute-start(f32[2,208,256]{2,1,0:T(8,128)S(1)} %get-tuple-element.75), channel_id=1, source_target_pairs={{0,16},{1,9},{2,18},{3,11},{4,20},{5,13},{6,22},{7,15},{8,24},{9,1... | collective-permute-start | bytes 1277960 | tf_op jit(solution)/shard_map/ppermute | solution.py:728
  111.1 5.9 %collective-permute-start.22 = (f32[208,256]{1,0:T(8,128)S(1)}, f32[208,256]{1,0:T(8,128)S(1)}, u32[]{:S(2)}, u32[]{:S(2)}) collective-permute-start(f32[208,256]{1,0:T(8,128)S(1)} %fusion.8), channel_id=1, source_target_pairs={{0,2},{1,17},{2,0},{3,19},{4,6},{5,21},{6,4},{7,23},{8,10},{9,25},... | collective-permute-start | bytes 638984 | tf_op jit(solution)/shard_map/ppermute | solution.py:728
  111.2 9.2 %collective-permute-start.13 = (f32[176,256]{1,0:T(8,128)S(1)}, f32[176,256]{1,0:T(8,128)S(1)}, u32[]{:S(2)}, u32[]{:S(2)}) collective-permute-start(f32[176,256]{1,0:T(8,128)S(1)} %pad_maximum_fusion.9), channel_id=1, source_target_pairs={{0,2},{1,17},{2,0},{3,19},{4,6},{5,21},{6,4},{7,23},{8,10},{9,25},... | collective-permute-start | bytes 540680 | tf_op jit(solution)/shard_map/ppermute | solution.py:728
  117.1 9.4 %collective-permute-start.23 = (f32[208,256]{1,0:T(8,128)S(1)}, f32[208,256]{1,0:T(8,128)S(1)}, u32[]{:S(2)}, u32[]{:S(2)}) collective-permute-start(f32[208,256]{1,0:T(8,128)S(1)} %fusion.10), channel_id=1, source_target_pairs={{0,4},{1,5},{2,6},{3,7},{4,0},{5,1},{6,2},{7,3},{8,12},{9,13},{10,... | collective-permute-start | bytes 638984 | tf_op jit(solution)/shard_map/ppermute | solution.py:728
  120.5 14.2 %copy-start.5 = (f32[256,256]{1,0:T(8,128)S(1)}, f32[256,256]{1,0:T(8,128)}, u32[]{:S(2)}) copy-start(f32[256,256]{1,0:T(8,128)} %get-tuple-element.62) | copy-start | bytes 786436
  126.5 5.9 %collective-permute-start.24 = (f32[208,256]{1,0:T(8,128)S(1)}, f32[208,256]{1,0:T(8,128)S(1)}, u32[]{:S(2)}, u32[]{:S(2)}) collective-permute-start(f32[208,256]{1,0:T(8,128)S(1)} %add.114), channel_id=1, source_target_pairs={{0,2},{1,17},{2,0},{3,19},{4,6},{5,21},{6,4},{7,23},{8,10},{9,25},... | collective-permute-start | bytes 638984 | tf_op jit(solution)/shard_map/ppermute | solution.py:728
  132.5 8.2 %collective-permute-start.25 = (f32[2,208,256]{2,1,0:T(8,128)S(1)}, f32[2,208,256]{2,1,0:T(8,128)S(1)}, u32[]{:S(2)}, u32[]{:S(2)}) collective-permute-start(f32[2,208,256]{2,1,0:T(8,128)S(1)} %get-tuple-element.85), channel_id=1, source_target_pairs={{0,16},{1,9},{2,18},{3,11},{4,20},{5,13},{6,22},{7,15},{8,24},{9,1... | collective-permute-start | bytes 1277960 | tf_op jit(solution)/shard_map/ppermute | solution.py:728
  134.2 10.2 %collective-permute-start.14 = (f32[336,256]{1,0:T(8,128)S(1)}, f32[336,256]{1,0:T(8,128)S(1)}, u32[]{:S(2)}, u32[]{:S(2)}) collective-permute-start(f32[336,256]{1,0:T(8,128)S(1)} %pad_maximum_fusion.7), channel_id=1, source_target_pairs={{0,16},{1,9},{2,18},{3,11},{4,20},{5,13},{6,22},{7,15},{8,24},{9,1... | collective-permute-start | bytes 1032200 | tf_op jit(solution)/shard_map/ppermute | solution.py:728
  134.8 19.0 %collective-permute-start.7 = (f32[256,256]{1,0:T(8,128)S(1)}, f32[256,256]{1,0:T(8,128)S(1)}, u32[]{:S(2)}, u32[]{:S(2)}) collective-permute-start(f32[256,256]{1,0:T(8,128)S(1)} %select_select_fusion), channel_id=1, source_target_pairs={{0,16},{1,9},{2,18},{3,11},{4,20},{5,13},{6,22},{7,15},{8,24},{9,1... | collective-permute-start | bytes 786440 | tf_op jit(solution)/shard_map/ppermute | solution.py:728
  140.8 12.8 %collective-permute-start.26 = (f32[2,2,208,256]{3,2,1,0:T(8,128)S(1)}, f32[2,2,208,256]{3,2,1,0:T(8,128)S(1)}, u32[]{:S(2)}, u32[]{:S(2)}) collective-permute-start(f32[2,2,208,256]{3,2,1,0:T(8,128)S(1)} %get-tuple-element.83), channel_id=1, source_target_pairs={{0,8},{1,3},{2,10},{3,1},{4,12},{5,7},{6,14},{7,5},{8,0},{9,11},{1... | collective-permute-start | bytes 2555912 | tf_op jit(solution)/shard_map/ppermute | solution.py:728
  144.6 16.2 %collective-permute-start.15 = (f32[656,256]{1,0:T(8,128)S(1)}, f32[656,256]{1,0:T(8,128)S(1)}, u32[]{:S(2)}, u32[]{:S(2)}) collective-permute-start(f32[656,256]{1,0:T(8,128)S(1)} %pad_maximum_fusion.4), channel_id=1, source_target_pairs={{0,8},{1,3},{2,10},{3,1},{4,12},{5,7},{6,14},{7,5},{8,0},{9,11},{1... | collective-permute-start | bytes 2015240 | tf_op jit(solution)/shard_map/ppermute | solution.py:728
  153.7 19.2 %collective-permute-start.27 = (f32[2,2,2,208,256]{4,3,2,1,0:T(8,128)S(1)}, f32[2,2,2,208,256]{4,3,2,1,0:T(8,128)S(1)}, u32[]{:S(2)}, u32[]{:S(2)}) collective-permute-start(f32[2,2,2,208,256]{4,3,2,1,0:T(8,128)S(1)} %pad_maximum_fusion), channel_id=1, source_target_pairs={{0,1},{1,0},{2,3},{3,2},{4,5},{5,4},{6,7},{7,6},{8,9},{9,8},{10,11... | collective-permute-start | bytes 5111816 | tf_op jit(solution)/shard_map/ppermute | solution.py:728
  160.9 7.8 %collective-permute-start.17 = (f32[8,144,256]{2,1,0:T(8,128)S(1)}, f32[8,144,256]{2,1,0:T(8,128)S(1)}, u32[]{:S(2)}, u32[]{:S(2)}) collective-permute-start(f32[8,144,256]{2,1,0:T(8,128)S(1)} %pad_maximum_fusion.2), channel_id=1, source_target_pairs={{0,1},{1,0},{2,3},{3,2},{4,5},{5,4},{6,7},{7,6},{8,9},{9,8},{10,11... | collective-permute-start | bytes 3538952 | tf_op jit(solution)/shard_map/ppermute | solution.py:728
  161.0 2.8 %collective-permute-start.16 = (f32[16,256]{1,0:T(8,128)S(1)}, f32[16,256]{1,0:T(8,128)S(1)}, u32[]{:S(2)}, u32[]{:S(2)}) collective-permute-start(f32[16,256]{1,0:T(8,128)S(1)} %slice_add_fusion.9), channel_id=1, source_target_pairs={{0,1},{1,0},{2,3},{3,2},{4,5},{5,4},{6,7},{7,6},{8,9},{9,8},{10,11... | collective-permute-start | bytes 49160 | tf_op jit(solution)/shard_map/ppermute | solution.py:728
  161.6 2.9 %collective-permute-start.18 = (f32[16,8,256]{2,1,0:T(8,128)S(1)}, f32[16,8,256]{2,1,0:T(8,128)S(1)}, u32[]{:S(2)}, u32[]{:S(2)}) collective-permute-start(f32[16,8,256]{2,1,0:T(8,128)S(1)} %fusion.14.refs_0_), channel_id=1, source_target_pairs={{0,1},{1,0},{2,3},{3,2},{4,5},{5,4},{6,7},{7,6},{8,9},{9,8},{10,11... | collective-permute-start | bytes 393224 | tf_op jit(solution)/shard_map/ppermute | solution.py:728
  (6 other events, 14.7 us)
where the time goes:
time: 179 us; the launch traced here: 178 us
  waiting for transfers between devices  69.8 us (39%)
  Pallas kernels  59 us (33%)
  starting transfers between devices  27.5 us (15%)
  local copies, waits for them, and re-layouts  10.2 us (6%)
  other arithmetic  5.95 us (3%)
  between operations  5.68 us (3%)
    ppermute x28, waiting for transfers between devices, send(): return lax.ppermute(v, AXES, perm)  69.8 us
    ppermute x28, starting transfers between devices, send(): return lax.ppermute(v, AXES, perm)  27.5 us
    pallas_call x1, Pallas kernels, call_one(): pl.pallas_call(kernel_one, name='front_of_own_images', in_specs=[SMEM, pa...  17 us
    pallas_call x1, Pallas kernels, call_two(): pl.pallas_call(kernel_two, name='front_of_last_image', in_specs=[SMEM, SM...  12.5 us
    pallas_call x1, Pallas kernels, call_three(): pl.pallas_call(kernel_three, name='back_to_first_out', in_specs=[SMEM, SM...  11.6 us
    pallas_call x2, Pallas kernels, assemble(): pl.pallas_call(lambda *refs: assemble_kernel(units, *refs), name='assembl...  7.22 us
    pallas_call x1, Pallas kernels, call_four(): pl.pallas_call(kernel_four, name='back_to_images', in_specs=[SMEM, part((...  7.2 us
    unnamed x24, local copies, waits for them, and re-layouts  3.87 us
  transfers between devices with their start and end apart: 28, of which 15 were waited for; matrix products, arithmetic and copies ran while one was open for 4% of the time, Pallas kernels for 17%

commit v1 on v0

v1 whole, which is shorter than its diff:
```python
import math

import jax
import jax.numpy as jnp
from jax import lax
from jax.experimental import pallas as pl
from jax.experimental.pallas import tpu as pltpu
from jax.sharding import PartitionSpec as P

TEMB = 512
GROUPS = 32
SIDE = 16
WORK = 4
TOK = SIDE * SIDE
C = 256
PAD = TOK + 2 * SIDE
EPSILON = 1e-06
COUNT = float(TOK * (C // GROUPS))
CHUNK = 64
F32 = jnp.float32
BATCH, BUCKET = "batch", "bucket"
BF16 = jnp.bfloat16
NT = (((1,), (1,)), ((), ()))
TN = (((0,), (0,)), ((), ()))

R_OUT_BIAS, R_QUERY_BIAS, R_VALUE_BIAS, R_ATT_GAIN, R_ATT_SHIFT, R_SEC_BIAS = 0, 1, 2, 3, 4, 5
R_SEC_GAIN, R_SEC_SHIFT, R_EMB_BIAS, R_FIRST_GAIN, R_FIRST_SHIFT, R_CLOCKS = 6, 7, 8, 9, 10, 11
SUMS = 16


(W_FIRST_GAIN, W_FIRST_SHIFT, W_FIRST_CONV, W_EMBED_WEIGHT, W_EMBED_BIAS, W_SECOND_GAIN, W_SECOND_SHIFT, W_SECOND_CONV,
    W_SECOND_BIAS, W_ATTEND_GAIN, W_ATTEND_SHIFT, W_TRIPLE_WEIGHT, W_QUERY_BIAS, W_VALUE_BIAS, W_OUTPUT_WEIGHT,
    W_OUTPUT_BIAS) = WEIGHTS = range(16)
(X, COT, OUT, DMID, OUT1, ACT1, ACT2, STATS, G_TRIPLE, G_OUT, GT, GO, FULL_ACT, FULL_MID, KERNEL, GAIN, SHIFT, BASE,
    LAST, LOW, GIVE, KEEP, GIVE_C, KEEP_C, GRAD, BACK, SLOT, TO, NOTE, SMALL_ONE) = range(16, 46)


def dot(a, b, dims=(((1,), (0,)), ((), ()))):
    return lax.dot_general(a, b, dims, preferred_element_type=F32)


def sigmoid(v):
    return 0.5 * jnp.tanh(0.5 * v) + 0.5


def group_matrix():
    row = lax.broadcasted_iota(jnp.int32, (C, C), 0) // (C // GROUPS)
    col = lax.broadcasted_iota(jnp.int32, (C, C), 1) // (C // GROUPS)
    return (row == col).astype(F32).astype(BF16)


def group_mean(sums, same):
    high = sums.astype(BF16).astype(F32)
    rest = sums - high
    mid = rest.astype(BF16).astype(F32)
    low = rest - mid
    total = dot(jnp.concatenate([high, mid, low], axis=0).astype(BF16), same)
    return (total[0:8] + total[8:16] + total[16:24]) * (1.0 / COUNT)


def over_chunks(count, body):
    for image in range(count):
        for row in range(0, TOK, CHUNK):
            body(image, row)


def fold(v):
    return jnp.sum(v.reshape(v.shape[0] // 8, 8, v.shape[1]), axis=0)


def column_sums(count, parts, body, hold):
    out = [[] for _ in range(parts)]
    for image in range(count):
        totals = [None] * parts
        for row in range(0, TOK, CHUNK):
            for part, v in enumerate(body(image, row)):
                f = fold(v)
                totals[part] = f if totals[part] is None else totals[part] + f
        for part in range(parts):
            out[part].append(jnp.sum(totals[part], axis=0, keepdims=True))
    return [jnp.concatenate(rows + [jnp.zeros((8 - count, C), F32)], axis=0) for rows in out]


def edge_masks():
    column = lax.broadcasted_iota(jnp.int32, (CHUNK, C), 0) % SIDE
    return column == 0, column == SIDE - 1


def store_shifted(ref, image, row, v, backward):
    first, last = edge_masks()
    before = jnp.where(first, 0.0, pltpu.roll(v, 1, 0)).astype(BF16)
    after = jnp.where(last, 0.0, pltpu.roll(v, CHUNK - 1, 0)).astype(BF16)
    rows = pl.ds(row + SIDE, CHUNK)
    left, right = (after, before) if backward else (before, after)
    ref[image, rows, 0:C] = left
    ref[image, rows, C : 2 * C] = v.astype(BF16)
    ref[image, rows, 2 * C : 3 * C] = right


def clear_borders(ref, count):
    for i in range(count):
        ref[i, 0:SIDE, :] = jnp.zeros((SIDE, 3 * C), BF16)
        ref[i, PAD - SIDE : PAD, :] = jnp.zeros((SIDE, 3 * C), BF16)


def window(ref, count, di):
    return ref[0:count, SIDE * di : SIDE * di + TOK, :].reshape(count * TOK, 3 * C)


def convolve(shifted, image, kernel):
    total = None
    for di in range(3):
        part = dot(shifted[image, SIDE * di : SIDE * di + TOK, :], kernel[di])
        total = part if total is None else total + part
    return total


def norm_stats(count, ref, hold, same):
    (sums,) = column_sums(count, 1, lambda i, r: (ref[i, pl.ds(r, CHUNK), :],), hold)
    return sums_to_stats(count, sums, ref, hold, same)


def sums_to_stats(count, sums, ref, hold, same):
    mean = group_mean(sums, same)

    def squares(i, r):
        d = ref[i, pl.ds(r, CHUNK), :] - mean[i : i + 1, :]
        return (d * d,)

    (second,) = column_sums(count, 1, squares, hold)
    return mean, lax.rsqrt(group_mean(second, same) + EPSILON)


def front(
    count, x, cot, times, w, out, dmid, out1, act1, act2, stats, sums, g_triple, g_out,
    shifted, hold, mid, normed, triple, mixed, dmixed, dtriple, dnormed, same_ref, accumulate, need, ready,
):
    same = same_ref[...]

    def vec(name):
        return w[name][...]

    need(X)
    mean, scale = norm_stats(count, x, hold, same)
    for i in range(count):
        stats[i, 0:1, :] = mean[i : i + 1]
        stats[i, 1:2, :] = scale[i : i + 1]
    clear_borders(shifted, count)
    gain, shift = vec(W_FIRST_GAIN), vec(W_FIRST_SHIFT)

    def first(i, r):
        rows = pl.ds(r, CHUNK)
        pre = (x[i, rows, :] - stats[i, 0:1, :]) * stats[i, 1:2, :] * gain + shift
        act = pre * sigmoid(pre)
        act1[i, rows, :] = act.astype(BF16)
        store_shifted(shifted, i, r, act, False)

    over_chunks(count, first)
    ready(ACT1)

    half = TEMB // 2
    lane = lax.broadcasted_iota(jnp.int32, (8, half), 1).astype(F32)
    row = lax.broadcasted_iota(jnp.int32, (8, half), 0)
    frequency = jnp.exp(lane * (-math.log(10000.0) / (half - 1)))
    clock = jnp.zeros((8, half), F32)
    for i in range(count):
        clock = jnp.where(row == i, times[i], clock)
    angles = clock * frequency
    waves = jnp.concatenate([jnp.sin(angles), jnp.cos(angles)], axis=1)
    waves = waves * sigmoid(waves)
    need(W_EMBED_WEIGHT)
    stepped = lax.dot_general(
        waves, w[W_EMBED_WEIGHT][...], (((1,), (0,)), ((), ())),
        precision=lax.Precision.HIGHEST, preferred_element_type=F32,
    ) + vec(W_EMBED_BIAS)

    need(W_FIRST_CONV)
    kernel = w[W_FIRST_CONV]
    low = [kernel[di].reshape(3 * C, C).astype(BF16) for di in range(3)]
    for i in range(count):
        out1[i] = convolve(shifted, i, low) + stepped[i : i + 1]
    ready(OUT1)

    mean, scale = norm_stats(count, out1, hold, same)
    for i in range(count):
        stats[i, 2:3, :] = mean[i : i + 1]
        stats[i, 3:4, :] = scale[i : i + 1]
    gain2, shift2 = vec(W_SECOND_GAIN), vec(W_SECOND_SHIFT)

    def second(i, r):
        rows = pl.ds(r, CHUNK)
        pre = (out1[i, rows, :] - stats[i, 2:3, :]) * stats[i, 3:4, :] * gain2 + shift2
        act = pre * sigmoid(pre)
        act2[i, rows, :] = act.astype(BF16)
        store_shifted(shifted, i, r, act, False)

    over_chunks(count, second)
    ready(ACT2)
    need(W_SECOND_CONV)
    kernel = w[W_SECOND_CONV]
    low = [kernel[di].reshape(3 * C, C).astype(BF16) for di in range(3)]
    bias = vec(W_SECOND_BIAS)
    for i in range(count):
        mid[i] = convolve(shifted, i, low) + (x[i] + bias)

    mean, scale = norm_stats(count, mid, hold, same)
    for i in range(count):
        stats[i, 4:5, :] = mean[i : i + 1]
        stats[i, 5:6, :] = scale[i : i + 1]
        stats[i, 6:8, :] = jnp.zeros((2, C), F32)
    ready(STATS)
    gain3, shift3 = vec(W_ATTEND_GAIN), vec(W_ATTEND_SHIFT)

    def third(i, r):
        rows = pl.ds(r, CHUNK)
        pre = (mid[i, rows, :] - stats[i, 4:5, :]) * stats[i, 5:6, :] * gain3 + shift3
        normed[i, rows, :] = pre.astype(BF16)

    over_chunks(count, third)
    flat = normed[0:count].reshape(count * TOK, C)
    need(W_TRIPLE_WEIGHT)
    need(W_OUTPUT_WEIGHT)
    w_triple = w[W_TRIPLE_WEIGHT][...].astype(BF16)
    w_out = w[W_OUTPUT_WEIGHT][...].astype(BF16)
    for i in range(count):
        for part, name in enumerate((W_QUERY_BIAS, None, W_VALUE_BIAS)):
            v = dot(normed[i], w_triple[:, part * C : (part + 1) * C])
            if name is not None:
                v = v + vec(name)
            triple[i, :, part * C : (part + 1) * C] = v.astype(BF16)

    need(COT)
    cot_low = cot[0:count].reshape(count * TOK, C).astype(BF16)
    for i in range(count):
        dmixed[i] = dot(cot[i].astype(BF16), w_out, NT).astype(BF16)

    factor = 1.0 / math.sqrt(C)
    query_sum = jnp.zeros((1, C), F32)
    value_sum = jnp.zeros((1, C), F32)
    for i in range(count):
        q = triple[i, :, 0:C]
        k = triple[i, :, C : 2 * C]
        v = triple[i, :, 2 * C : 3 * C]
        dm = dmixed[i]
        s = dot(q, k, NT) * factor
        e = jnp.exp(s - jnp.max(s, axis=1, keepdims=True))
        p = e * (1.0 / jnp.sum(e, axis=1, keepdims=True))
        p_low = p.astype(BF16)
        mixed[i] = dot(p_low, v).astype(BF16)
        dp = dot(dm, v, NT)
        ds = (p * (dp - jnp.sum(p * dp, axis=1, keepdims=True))).astype(BF16)
        dq = dot(ds, k) * factor
        dk = dot(ds, q, TN) * factor
        dv = dot(p_low, dm, TN)
        query_sum = query_sum + jnp.sum(dq, axis=0, keepdims=True)
        value_sum = value_sum + jnp.sum(dv, axis=0, keepdims=True)
        dtriple[i, :, 0:C] = dq.astype(BF16)
        dtriple[i, :, C : 2 * C] = dk.astype(BF16)
        dtriple[i, :, 2 * C : 3 * C] = dv.astype(BF16)

    flat_mixed = mixed[0:count].reshape(count * TOK, C)
    bias = vec(W_OUTPUT_BIAS)
    for i in range(count):
        out[i] = dot(mixed[i], w_out) + (mid[i] + bias)
    ready(OUT)
    flat_d = dtriple[0:count].reshape(count * TOK, 3 * C)
    gw_out = dot(flat_mixed, cot_low, TN)
    gw_triple = dot(flat, flat_d, TN)
    if accumulate is None:
        g_out[...] = gw_out
        g_triple[...] = gw_triple
        ready(G_OUT)
        ready(G_TRIPLE)
    else:
        accumulate(gw_out, gw_triple)
    for i in range(count):
        dnormed[i] = dot(dtriple[i], w_triple, NT)

    def sums3(i, r):
        rows = pl.ds(r, CHUNK)
        d = dnormed[i, rows, :]
        unit = (mid[i, rows, :] - stats[i, 4:5, :]) * stats[i, 5:6, :]
        return d, d * unit, cot[i, rows, :]

    sum_d, sum_du, sum_cot = column_sums(count, 3, sums3, hold)
    first_mean = group_mean(sum_d * gain3, same)
    second_mean = group_mean(sum_du * gain3, same)

    def inner3(i, r):
        rows = pl.ds(r, CHUNK)
        d = dnormed[i, rows, :] * gain3
        scaled = stats[i, 5:6, :]
        unit = (mid[i, rows, :] - stats[i, 4:5, :]) * scaled
        m1 = first_mean[i : i + 1, :]
        m2 = second_mean[i : i + 1, :]
        g = (d - m1 - unit * m2) * scaled + cot[i, rows, :]
        dmid[i, rows, :] = g
        return (g,)

    (sum_mid,) = column_sums(count, 1, inner3, hold)
    ready(DMID)
    pieces = [
        jnp.sum(sum_cot, axis=0, keepdims=True), query_sum, value_sum,
        jnp.sum(sum_du, axis=0, keepdims=True), jnp.sum(sum_d, axis=0, keepdims=True),
        jnp.sum(sum_mid, axis=0, keepdims=True),
    ]
    return pieces


BIG = {
    W_FIRST_CONV: (3, 3, C, C), W_EMBED_WEIGHT: (TEMB, C), W_SECOND_CONV: (3, 3, C, C),
    W_TRIPLE_WEIGHT: (C, 3 * C), W_OUTPUT_WEIGHT: (C, C),
}
SMALL = tuple(name for name in WEIGHTS if name not in BIG)


def front_scratch(count):
    return [
        pltpu.VMEM((count, PAD, 3 * C), BF16),
        pltpu.VMEM((16, 8, C), F32),
        pltpu.VMEM((count, TOK, C), F32),
        pltpu.VMEM((count, TOK, C), BF16),
        pltpu.VMEM((count, TOK, 3 * C), BF16),
        pltpu.VMEM((count, TOK, C), BF16),
        pltpu.VMEM((count, TOK, C), BF16),
        pltpu.VMEM((count, TOK, 3 * C), BF16),
        pltpu.VMEM((count, TOK, C), F32),
        pltpu.VMEM((C, C), BF16),
    ]


def held(count):
    return [pltpu.VMEM(BIG[name], F32) for name in BIG] + [
        pltpu.VMEM((count, TOK, C), F32),
        pltpu.VMEM((count, TOK, C), F32),
        pltpu.VMEM((count, TOK, C), F32),
        pltpu.VMEM((count, TOK, C), F32),
        pltpu.VMEM((count, TOK, C), F32),
        pltpu.VMEM((count, TOK, C), BF16),
        pltpu.VMEM((count, TOK, C), BF16),
        pltpu.VMEM((count, 8, C), F32),
    ]


def small_copies(copies, small, held_small):
    for r, name in enumerate(SMALL):
        copies.start((SMALL_ONE, name), small[name], held_small.at[r])
    return {name: held_small.at[r] for r, name in enumerate(SMALL)}


HELD = tuple(BIG) + (X, COT, OUT, DMID, OUT1, ACT1, ACT2, STATS)


class Copies:
    def __init__(self, sems):
        self.sems = sems
        self.count = 0
        self.by_name = {}
        self.open = []

    def add(self, name, src, dst):
        copy = pltpu.make_async_copy(src, dst, self.sems.at[self.count])
        self.count += 1
        self.by_name[name] = copy
        return copy

    def start(self, name, src, dst):
        self.add(name, src, dst).start()
        self.open.append(name)

    def need(self, name):
        if name in self.open:
            self.open.remove(name)
            self.by_name[name].wait()

    def finish(self):
        for name in list(self.open):
            self.need(name)


def store_sums(sums, pieces, before=None):
    sums[...] = jnp.zeros((SUMS, C), F32) if before is None else before[...]
    for r, piece in enumerate(pieces):
        sums[r : r + 1, :] += piece


FRONT_SEMS = 48


def kernel_one(times, images, cotangent, *rest):
    small = dict(zip(SMALL, rest[: len(SMALL)]))
    rest = rest[len(SMALL) :]
    big = dict(zip(BIG, rest[: len(BIG)]))
    rest = rest[len(BIG) :]
    out, dmid, out1, act1, act2, stats, g_triple, g_out, sums = rest[:9]
    rest = rest[9:]
    scratch, rest = rest[:10], rest[10:]
    kept = dict(zip(HELD, rest[: len(HELD)]))
    v_triple, v_out, held_small, sems = rest[len(HELD) :]
    n = WORK - 1
    copies = Copies(sems)
    copies.start(X, images.at[0:n], kept[X])
    small = small_copies(copies, small, held_small)
    for name in (W_EMBED_WEIGHT, W_FIRST_CONV):
        copies.start(name, big[name], kept[name])
    scratch[-1][...] = group_matrix()
    moments = [times[0, 0, i].astype(F32) for i in range(n)]
    targets = {
        OUT: out.at[0:n], DMID: dmid.at[0:n], OUT1: out1.at[0:n], ACT1: act1.at[0:n], ACT2: act2.at[0:n],
        STATS: stats.at[0:n], G_TRIPLE: g_triple, G_OUT: g_out,
    }
    sources = {**kept, G_TRIPLE: v_triple, G_OUT: v_out}

    def need(name):
        if name == X:
            for first in [X, W_EMBED_WEIGHT, W_FIRST_CONV] + [(SMALL_ONE, v) for v in SMALL]:
                copies.need(first)
            for later in (W_SECOND_CONV, W_TRIPLE_WEIGHT, W_OUTPUT_WEIGHT):
                copies.start(later, big[later], kept[later])
            copies.start(COT, cotangent.at[0:n], kept[COT])
        if name == W_SECOND_CONV:
            for later in (W_SECOND_CONV, W_TRIPLE_WEIGHT, W_OUTPUT_WEIGHT, COT):
                copies.need(later)

    def ready(name):
        for v in {ACT2: (OUT1, ACT1, ACT2), DMID: (OUT, DMID, STATS, G_TRIPLE, G_OUT)}.get(name, ()):
            copies.start((TO, v), sources[v], targets[v])

    w = {**small, **{name: kept[name] for name in BIG}}
    pieces = front(
        n, kept[X], kept[COT], moments, w, kept[OUT], kept[DMID], kept[OUT1], kept[ACT1], kept[ACT2],
        kept[STATS], None, v_triple, v_out, *scratch, None, need, ready,
    )
    store_sums(sums, pieces)
    copies.finish()


ORDERS = (("xyz", "zxy"), ("yzx", "zxy"), ("yxz", "xyz"))
CHUNK_A, CHUNK_B, CHUNK_C = ORDERS[0], ORDERS[1], ORDERS[2]


def chip_bits():
    b, t = lax.axis_index(BUCKET), lax.axis_index(BATCH)
    return {"x": b % 2, "y": (b // 2) % 2, "z": (t // 2) % 2}


def owner_codes(order):
    bits = chip_bits()
    even, odd = (bits[o[0]] * 4 + bits[o[1]] * 2 + bits[o[2]] for o in order)
    return lax.axis_index(BATCH) % 2, even, odd


def scatter_unit(dst, unit, value, codes):
    core, even, odd = codes
    for block in range(16):
        half, low = divmod(block, 8)
        mine = jnp.where(core == half, 0, 1)
        code = even if half == 0 else odd
        dst[mine * 8 + (low ^ code), unit] = value[16 * block : 16 * block + 16]


def place_offset(counts, source):
    keeps = counts[0, 0] >= WORK
    return keeps, jnp.where(keeps, 0, source[0, 0] ^ lax.axis_index(BUCKET))


def kernel_two(n_bucket, times, counts, source, images, cotangent, *rest):
    arrived, rest = rest[: n_bucket - 1], rest[n_bucket - 1 :]
    small = dict(zip(SMALL, rest[: len(SMALL)]))
    rest = rest[len(SMALL) :]
    big = dict(zip(BIG, rest[: len(BIG)]))
    rest = rest[len(BIG) :]
    sums_in, gt_in, go_in, dmid_in, act2_in = rest[:5]
    rest = rest[9:]
    out, dmid, out1, act1, act2, stats, sums, give, keep, give_c, keep_c, last, notes = rest[:13]
    rest = rest[13:]
    scratch, rest = rest[:10], rest[10:]
    kept = dict(zip(HELD, rest[: len(HELD)]))
    full_act, full_shift, full_mid, blocks, blocks_c, v_triple, v_out, note, held_small, sems = rest[len(HELD) :]
    n = WORK - 1
    copies = Copies(sems)
    keeps, offset = place_offset(counts, source)

    def rows_of(k):
        return arrived[k - 1].at[0:TOK]

    choose = copies.add(X, images.at[n], kept[X].at[0])
    pl.when(keeps)(lambda: choose.start())
    pl.when(jnp.logical_not(keeps) & (offset == 0))(
        lambda: pltpu.make_async_copy(images.at[WORK], kept[X].at[0], sems.at[0]).start()
    )
    for k in range(1, n_bucket):
        pl.when(offset == k)(
            lambda k=k: pltpu.make_async_copy(rows_of(k), kept[X].at[0], sems.at[0]).start()
        )
    copies.open.append(X)
    copies.start(W_FIRST_CONV, big[W_FIRST_CONV], kept[W_FIRST_CONV])
    for k in range(1, n_bucket):
        copies.start((NOTE, k), arrived[k - 1].at[TOK : TOK + 8], note.at[k])
    small = small_copies(copies, small, held_small)
    copies.start(W_EMBED_WEIGHT, big[W_EMBED_WEIGHT], kept[W_EMBED_WEIGHT])
    same = scratch[-1]
    same[...] = group_matrix()
    codes, codes_c = owner_codes(CHUNK_A), owner_codes(CHUNK_C)
    first_wave = [X, W_EMBED_WEIGHT, W_FIRST_CONV] + [(SMALL_ONE, v) for v in SMALL]
    for name in first_wave + [(NOTE, k) for k in range(1, n_bucket)]:
        copies.need(name)
    for name in (W_SECOND_CONV, W_TRIPLE_WEIGHT, W_OUTPUT_WEIGHT):
        copies.start(name, big[name], kept[name])
    copies.start(COT, cotangent.at[n : n + 1], kept[COT])
    copies.start(GT, gt_in, v_triple)
    copies.start(GO, go_in, v_out)
    copies.start(FULL_ACT, act2_in.at[0:n], full_act.at[0:n])
    copies.start(FULL_MID, dmid_in.at[0:n], full_mid)
    moment = jnp.where(keeps, times[0, 0, n], times[0, 0, WORK]).astype(F32)
    moment = jnp.full((1, 1), moment, F32)
    for k in range(1, n_bucket):
        moment = jnp.where(offset == k, note[k, 0:1, 0:1], moment)

    lane = lax.broadcasted_iota(jnp.int32, (1, C), 1)
    clock = jnp.where(lane == n, moment, 0.0)
    for i in range(n):
        clock = jnp.where(lane == i, times[0, 0, i].astype(F32), clock)
    notes[...] = jnp.zeros(notes.shape, F32)
    notes[0:1, :] = clock
    if n_bucket == 4:
        even = codes[0] == 0
        neighbour = jnp.where(even, note[1, 0:1, 1:2], note[2, 0:1, 1:2])
        first = jnp.where(even, 1.0, 2.0)
        notes[1:2, :] = jnp.broadcast_to(jnp.where(neighbour == 3.0, 1.0, 0.0), (1, C))
        notes[2:3, :] = jnp.broadcast_to(jnp.where(neighbour == first, 1.0, 0.0), (1, C))

    def accumulate(gw_out, gw_triple):
        scatter_unit(blocks_c, 3, gw_out + v_out[...], codes_c)
        total = gw_triple + v_triple[...]
        for part in range(3):
            scatter_unit(blocks_c, part, total[:, part * C : (part + 1) * C], codes_c)

    targets = {
        OUT: out.at[n:WORK], DMID: dmid.at[n:WORK], OUT1: out1.at[n:WORK], ACT1: act1.at[n:WORK],
        ACT2: act2.at[n:WORK], STATS: stats.at[n:WORK],
    }
    def need(name):
        if name == W_SECOND_CONV:
            for later in (W_SECOND_CONV, W_TRIPLE_WEIGHT, W_OUTPUT_WEIGHT, COT, GT, GO, FULL_ACT, FULL_MID):
                copies.need(later)

    def ready(name):
        if name == DMID:
            for v in targets:
                copies.start((TO, v), kept[v], targets[v])
            copies.start((TO, LAST), kept[X].at[0], last)
            copies.start((TO, GIVE_C), blocks_c.at[8:16], give_c)
            copies.start((TO, KEEP_C), blocks_c.at[0:8], keep_c)

    w = {**small, **{name: kept[name] for name in BIG}}
    pieces = front(
        1, kept[X], kept[COT], [moment], w, kept[OUT], kept[DMID], kept[OUT1], kept[ACT1], kept[ACT2],
        kept[STATS], None, None, None, *scratch, accumulate, need, ready,
    )
    store_sums(sums, pieces, sums_in)

    clear_borders(full_shift, WORK)

    def early(i, r):
        store_shifted(full_shift, i, r, full_mid[i, pl.ds(r, CHUNK), :], True)

    def late(i, r):
        store_shifted(full_shift, i + n, r, kept[DMID][i, pl.ds(r, CHUNK), :], True)

    over_chunks(n, early)
    over_chunks(1, late)
    full_act[n] = kept[ACT2][0]
    act = full_act[...].reshape(WORK * TOK, C)
    for di in range(3):
        g = dot(act, window(full_shift, WORK, 2 - di), TN)
        for dj in range(3):
            scatter_unit(blocks, di * 3 + dj, g[:, dj * C : (dj + 1) * C], codes)
    copies.start((TO, GIVE), blocks.at[8:16], give)
    copies.start((TO, KEEP), blocks.at[0:8], keep)
    copies.finish()


def swish_norm_backward(dact, values, base, stats, row, gain, shift, hold, same, dpre, write):
    def sums_of(i, r):
        rows = pl.ds(r, CHUNK)
        unit = (base[i, rows, :] - stats[i, row : row + 1, :]) * stats[i, row + 1 : row + 2, :]
        pre = unit * gain + shift
        s = sigmoid(pre)
        d = dact[i, rows, :] * (s * (1.0 + pre * (1.0 - s)))
        dpre[i, rows, :] = d
        return d, d * unit

    sum_d, sum_du = column_sums(WORK, 2, sums_of, hold)
    first_mean = group_mean(sum_d * gain, same)
    second_mean = group_mean(sum_du * gain, same)

    def inner(i, r):
        rows = pl.ds(r, CHUNK)
        scaled = stats[i, row + 1 : row + 2, :]
        unit = (base[i, rows, :] - stats[i, row : row + 1, :]) * scaled
        m1 = first_mean[i : i + 1, :]
        m2 = second_mean[i : i + 1, :]
        return write(i, r, (dpre[i, rows, :] * gain - m1 - unit * m2) * scaled)

    sums = column_sums(WORK, 1, inner, hold)[0]
    return sum_d, sum_du, sums


def conv_backward(shifted, kernel, dact):
    low = [jnp.concatenate([kernel[di, dj].astype(BF16) for dj in range(3)], axis=1) for di in range(3)]
    for i in range(WORK):
        total = None
        for di in range(3):
            part = dot(shifted[i, SIDE * (2 - di) : SIDE * (2 - di) + TOK, :], low[di], NT)
            total = part if total is None else total + part
        dact[i] = total


def kernel_three(notes, dmid_in, out1_in, act1_in, stats, sums_in, kernel_in, gain_ref, shift_ref,
                 give, keep, low, sums, rows_out,
                 shifted, hold, dact, dpre, same_ref, dmid, out1, act1, kernel, blocks, v_low, v_small, sems):
    copies = Copies(sems)
    copies.start(GAIN, gain_ref, v_small.at[0])
    copies.start(SHIFT, shift_ref, v_small.at[1])
    gain_ref, shift_ref = v_small.at[0], v_small.at[1]
    copies.start(DMID, dmid_in, dmid)
    copies.start(KERNEL, kernel_in, kernel)
    copies.start(OUT1, out1_in, out1)
    copies.start(ACT1, act1_in, act1)
    same_ref[...] = group_matrix()
    same = same_ref[...]
    codes = owner_codes(CHUNK_B)
    clear_borders(shifted, WORK)
    copies.need(DMID)

    def load(i, r):
        store_shifted(shifted, i, r, dmid[i, pl.ds(r, CHUNK), :], True)

    over_chunks(WORK, load)
    copies.need(KERNEL)
    conv_backward(shifted, kernel, dact)
    for name in (OUT1, ACT1, GAIN, SHIFT):
        copies.need(name)

    def write(i, r, g):
        v_low[i, pl.ds(r, CHUNK), :] = g.astype(BF16)
        store_shifted(shifted, i, r, g, True)
        return (g,)

    sum_d, sum_du, sum_first = swish_norm_backward(
        dact, None, out1, stats, 2, gain_ref[...], shift_ref[...], hold, same, dpre, write
    )
    copies.start((TO, LOW), v_low, low)

    def tap(di, carry):
        rows = pl.ds(pl.multiple_of(SIDE * (2 - di), SIDE), TOK)
        g = dot(act1[...].reshape(WORK * TOK, C), shifted[:, rows, :].reshape(WORK * TOK, 3 * C), TN)
        for dj in range(3):
            scatter_unit(blocks, di * 3 + dj, g[:, dj * C : (dj + 1) * C], codes)
        return carry

    lax.fori_loop(0, 3, tap, 0)
    copies.start((TO, GIVE), blocks.at[8:16], give)
    copies.start((TO, KEEP), blocks.at[0:8], keep)
    sums[...] = sums_in[...]
    sums[R_SEC_GAIN : R_SEC_GAIN + 1, :] = jnp.sum(sum_du, axis=0, keepdims=True)
    sums[R_SEC_SHIFT : R_SEC_SHIFT + 1, :] = jnp.sum(sum_d, axis=0, keepdims=True)
    sums[R_EMB_BIAS : R_EMB_BIAS + 1, :] = jnp.sum(sum_first, axis=0, keepdims=True)
    core = lax.axis_index(BATCH) % 2
    place = chip_place() * 2 + core
    spots = lax.broadcasted_iota(jnp.int32, (4, C), 0) * C + lax.broadcasted_iota(jnp.int32, (4, C), 1)
    clocks = jnp.zeros((4, C), F32)
    for i in range(WORK):
        clocks = jnp.where(spots == place * WORK + i, notes[0:1, i : i + 1], clocks)
    sums[R_CLOCKS : R_CLOCKS + 4, :] = clocks
    four = sum_first[0:WORK]
    both = jnp.concatenate([four, four], axis=0)
    half = lax.broadcasted_iota(jnp.int32, (8, C), 0) // WORK
    rows_out[...] = jnp.where(half == core, both, 0.0)
    copies.finish()


def kernel_four(n_bucket, counts, source, images, last, dmid_in, low_in, stats, sums_in, rows_in, kernel_in, gain_ref, shift_ref,
                grad, back, sums,
                shifted, hold, dact, dpre, same_ref, dmid, base, low, kernel, v_back, v_small, sems):
    n = WORK - 1
    copies = Copies(sems)
    copies.start(GAIN, gain_ref, v_small.at[0])
    copies.start(SHIFT, shift_ref, v_small.at[1])
    gain_ref, shift_ref = v_small.at[0], v_small.at[1]
    copies.start(LOW, low_in, low)
    copies.start(KERNEL, kernel_in, kernel)
    copies.start(BASE, images.at[0:n], base.at[0:n])
    copies.start(LAST, last, base.at[n])
    copies.start(DMID, dmid_in, dmid)
    same_ref[...] = group_matrix()
    same = same_ref[...]
    clear_borders(shifted, WORK)
    copies.need(LOW)

    def load(i, r):
        store_shifted(shifted, i, r, low[i, pl.ds(r, CHUNK), :].astype(F32), True)

    over_chunks(WORK, load)
    copies.need(KERNEL)
    conv_backward(shifted, kernel, dact)
    for name in (BASE, LAST, DMID, GAIN, SHIFT):
        copies.need(name)

    def write(i, r, g):
        rows = pl.ds(r, CHUNK)
        dpre[i, rows, :] = g + dmid[i, rows, :]
        return (g,)

    sum_d, sum_du, _ = swish_norm_backward(
        dact, None, base, stats, 0, gain_ref[...], shift_ref[...], hold, same, dpre, write
    )
    copies.start((TO, GRAD), dpre.at[0:n], grad.at[0:n])
    keeps, offset = place_offset(counts, source)
    if n_bucket == 4:
        even = lax.axis_index(BATCH) % 2 == 0
        first = jnp.where(even, 1, 2)
        v_back[0] = jnp.where((offset & first) != 0, dpre[n], 0.0)
        v_back[1] = jnp.where(offset == 3 - first, dpre[n], 0.0)
    else:
        for k in range(1, n_bucket):
            v_back[k - 1] = jnp.where(offset == k, dpre[n], 0.0)
    copies.start((TO, BACK), v_back, back)
    dmid[n] = jnp.where(keeps, dpre[n], 0.0)
    copies.start((TO, SLOT), dmid.at[n], grad.at[n])
    sums[0:SUMS] = sums_in[...]
    sums[SUMS : SUMS + 8] = rows_in[...]
    sums[R_FIRST_GAIN : R_FIRST_GAIN + 1, :] = jnp.sum(sum_du, axis=0, keepdims=True)
    sums[R_FIRST_SHIFT : R_FIRST_SHIFT + 1, :] = jnp.sum(sum_d, axis=0, keepdims=True)
    copies.finish()


def kernel_pack(times, counts, source, images, out, sem):
    copy = pltpu.make_async_copy(images.at[WORK], out.at[0:TOK], sem)
    copy.start()
    _, offset = place_offset(counts, source)
    lane = lax.broadcasted_iota(jnp.int32, (8, C), 1)
    moment = times[0, 0, WORK].astype(F32)
    out[TOK : TOK + 8] = jnp.where(lane == 0, moment, jnp.where(lane == 1, offset.astype(F32), 0.0))
    copy.wait()


def whole(shape):
    return pl.BlockSpec(shape, lambda *_: (0,) * len(shape), memory_space=pltpu.VMEM)


def part(shape, first):
    return pl.BlockSpec(shape, lambda *_: (first,) + (0,) * (len(shape) - 1), memory_space=pltpu.VMEM)


SMEM = pl.BlockSpec(memory_space=pltpu.SMEM)
ANY = pl.BlockSpec(memory_space=pl.ANY)
HBM = pl.BlockSpec(memory_space=pltpu.HBM)


def params(mebibytes=26):
    return pltpu.CompilerParams(vmem_limit_bytes=mebibytes * 1024 * 1024)


def shape(dims, dtype=F32):
    return jax.ShapeDtypeStruct(dims, dtype)


def weight_specs(w):
    return [whole(w[name].shape) for name in WEIGHTS]


def call_pack(timesteps, counts, source, images):
    return pl.pallas_call(
        kernel_pack,
        name="pack_spare",
        in_specs=[SMEM, SMEM, SMEM, ANY],
        out_specs=pl.BlockSpec(memory_space=pltpu.VMEM),
        out_shape=shape((TOK + 8, C)),
        scratch_shapes=[pltpu.SemaphoreType.DMA],
        cost_estimate=pl.CostEstimate(flops=20_000_000_000, bytes_accessed=1_000_000, transcendentals=0),
        compiler_params=params(),
    )(timesteps, counts, source, images)


VMEM = pl.BlockSpec(memory_space=pltpu.VMEM)
IMAGE_ARRAYS = (
    ((WORK, TOK, C), F32), ((WORK, TOK, C), F32), ((WORK, TOK, C), F32), ((WORK, TOK, C), BF16), ((WORK, TOK, C), BF16),
    ((WORK, 8, C), F32),
)


def call_one(timesteps, images, cot, w):
    n = WORK - 1
    return pl.pallas_call(
        kernel_one,
        name="front_of_own_images",
        in_specs=[SMEM, HBM, HBM] + [HBM] * (len(SMALL) + len(BIG)),
        out_specs=[ANY] * 8 + [VMEM],
        out_shape=[shape(*s) for s in IMAGE_ARRAYS] + [shape((C, 3 * C)), shape((C, C)), shape((SUMS, C))],
        scratch_shapes=front_scratch(n) + held(n)
        + [pltpu.VMEM((C, 3 * C), F32), pltpu.VMEM((C, C), F32), pltpu.VMEM((len(SMALL), 1, C), F32),
           pltpu.SemaphoreType.DMA((FRONT_SEMS,))],
        cost_estimate=pl.CostEstimate(flops=20_000_000_000, bytes_accessed=1_000_000, transcendentals=0),
        compiler_params=params(),
    )(timesteps, images, cot, *[w[name] for name in SMALL], *[w[name] for name in BIG])


def call_two(timesteps, counts, source, images, cot, arrived, w, early):
    out, dmid, out1, act1, act2, stats, g_triple, g_out, sums = early
    n_bucket = len(arrived) + 1
    first = 5 + len(arrived) + len(SMALL) + len(BIG)
    half, half_c = (8, 9, 16, C), (8, 4, 16, C)
    return pl.pallas_call(
        lambda *refs: kernel_two(n_bucket, *refs),
        name="front_of_last_image",
        in_specs=[SMEM, SMEM, SMEM, HBM, HBM] + [ANY] * len(arrived) + [HBM] * (len(SMALL) + len(BIG))
        + [VMEM] + [ANY] * 8,
        out_specs=[ANY] * 6 + [VMEM] + [ANY] * 5 + [VMEM],
        out_shape=[shape(*s) for s in IMAGE_ARRAYS]
        + [shape((SUMS, C)), shape(half), shape(half), shape(half_c), shape(half_c), shape((TOK, C)), shape((8, C))],
        scratch_shapes=front_scratch(1) + held(1)
        + [
            pltpu.VMEM((WORK, TOK, C), BF16), pltpu.VMEM((WORK, PAD, 3 * C), BF16), pltpu.VMEM((WORK - 1, TOK, C), F32),
            pltpu.VMEM((16, 9, 16, C), F32), pltpu.VMEM((16, 4, 16, C), F32), pltpu.VMEM((C, 3 * C), F32), pltpu.VMEM((C, C), F32),
            pltpu.VMEM((n_bucket, 8, C), F32), pltpu.VMEM((len(SMALL), 1, C), F32),
            pltpu.SemaphoreType.DMA((FRONT_SEMS + n_bucket,)),
        ],
        input_output_aliases={first + 5: 0, first + 3: 1, first + 6: 2, first + 7: 3, first + 4: 4, first + 8: 5},
        cost_estimate=pl.CostEstimate(flops=20_000_000_000, bytes_accessed=1_000_000, transcendentals=0),
        compiler_params=params(),
    )(
        timesteps, counts, source, images, cot, *arrived, *[w[name] for name in SMALL], *[w[name] for name in BIG],
        sums, g_triple, g_out, dmid, act2, out, out1, act1, stats,
    )


def back_scratch():
    return [
        pltpu.VMEM((WORK, PAD, 3 * C), BF16),
        pltpu.VMEM((16, 8, C), F32),
        pltpu.VMEM((WORK, TOK, C), F32),
        pltpu.VMEM((WORK, TOK, C), F32),
        pltpu.VMEM((C, C), BF16),
    ]


def call_three(notes, dmid, out1, act1, stats, sums, w):
    full = (WORK, TOK, C)
    half = (8, 9, 16, C)
    return pl.pallas_call(
        kernel_three,
        name="back_to_first_out",
        in_specs=[VMEM, ANY, ANY, ANY, VMEM, VMEM, HBM, HBM, HBM],
        out_specs=[ANY, ANY, ANY, VMEM, VMEM],
        out_shape=[shape(half), shape(half), shape(full, BF16), shape((SUMS, C)), shape((8, C))],
        scratch_shapes=back_scratch()
        + [
            pltpu.VMEM(full, F32), pltpu.VMEM(full, F32), pltpu.VMEM(full, BF16), pltpu.VMEM((3, 3, C, C), F32),
            pltpu.VMEM((16, 9, 16, C), F32), pltpu.VMEM(full, BF16), pltpu.VMEM((2, 1, C), F32),
            pltpu.SemaphoreType.DMA((12,)),
        ],
        compiler_params=params(),
    )(notes, dmid, out1, act1, stats, sums, w[W_SECOND_CONV], w[W_SECOND_GAIN], w[W_SECOND_SHIFT])


def call_four(n_bucket, counts, source, images, last, dmid, low, stats, sums, rows, w):
    full = (WORK, TOK, C)
    backs = 2 if n_bucket == 4 else n_bucket - 1
    return pl.pallas_call(
        lambda *refs: kernel_four(n_bucket, *refs),
        name="back_to_images",
        in_specs=[SMEM, SMEM, HBM, ANY, ANY, ANY, VMEM, VMEM, VMEM, HBM, HBM, HBM],
        out_specs=[ANY, ANY, VMEM],
        out_shape=[shape((WORK + 1, TOK, C)), shape((backs, TOK, C)), shape((SUMS + 8, C))],
        scratch_shapes=back_scratch()
        + [
            pltpu.VMEM(full, F32), pltpu.VMEM(full, F32), pltpu.VMEM(full, BF16), pltpu.VMEM((3, 3, C, C), F32),
            pltpu.VMEM((backs, TOK, C), F32), pltpu.VMEM((2, 1, C), F32), pltpu.SemaphoreType.DMA((12,)),
        ],
        compiler_params=params(),
    )(counts, source, images, last, dmid, low, stats, sums, rows, w[W_FIRST_CONV], w[W_FIRST_GAIN], w[W_FIRST_SHIFT])


def assemble_kernel(*refs):
    first, second, triple, out = refs[6:10]
    copies = Copies(refs[-1])
    for n, order in enumerate((CHUNK_A, CHUNK_C, CHUNK_B)):
        core, even, odd = owner_codes(order)
        for half in range(2):
            src = refs[2 * n + half]
            holder = core if half == 0 else 1 - core
            code = jnp.where(holder == 0, even, odd)
            for low in range(8):
                block = holder * 8 + (low ^ code)
                rows = pl.ds(pl.multiple_of(block * 16, 16), 16)
                if n != 1:
                    copies.start((n, half, low), src.at[low], (second if n == 0 else first).at[:, rows, :])
                    continue
                for p in range(3):
                    copies.start((n, half, low, p), src.at[low, p], triple.at[rows, p * C : (p + 1) * C])
                copies.start((n, half, low), src.at[low, 3], out.at[rows, :])
    copies.finish()


def assemble(*halves):
    return pl.pallas_call(
        assemble_kernel,
        name="assemble",
        in_specs=[ANY] * 6,
        out_specs=[ANY] * 4,
        out_shape=[shape((9, C, C)), shape((9, C, C)), shape((C, 3 * C)), shape((C, C))],
        scratch_shapes=[pltpu.SemaphoreType.DMA((16 + 16 + 16 * 4,))],
        cost_estimate=pl.CostEstimate(flops=1, bytes_accessed=1, transcendentals=0),
        compiler_params=params(2),
    )(*halves)


def high_code():
    b, t = lax.axis_index(BUCKET), lax.axis_index(BATCH)
    return (t // 4) * (lax.axis_size(BUCKET) // 4) + b // 4


def chip_place():
    bits = chip_bits()
    many = lax.axis_size(BUCKET) * lax.axis_size(BATCH) // 16
    return (bits["x"] * 4 + bits["y"] * 2 + bits["z"]) * many + high_code()


def embed_kernel(devices, order, gathered, sums, out, rows):
    core = lax.axis_index(BATCH) % 2
    bits = chip_bits()
    mine = bits["x"] * 4 + bits["y"] * 2 + bits["z"]
    high = high_code()
    many = devices // 16
    weight = {"x": 4, "y": 2, "z": 1}
    for place in range(devices // 2):
        rest, code = place % many, place // many
        turned = [
            sum(((code >> (2 - n)) & 1) * weight[o[n]] for n in range(3)) for o in order
        ]
        code = jnp.where(core == 0, turned[0], turned[1]) ^ mine
        rows[code * many + (rest ^ high)] = gathered[place]
    count = WORK * devices
    grads = rows[...].reshape(count, C)
    half = TEMB // 2
    moments = []
    for n in range(0, count, C):
        size = min(C, count)
        row = lax.broadcasted_iota(jnp.int32, (size, C), 0)
        lane = lax.broadcasted_iota(jnp.int32, (size, C), 1)
        clocks = sums[R_CLOCKS + n // C : R_CLOCKS + n // C + 1, :]
        moments.append(jnp.sum(jnp.where(row == lane, clocks, 0.0), axis=1, keepdims=True))
    moments = jnp.concatenate(moments, axis=0) if len(moments) > 1 else moments[0]
    frequency = jnp.exp(
        lax.broadcasted_iota(jnp.int32, (count, half), 1).astype(F32) * (-math.log(10000.0) / (half - 1))
    )
    angles = moments * frequency
    waves = jnp.concatenate([jnp.sin(angles), jnp.cos(angles)], axis=1)
    waves = waves * sigmoid(waves)
    out[...] = lax.dot_general(waves, grads, TN, precision=lax.Precision.HIGHEST, preferred_element_type=F32)


def embed_gradient(devices, order, gathered, sums):
    return pl.pallas_call(
        lambda *refs: embed_kernel(devices, order, *refs),
        name="embed_gradient",
        in_specs=[VMEM, VMEM],
        out_specs=VMEM,
        out_shape=shape((TEMB, C)),
        scratch_shapes=[pltpu.VMEM((devices // 2, 8, C), F32)],
        cost_estimate=pl.CostEstimate(flops=1, bytes_accessed=1, transcendentals=0),
        compiler_params=params(),
    )(gathered, sums)


AXES = (BUCKET, BATCH)


def solution(mesh):
    n_bucket, n_batch = mesh.shape[BUCKET], mesh.shape[BATCH]
    devices = n_bucket * n_batch

    def flips(fn):
        pairs = []
        for b in range(n_bucket):
            for t in range(n_batch):
                nb, nt = fn(b, t)
                pairs.append((b * n_batch + t, nb * n_batch + nt))
        return pairs

    def by_core(even, odd):
        def fn(b, t):
            kind, bit = even if t % 2 == 0 else odd
            return (b ^ bit, t) if kind == 0 else (b, t ^ bit)

        return flips(fn)

    x, y, z = (0, 1), (0, 2), (1, 2)
    core_perm = flips(lambda b, t: (b, t ^ 1))
    links = {"x": x, "y": y, "z": z}
    rest = []
    bit = 4
    while bit < n_bucket:
        rest.append((0, bit))
        bit *= 2
    bit = 4
    while bit < n_batch:
        rest.append((1, bit))
        bit *= 2
    rest_perms = [by_core(s, s) for s in rest]
    bucket_perms = [flips(lambda b, t, k=k: (b ^ k, t)) for k in range(1, n_bucket)]

    def send(v, perm):
        return lax.ppermute(v, AXES, perm)

    def after(v, *others):
        return lax.optimization_barrier((v,) + others)[0]

    def held_by(v, other):
        row = other.reshape(-1, C)[0:1]
        return v + 0.0 * row.reshape((1,) * (v.ndim - 1) + (C,))

    class Chunk:
        def __init__(self, order, give, keep, units):
            self.perms = [by_core(links[p], links[q]) for p, q in zip(*order)]
            self.rows = units * 16
            self.stage = 0
            self.size = give.shape
            self.keep = keep.reshape(2, 2, 2, self.rows, C)
            self.got = send(give, core_perm).reshape(2, 2, 2, self.rows, C)
            self.extra = None

        def step(self, *deps, late=None):
            n_rest = len(rest_perms)
            k = self.stage
            self.stage += 1
            if k < 3:
                out, self.keep = self.keep[1] + self.got[1], self.keep[0] + self.got[0]
                perm = self.perms[k]
            else:
                self.take()
                if k < 3 + n_rest:
                    perm = rest_perms[k - 3]
                else:
                    if k == 3 + n_rest:
                        self.keep = self.keep[None]
                    j = k - 3 - n_rest
                    perm = self.perms[2 - j] if j < 3 else core_perm
                out = self.keep
                if self.extra is not None and perm is not core_perm:
                    sums, rows = self.extra
                    out = jnp.concatenate([out.reshape(-1, C), sums, rows.reshape(-1, C)], axis=0)
            if late is not None:
                out = held_by(out, late)
            out = after(out, *deps)
            self.got = send(out, perm)
            return out

        def take(self):
            n_rest = len(rest_perms)
            k = self.stage - 1
            got = self.got
            if k == 3:
                self.keep = self.keep + got
                return
            if self.extra is not None:
                sums, rows = self.extra
                size = self.keep.size // C
                rows = jnp.concatenate([rows, got[size + SUMS :].reshape(rows.shape)], axis=0)
                self.extra = sums + got[size : size + SUMS], rows
                got = got[:size]
            got = got.reshape(self.keep.shape)
            if k <= 3 + n_rest:
                self.keep = self.keep + got
            else:
                self.keep = jnp.concatenate([self.keep, got], axis=0)

        def halves(self):
            dims = (8, self.rows // 16, 16, C)
            return self.keep.reshape(dims), self.got.reshape(dims)

    def shards(images, timesteps, counts, source, cotangent, *weights):
        w = dict(zip(WEIGHTS, weights))
        w = {k: v.reshape(1, C) if v.ndim == 1 else v for k, v in w.items()}
        slots = images[0, 0]
        cot = cotangent[0, 0]

        spare = call_pack(timesteps, counts, source, slots)
        arrived = [send(spare, p) for p in bucket_perms]
        early = call_one(timesteps, slots, cot, w)
        out, dmid, out1, act1, act2, stats, sums, give_a, keep_a, give_c, keep_c, last, notes = call_two(
            timesteps, counts, source, slots, cot, arrived, w, early
        )
        chunk_a = Chunk(CHUNK_A, give_a, keep_a, 9)
        chunk_c = Chunk(CHUNK_C, give_c, keep_c, 4)
        give_b, keep_b, low, sums, rows = call_three(notes, dmid, out1, act1, stats, sums, w)
        chunk_b = Chunk(CHUNK_B, give_b, keep_b, 9)

        tie = chunk_a.step()
        tie = chunk_c.step(tie)
        tie = chunk_b.step(tie)
        grad, back, extra = call_four(n_bucket, counts, source, slots, last, dmid, after(low, tie), stats, sums, rows, w)
        extra = extra + send(extra, core_perm)
        total = 3 + len(rest_perms) + 3
        home = None
        for k in range(1, total):
            if k == 3:
                chunk_c.extra = extra[:SUMS], extra[None, SUMS:]
            tie = chunk_a.step(tie)
            tie = chunk_c.step(tie)
            tie = chunk_b.step(tie, late=home if k == 4 else None)
            if n_bucket == 4:
                if k == 1:
                    hop = send(after(back[0], tie), by_core(x, y))
                if k == 2:
                    turn = after(jnp.where(notes[1:2] != 0.0, hop, back[1]), tie)
                    got = send(turn, by_core(y, x))
                if k == 3:
                    home = jnp.where(notes[2:3] != 0.0, hop, got)
                    grad = lax.dynamic_update_slice(grad, home[None], (WORK, 0, 0))
            elif k == 1:
                home = send(back[0], bucket_perms[0])
                for n in range(2, n_bucket):
                    home = home + send(back[n - 1], bucket_perms[n - 1])
                grad = lax.dynamic_update_slice(grad, home[None], (WORK, 0, 0))
        tie = chunk_a.step(tie)
        tie = chunk_c.step(tie)
        tie = chunk_b.step(tie)
        sums, rows = chunk_c.extra
        g_embed = embed_gradient(devices, CHUNK_C, rows, sums)
        g_first, g_second, g_triple, g_out = assemble(*chunk_a.halves(), *chunk_c.halves(), *chunk_b.halves())

        def vec(r):
            return sums[r]

        return (
            out[None, None], grad[None, None],
            vec(R_FIRST_GAIN), vec(R_FIRST_SHIFT), g_first.reshape(3, 3, C, C), g_embed, vec(R_EMB_BIAS),
            vec(R_SEC_GAIN), vec(R_SEC_SHIFT), g_second.reshape(3, 3, C, C), vec(R_SEC_BIAS),
            vec(R_ATT_GAIN), vec(R_ATT_SHIFT), g_triple, vec(R_QUERY_BIAS), vec(R_VALUE_BIAS),
            g_out, vec(R_OUT_BIAS),
        )

    placed = (
        P(BATCH, BUCKET, None, None, None), P(BATCH, BUCKET, None), P(BATCH, BUCKET),
        P(BATCH, BUCKET), P(BATCH, BUCKET, None, None, None),
    ) + (P(),) * 16
    return jax.shard_map(
        shards,
        mesh=mesh,
        in_specs=placed,
        out_specs=(P(BATCH, BUCKET, None, None, None),) * 2 + (P(),) * 16,
        check_vma=False,
    )
```

time: 179 us -> 123 us (0.69)
  Pallas kernels: 59 us -> 35.1 us
  waiting for transfers between devices: 69.8 us -> 46.1 us
  local copies, waits for them, and re-layouts: 10.2 us -> 2.83 us
  starting transfers between devices: 27.5 us -> 33.1 us
  other arithmetic: 5.95 us -> 2.46 us
  between operations: 5.68 us -> 2.82 us
    pallas_call x7, Pallas kernels: 59 us -> 35.1 us  [the longest x1 10.4 us: call_one(): pl.pallas_call(kernel_one, name='front_of_own_images', in_specs=[SMEM, HB...]
    ppermute x28 -> x33, waiting for transfers between devices: 69.8 us -> 46.1 us  [send(): return lax.ppermute(v, AXES, perm)]
    ppermute x28 -> x33, starting transfers between devices: 27.5 us -> 33.1 us  [send(): return lax.ppermute(v, AXES, perm)]
    slice x10 -> x6, local copies, waits for them, and re-layouts: 4.2 us -> 0.14 us  [the longest x3 0.11 us: step(): out, self.keep = (self.keep[1] + self.got[1], self.keep[0] + self.got[0])]
    unnamed x24 -> x44, local copies, waits for them, and re-layouts: 3.87 us -> 2.05 us
  transfers between devices with their start and end apart: 28 -> 33, of which waited for: 15 -> 18; matrix products, arithmetic and copies ran while one was open for 4% -> 3% of each run, Pallas kernels for 17% -> 18%
where the time goes in v1:
time: 123 us; the launch traced here: 122 us
  waiting for transfers between devices  46.1 us (37%)
  Pallas kernels  35.1 us (29%)
  starting transfers between devices  33.1 us (27%)
  local copies, waits for them, and re-layouts  2.83 us (2%)
  between operations  2.82 us (2%)
  other arithmetic  2.46 us (2%)
    ppermute x33, waiting for transfers between devices, send(): return lax.ppermute(v, AXES, perm)  46.1 us
    ppermute x33, starting transfers between devices, send(): return lax.ppermute(v, AXES, perm)  33.1 us
    pallas_call x1, Pallas kernels, call_one(): pl.pallas_call(kernel_one, name='front_of_own_images', in_specs=[SMEM, HB...  10.4 us
    pallas_call x1, Pallas kernels, call_two(): pl.pallas_call(lambda *refs: kernel_two(n_bucket, *refs), name='front_of_...  8.99 us
    pallas_call x1, Pallas kernels, call_three(): pl.pallas_call(kernel_three, name='back_to_first_out', in_specs=[VMEM, AN...  5.79 us
    pallas_call x1, Pallas kernels, call_four(): pl.pallas_call(lambda *refs: kernel_four(n_bucket, *refs), name='back_to_...  4.08 us
    pallas_call x1, Pallas kernels, assemble(): pl.pallas_call(assemble_kernel, name='assemble', in_specs=[ANY] * 6, out_...  3.32 us
  transfers between devices with their start and end apart: 33, of which 18 were waited for; matrix products, arithmetic and copies ran while one was open for 3% of the time, Pallas kernels for 18%

profile of v1, /device:TPU:0, one launch (start us, length us, event | category | flops | bytes accessed | tf_op | source)
XLA Modules:
  0.0 122.4 jit_solution(16824921682152142455)
XLA Ops:
  2.0 1.3 %copy-done.2 = f32[1,1,5,256,256]{4,3,2,1,0:T(8,128)S(1)} copy-done((f32[1,1,5,256,256]{4,3,2,1,0:T(8,128)S(1)}, f32[1,1,5,256,256]{4,3,2,1,0:T(8,128)}, u32[]{:S(2)}) %copy-start.2) | copy-done | bytes 1310744
  4.7 4.0 %collective-permute-start.2 = (f32[264,256]{1,0:T(8,128)S(1)}, f32[264,256]{1,0:T(8,128)S(1)}, u32[]{:S(2)}, u32[]{:S(2)}) collective-permute-start(f32[264,256]{1,0:T(8,128)S(1)} %pack_spare.1), channel_id=1, source_target_pairs={{0,24},{1,25},{2,26},{3,27},{4,28},{5,29},{6,30},{7,31},{8,16},{9,... | collective-permute-start | bytes 811016 | tf_op jit(solution)/shard_map/ppermute | solution.py:1016
  9.4 10.4 %front_of_own_images.1 = (f32[4,256,256]{2,1,0:T(8,128)}, f32[4,256,256]{2,1,0:T(8,128)S(1)}, f32[4,256,256]{2,1,0:T(8,128)S(1)}, bf16[4,256,256]{2,1,0:T(8,128)...) custom-call(s32[1,1,5]{2,1,0:T(1,128)S(1)} %copy-done.19, ...), custom_call_target="tpu_custom_call" | custom-call | flops 20000000000 | bytes 1000000 | tf_op jit(solution)/shard_map/front_of_own_images/pallas_call | solution.py:796
  19.8 1.1 collective-permute-done.1.refs_6_
  21.2 9.0 %front_of_last_image.1 = (f32[4,256,256]{2,1,0:T(8,128)}, f32[4,256,256]{2,1,0:T(8,128)S(1)}, f32[4,256,256]{2,1,0:T(8,128)S(1)}, bf16[4,256,256]{2,1,0:T(8,128)...) custom-call(s32[1,1,5]{2,1,0:T(1,128)S(1)} %copy-done.19, ...), custom_call_target="tpu_custom_call", output_to_operand_aliasing={{0}: (29, {}), {1}: (27, {}), {2}: (30, {}), {3}: (31, {}),... | custom-call | flops 20000000000 | bytes 1000000 | tf_op jit(solution)/shard_map/front_of_last_image/pallas_call | solution.py:815
  30.8 5.8 %back_to_first_out.1 = (f32[8,9,16,256]{3,2,1,0:T(8,128)S(1)}, f32[8,9,16,256]{3,2,1,0:T(8,128)S(1)}, bf16[4,256,256]{2,1,0:T(8,128)(2,1)S(1)}, f32[16,256]{1,0:T(8,128)S(1)}, f32[8,256]{1,0:T(8,128)S(1)}) custom-call(f32[8,256]{1,0:T(8,128)S(1)} %get-tuple-element.89.notes, f32[4,256,256]{2,1,0:T(8,128)S(1)} %get-tuple-element.88.dmid_in.refs_4_, ...), custom_call_target="tpu_custom_call" | custom-call | tf_op jit(solution)/shard_map/back_to_first_out/pallas_call | solution.py:852
  37.1 1.6 %collective-permute-start.8 = (f32[2,2,144,256]{3,2,1,0:T(8,128)S(1)}, f32[2,2,144,256]{3,2,1,0:T(8,128)S(1)}, u32[]{:S(2)}, u32[]{:S(2)}) collective-permute-start(f32[2,2,144,256]{3,2,1,0:T(8,128)S(1)} %bitcast.208), channel_id=1, source_target_pairs={{0,8},{1,3},{2,10},{3,1},{4,12},{5,7},{6,14},{7,5},{8,0},{9,11},{1... | collective-permute-start | bytes 1769480 | tf_op jit(solution)/shard_map/ppermute | solution.py:1016
  39.8 1.5 %collective-permute-start.6 = (f32[2,2,144,256]{3,2,1,0:T(8,128)S(1)}, f32[2,2,144,256]{3,2,1,0:T(8,128)S(1)}, u32[]{:S(2)}, u32[]{:S(2)}) collective-permute-start(f32[2,2,144,256]{3,2,1,0:T(8,128)S(1)} %bitcast.209), channel_id=1, source_target_pairs={{0,16},{1,3},{2,18},{3,1},{4,20},{5,7},{6,22},{7,5},{8,24},{9,11},... | collective-permute-start | bytes 1769480 | tf_op jit(solution)/shard_map/ppermute | solution.py:1016
  41.3 4.1 %back_to_images.1 = (f32[5,256,256]{2,1,0:T(8,128)}, f32[2,256,256]{2,1,0:T(8,128)S(1)}, f32[24,256]{1,0:T(8,128)S(1)}) custom-call(s32[1,1]{1,0:T(1,128)S(6)} %copy.56.counts.refs_1_.refs_0_, s32[1,1]{1,0:T(1,128)S(6)} %copy.57.source.refs_2_.refs_1_, f32[5,256,256]{2,1,0:T(8,128)S(1)} %bitcast.147, f32[256,256]{1,0:T(8,128)S(1)} %get-tuple-element.87.refs_3_, ...), custom_call_target="tpu_custom_call" | custom-call | tf_op jit(solution)/shard_map/back_to_images/pallas_call | solution.py:871
  46.7 3.2 %collective-permute-done.8 = f32[2,2,144,256]{3,2,1,0:T(8,128)S(1)} collective-permute-done((f32[2,2,144,256]{3,2,1,0:T(8,128)S(1)}, f32[2,2,144,256]{3,2,1,0:T(8,128)S(1)}, u32[]{:S(2)}, u32[]{:S(2)}) %collective-permute-start.8) | collective-permute-done | bytes 589856 | tf_op jit(solution)/shard_map/ppermute | solution.py:1016
  50.0 1.5 %collective-permute-start.11 = (f32[2,64,256]{2,1,0:T(8,128)S(1)}, f32[2,64,256]{2,1,0:T(8,128)S(1)}, u32[]{:S(2)}, u32[]{:S(2)}) collective-permute-start(f32[2,64,256]{2,1,0:T(8,128)S(1)} %get-tuple-element.109), channel_id=1, source_target_pairs={{0,8},{1,17},{2,10},{3,19},{4,12},{5,21},{6,14},{7,23},{8,0},{9,25... | collective-permute-start | bytes 393224 | tf_op jit(solution)/shard_map/ppermute | solution.py:1016
  51.6 1.1 collective-permute-done.6
  52.8 1.7 %collective-permute-start.12 = (f32[2,144,256]{2,1,0:T(8,128)S(1)}, f32[2,144,256]{2,1,0:T(8,128)S(1)}, u32[]{:S(2)}, u32[]{:S(2)}) collective-permute-start(f32[2,144,256]{2,1,0:T(8,128)S(1)} %get-tuple-element.108), channel_id=1, source_target_pairs={{0,16},{1,9},{2,18},{3,11},{4,20},{5,13},{6,22},{7,15},{8,24},{9,1... | collective-permute-start | bytes 884744 | tf_op jit(solution)/shard_map/ppermute | solution.py:1016
  54.5 2.0 %collective-permute-start.10 = (f32[2,144,256]{2,1,0:T(8,128)S(1)}, f32[2,144,256]{2,1,0:T(8,128)S(1)}, u32[]{:S(2)}, u32[]{:S(2)}) collective-permute-start(f32[2,144,256]{2,1,0:T(8,128)S(1)} %get-tuple-element.110), channel_id=1, source_target_pairs={{0,2},{1,9},{2,0},{3,11},{4,6},{5,13},{6,4},{7,15},{8,10},{9,1},{1... | collective-permute-start | bytes 884744 | tf_op jit(solution)/shard_map/ppermute | solution.py:1016
  56.5 5.3 %collective-permute-done.9 = f32[256,256]{1,0:T(8,128)S(1)} collective-permute-done((f32[256,256]{1,0:T(8,128)S(1)}, f32[256,256]{1,0:T(8,128)S(1)}, u32[]{:S(2)}, u32[]{:S(2)}) %collective-permute-start.9) | collective-permute-done | bytes 262176 | tf_op jit(solution)/shard_map/ppermute | solution.py:1016
  61.9 1.9 %collective-permute-start.16 = (f32[144,256]{1,0:T(8,128)S(1)}, f32[144,256]{1,0:T(8,128)S(1)}, u32[]{:S(2)}, u32[]{:S(2)}) collective-permute-start(f32[144,256]{1,0:T(8,128)S(1)} %fusion.6), channel_id=1, source_target_pairs={{0,2},{1,17},{2,0},{3,19},{4,6},{5,21},{6,4},{7,23},{8,10},{9,25},... | collective-permute-start | bytes 442376 | tf_op jit(solution)/shard_map/ppermute | solution.py:1016
  64.0 1.1 collective-permute-start.19
  65.8 2.4 %collective-permute-done.15 = f32[64,256]{1,0:T(8,128)S(1)} collective-permute-done((f32[64,256]{1,0:T(8,128)S(1)}, f32[64,256]{1,0:T(8,128)S(1)}, u32[]{:S(2)}, u32[]{:S(2)}) %collective-permute-start.15) | collective-permute-done | bytes 65568 | tf_op jit(solution)/shard_map/ppermute | solution.py:1016
  68.2 2.7 %collective-permute-start.18 = (f32[144,256]{1,0:T(8,128)S(1)}, f32[144,256]{1,0:T(8,128)S(1)}, u32[]{:S(2)}, u32[]{:S(2)}) collective-permute-start(f32[144,256]{1,0:T(8,128)S(1)} %fusion.5), channel_id=1, source_target_pairs={{0,4},{1,5},{2,6},{3,7},{4,0},{5,1},{6,2},{7,3},{8,12},{9,13},{10,... | collective-permute-start | bytes 442376 | tf_op jit(solution)/shard_map/ppermute | solution.py:1016
  71.3 2.7 %collective-permute-start.22 = (f32[144,256]{1,0:T(8,128)S(1)}, f32[144,256]{1,0:T(8,128)S(1)}, u32[]{:S(2)}, u32[]{:S(2)}) collective-permute-start(f32[144,256]{1,0:T(8,128)S(1)} %fusion.3), channel_id=1, source_target_pairs={{0,4},{1,5},{2,6},{3,7},{4,0},{5,1},{6,2},{7,3},{8,12},{9,13},{10,... | collective-permute-start | bytes 442376 | tf_op jit(solution)/shard_map/ppermute | solution.py:1016
  73.9 11.5 %collective-permute-done.17 = f32[88,256]{1,0:T(8,128)S(1)} collective-permute-done((f32[88,256]{1,0:T(8,128)S(1)}, f32[88,256]{1,0:T(8,128)S(1)}, u32[]{:S(2)}, u32[]{:S(2)}) %collective-permute-start.17) | collective-permute-done | bytes 90144 | tf_op jit(solution)/shard_map/ppermute | solution.py:1016
  86.3 2.0 %collective-permute-start.20 = (f32[96,256]{1,0:T(8,128)S(1)}, f32[96,256]{1,0:T(8,128)S(1)}, u32[]{:S(2)}, u32[]{:S(2)}) collective-permute-start(f32[96,256]{1,0:T(8,128)S(1)} %pad_maximum_fusion.14), channel_id=1, source_target_pairs={{0,2},{1,3},{2,0},{3,1},{4,6},{5,7},{6,4},{7,5},{8,10},{9,11},{10,... | collective-permute-start | bytes 294920 | tf_op jit(solution)/shard_map/ppermute | solution.py:1016
  89.4 3.1 %collective-permute-done.20 = f32[96,256]{1,0:T(8,128)S(1)} collective-permute-done((f32[96,256]{1,0:T(8,128)S(1)}, f32[96,256]{1,0:T(8,128)S(1)}, u32[]{:S(2)}, u32[]{:S(2)}) %collective-permute-start.20) | collective-permute-done | bytes 98336 | tf_op jit(solution)/shard_map/ppermute | solution.py:1016
  95.2 5.0 %collective-permute-done.23 = f32[176,256]{1,0:T(8,128)S(1)} collective-permute-done((f32[176,256]{1,0:T(8,128)S(1)}, f32[176,256]{1,0:T(8,128)S(1)}, u32[]{:S(2)}, u32[]{:S(2)}) %collective-permute-start.23) | collective-permute-done | bytes 180256 | tf_op jit(solution)/shard_map/ppermute | solution.py:1016
  100.4 1.2 collective-permute-start.27
  102.6 2.0 %collective-permute-done.28 = f32[2,144,256]{2,1,0:T(8,128)S(1)} collective-permute-done((f32[2,144,256]{2,1,0:T(8,128)S(1)}, f32[2,144,256]{2,1,0:T(8,128)S(1)}, u32[]{:S(2)}, u32[]{:S(2)}) %collective-permute-start.28) | collective-permute-done | bytes 294944 | tf_op jit(solution)/shard_map/ppermute | solution.py:1016
  104.6 1.2 collective-permute-start.31
  105.8 3.0 %collective-permute-done.26 = f32[336,256]{1,0:T(8,128)S(1)} collective-permute-done((f32[336,256]{1,0:T(8,128)S(1)}, f32[336,256]{1,0:T(8,128)S(1)}, u32[]{:S(2)}, u32[]{:S(2)}) %collective-permute-start.26) | collective-permute-done | bytes 344096 | tf_op jit(solution)/shard_map/ppermute | solution.py:1016
  108.9 2.6 %collective-permute-done.27 = f32[4,144,256]{2,1,0:T(8,128)S(1)} collective-permute-done((f32[4,144,256]{2,1,0:T(8,128)S(1)}, f32[4,144,256]{2,1,0:T(8,128)S(1)}, u32[]{:S(2)}, u32[]{:S(2)}) %collective-permute-start.27) | collective-permute-done | bytes 589856 | tf_op jit(solution)/shard_map/ppermute | solution.py:1016
  111.6 3.5 %collective-permute-done.31 = f32[4,144,256]{2,1,0:T(8,128)S(1)} collective-permute-done((f32[4,144,256]{2,1,0:T(8,128)S(1)}, f32[4,144,256]{2,1,0:T(8,128)S(1)}, u32[]{:S(2)}, u32[]{:S(2)}) %collective-permute-start.31) | collective-permute-done | bytes 589856 | tf_op jit(solution)/shard_map/ppermute | solution.py:1016
  115.9 1.9 %embed_gradient.1 = f32[512,256]{1,0:T(8,128)} custom-call(f32[16,8,256]{2,1,0:T(8,128)S(1)} %fusion.9.refs_0_, f32[16,256]{1,0:T(8,128)S(1)} %slice_add_fusion.19.refs_1_), custom_call_target="tpu_custom_call" | custom-call | flops 1 | bytes 1 | tf_op jit(solution)/shard_map/embed_gradient/pallas_call | solution.py:966
  118.9 3.3 %assemble.1 = (f32[9,256,256]{2,1,0:T(8,128)}, f32[9,256,256]{2,1,0:T(8,128)}, f32[256,768]{1,0:T(8,128)}, f32[256,256]{1,0:T(8,128)}) custom-call(f32[8,9,16,256]{3,2,1,0:T(8,128)S(1)} %pad_maximum_fusion.refs_0_, f32[8,9,16,256]{3,2,1,0:T(8,128)S(1)} %bitcast.148, f32[8,4,16,256]{3,2,1,0:T(8,128)S(1)} %pad_maximum_fusion.6.refs_2_, ...), custom_call_target="tpu_custom_call" | custom-call | flops 1 | bytes 1 | tf_op jit(solution)/shard_map/assemble/pallas_call | solution.py:908
  (140 shorter events, 15.1 us)
Async XLA Ops:
  4.7 15.1 %collective-permute-start.2 = (f32[264,256]{1,0:T(8,128)S(1)}, f32[264,256]{1,0:T(8,128)S(1)}, u32[]{:S(2)}, u32[]{:S(2)}) collective-permute-start(f32[264,256]{1,0:T(8,128)S(1)} %pack_spare.1), channel_id=1, source_target_pairs={{0,24},{1,25},{2,26},{3,27},{4,28},{5,29},{6,30},{7,31},{8,16},{9,... | collective-permute-start | bytes 811016 | tf_op jit(solution)/shard_map/ppermute | solution.py:1016
  8.6 12.3 %collective-permute-start.1 = (f32[264,256]{1,0:T(8,128)S(1)}, f32[264,256]{1,0:T(8,128)S(1)}, u32[]{:S(2)}, u32[]{:S(2)}) collective-permute-start(f32[264,256]{1,0:T(8,128)S(1)} %pack_spare.1), channel_id=1, source_target_pairs={{0,16},{1,17},{2,18},{3,19},{4,20},{5,21},{6,22},{7,23},{8,24},{9,... | collective-permute-start | bytes 811016 | tf_op jit(solution)/shard_map/ppermute | solution.py:1016
  9.1 12.1 %collective-permute-start = (f32[264,256]{1,0:T(8,128)S(1)}, f32[264,256]{1,0:T(8,128)S(1)}, u32[]{:S(2)}, u32[]{:S(2)}) collective-permute-start(f32[264,256]{1,0:T(8,128)S(1)} %pack_spare.1), channel_id=1, source_target_pairs={{0,8},{1,9},{2,10},{3,11},{4,12},{5,13},{6,14},{7,15},{8,0},{9,1},... | collective-permute-start | bytes 811016 | tf_op jit(solution)/shard_map/ppermute | solution.py:1016
  30.2 6.7 %collective-permute-start.5 = (f32[8,9,16,256]{3,2,1,0:T(8,128)S(1)}, f32[8,9,16,256]{3,2,1,0:T(8,128)S(1)}, u32[]{:S(2)}, u32[]{:S(2)}) collective-permute-start(f32[8,9,16,256]{3,2,1,0:T(8,128)S(1)} %get-tuple-element.100), channel_id=1, source_target_pairs={{0,1},{1,0},{2,3},{3,2},{4,5},{5,4},{6,7},{7,6},{8,9},{9,8},{10,11... | collective-permute-start | bytes 3538952 | tf_op jit(solution)/shard_map/ppermute | solution.py:1016
  30.3 6.5 %collective-permute-start.4 = (f32[8,4,16,256]{3,2,1,0:T(8,128)S(1)}, f32[8,4,16,256]{3,2,1,0:T(8,128)S(1)}, u32[]{:S(2)}, u32[]{:S(2)}) collective-permute-start(f32[8,4,16,256]{3,2,1,0:T(8,128)S(1)} %get-tuple-element.98), channel_id=1, source_target_pairs={{0,1},{1,0},{2,3},{3,2},{4,5},{5,4},{6,7},{7,6},{8,9},{9,8},{10,11... | collective-permute-start | bytes 1572872 | tf_op jit(solution)/shard_map/ppermute | solution.py:1016
  36.6 2.9 %collective-permute-start.3 = (f32[8,9,16,256]{3,2,1,0:T(8,128)S(1)}, f32[8,9,16,256]{3,2,1,0:T(8,128)S(1)}, u32[]{:S(2)}, u32[]{:S(2)}) collective-permute-start(f32[8,9,16,256]{3,2,1,0:T(8,128)S(1)} %get-tuple-element.96), channel_id=1, source_target_pairs={{0,1},{1,0},{2,3},{3,2},{4,5},{5,4},{6,7},{7,6},{8,9},{9,8},{10,11... | collective-permute-start | bytes 3538952 | tf_op jit(solution)/shard_map/ppermute | solution.py:1016
  37.1 12.8 %collective-permute-start.8 = (f32[2,2,144,256]{3,2,1,0:T(8,128)S(1)}, f32[2,2,144,256]{3,2,1,0:T(8,128)S(1)}, u32[]{:S(2)}, u32[]{:S(2)}) collective-permute-start(f32[2,2,144,256]{3,2,1,0:T(8,128)S(1)} %bitcast.208), channel_id=1, source_target_pairs={{0,8},{1,3},{2,10},{3,1},{4,12},{5,7},{6,14},{7,5},{8,0},{9,11},{1... | collective-permute-start | bytes 1769480 | tf_op jit(solution)/shard_map/ppermute | solution.py:1016
  38.7 8.0 %collective-permute-start.7 = (f32[2,2,64,256]{3,2,1,0:T(8,128)S(1)}, f32[2,2,64,256]{3,2,1,0:T(8,128)S(1)}, u32[]{:S(2)}, u32[]{:S(2)}) collective-permute-start(f32[2,2,64,256]{3,2,1,0:T(8,128)S(1)} %bitcast.214), channel_id=1, source_target_pairs={{0,16},{1,9},{2,18},{3,11},{4,20},{5,13},{6,22},{7,15},{8,24},{9,1... | collective-permute-start | bytes 786440 | tf_op jit(solution)/shard_map/ppermute | solution.py:1016
  39.8 12.9 %collective-permute-start.6 = (f32[2,2,144,256]{3,2,1,0:T(8,128)S(1)}, f32[2,2,144,256]{3,2,1,0:T(8,128)S(1)}, u32[]{:S(2)}, u32[]{:S(2)}) collective-permute-start(f32[2,2,144,256]{3,2,1,0:T(8,128)S(1)} %bitcast.209), channel_id=1, source_target_pairs={{0,16},{1,3},{2,18},{3,1},{4,20},{5,7},{6,22},{7,5},{8,24},{9,11},... | collective-permute-start | bytes 1769480 | tf_op jit(solution)/shard_map/ppermute | solution.py:1016
  50.0 6.5 %collective-permute-start.11 = (f32[2,64,256]{2,1,0:T(8,128)S(1)}, f32[2,64,256]{2,1,0:T(8,128)S(1)}, u32[]{:S(2)}, u32[]{:S(2)}) collective-permute-start(f32[2,64,256]{2,1,0:T(8,128)S(1)} %get-tuple-element.109), channel_id=1, source_target_pairs={{0,8},{1,17},{2,10},{3,19},{4,12},{5,21},{6,14},{7,23},{8,0},{9,25... | collective-permute-start | bytes 393224 | tf_op jit(solution)/shard_map/ppermute | solution.py:1016
  52.8 9.0 %collective-permute-start.9 = (f32[256,256]{1,0:T(8,128)S(1)}, f32[256,256]{1,0:T(8,128)S(1)}, u32[]{:S(2)}, u32[]{:S(2)}) collective-permute-start(f32[256,256]{1,0:T(8,128)S(1)} %slice_bitcast_fusion), channel_id=1, source_target_pairs={{0,8},{1,17},{2,10},{3,19},{4,12},{5,21},{6,14},{7,23},{8,0},{9,25... | collective-permute-start | bytes 786440 | tf_op jit(solution)/shard_map/ppermute | solution.py:1016
  52.8 9.0 %collective-permute-start.12 = (f32[2,144,256]{2,1,0:T(8,128)S(1)}, f32[2,144,256]{2,1,0:T(8,128)S(1)}, u32[]{:S(2)}, u32[]{:S(2)}) collective-permute-start(f32[2,144,256]{2,1,0:T(8,128)S(1)} %get-tuple-element.108), channel_id=1, source_target_pairs={{0,16},{1,9},{2,18},{3,11},{4,20},{5,13},{6,22},{7,15},{8,24},{9,1... | collective-permute-start | bytes 884744 | tf_op jit(solution)/shard_map/ppermute | solution.py:1016
  54.5 9.5 %collective-permute-start.10 = (f32[2,144,256]{2,1,0:T(8,128)S(1)}, f32[2,144,256]{2,1,0:T(8,128)S(1)}, u32[]{:S(2)}, u32[]{:S(2)}) collective-permute-start(f32[2,144,256]{2,1,0:T(8,128)S(1)} %get-tuple-element.110), channel_id=1, source_target_pairs={{0,2},{1,9},{2,0},{3,11},{4,6},{5,13},{6,4},{7,15},{8,10},{9,1},{1... | collective-permute-start | bytes 884744 | tf_op jit(solution)/shard_map/ppermute | solution.py:1016
  61.9 6.3 %collective-permute-start.16 = (f32[144,256]{1,0:T(8,128)S(1)}, f32[144,256]{1,0:T(8,128)S(1)}, u32[]{:S(2)}, u32[]{:S(2)}) collective-permute-start(f32[144,256]{1,0:T(8,128)S(1)} %fusion.6), channel_id=1, source_target_pairs={{0,2},{1,17},{2,0},{3,19},{4,6},{5,21},{6,4},{7,23},{8,10},{9,25},... | collective-permute-start | bytes 442376 | tf_op jit(solution)/shard_map/ppermute | solution.py:1016
  63.8 4.4 %collective-permute-start.15 = (f32[64,256]{1,0:T(8,128)S(1)}, f32[64,256]{1,0:T(8,128)S(1)}, u32[]{:S(2)}, u32[]{:S(2)}) collective-permute-start(f32[64,256]{1,0:T(8,128)S(1)} %fusion.12), channel_id=1, source_target_pairs={{0,2},{1,3},{2,0},{3,1},{4,6},{5,7},{6,4},{7,5},{8,10},{9,11},{10,... | collective-permute-start | bytes 196616 | tf_op jit(solution)/shard_map/ppermute | solution.py:1016
  64.0 7.2 %collective-permute-start.19 = (f32[144,256]{1,0:T(8,128)S(1)}, f32[144,256]{1,0:T(8,128)S(1)}, u32[]{:S(2)}, u32[]{:S(2)}) collective-permute-start(f32[144,256]{1,0:T(8,128)S(1)} %fusion.7), channel_id=1, source_target_pairs={{0,8},{1,17},{2,10},{3,19},{4,12},{5,21},{6,14},{7,23},{8,0},{9,25... | collective-permute-start | bytes 442376 | tf_op jit(solution)/shard_map/ppermute | solution.py:1016
  65.1 20.3 %collective-permute-start.13 = (f32[256,256]{1,0:T(8,128)S(1)}, f32[256,256]{1,0:T(8,128)S(1)}, u32[]{:S(2)}, u32[]{:S(2)}) collective-permute-start(f32[256,256]{1,0:T(8,128)S(1)} %bitcast_select_fusion), channel_id=1, source_target_pairs={{0,16},{1,9},{2,18},{3,11},{4,20},{5,13},{6,22},{7,15},{8,24},{9,1... | collective-permute-start | bytes 786440 | tf_op jit(solution)/shard_map/ppermute | solution.py:1016
  68.2 18.0 %collective-permute-start.18 = (f32[144,256]{1,0:T(8,128)S(1)}, f32[144,256]{1,0:T(8,128)S(1)}, u32[]{:S(2)}, u32[]{:S(2)}) collective-permute-start(f32[144,256]{1,0:T(8,128)S(1)} %fusion.5), channel_id=1, source_target_pairs={{0,4},{1,5},{2,6},{3,7},{4,0},{5,1},{6,2},{7,3},{8,12},{9,13},{10,... | collective-permute-start | bytes 442376 | tf_op jit(solution)/shard_map/ppermute | solution.py:1016
  70.9 14.5 %collective-permute-start.17 = (f32[88,256]{1,0:T(8,128)S(1)}, f32[88,256]{1,0:T(8,128)S(1)}, u32[]{:S(2)}, u32[]{:S(2)}) collective-permute-start(f32[88,256]{1,0:T(8,128)S(1)} %pad_maximum_fusion.15), channel_id=1, source_target_pairs={{0,4},{1,5},{2,6},{3,7},{4,0},{5,1},{6,2},{7,3},{8,12},{9,13},{10,... | collective-permute-start | bytes 270344 | tf_op jit(solution)/shard_map/ppermute | solution.py:1016
  71.3 17.1 %collective-permute-start.22 = (f32[144,256]{1,0:T(8,128)S(1)}, f32[144,256]{1,0:T(8,128)S(1)}, u32[]{:S(2)}, u32[]{:S(2)}) collective-permute-start(f32[144,256]{1,0:T(8,128)S(1)} %fusion.3), channel_id=1, source_target_pairs={{0,4},{1,5},{2,6},{3,7},{4,0},{5,1},{6,2},{7,3},{8,12},{9,13},{10,... | collective-permute-start | bytes 442376 | tf_op jit(solution)/shard_map/ppermute | solution.py:1016
  86.2 6.3 %collective-permute-start.21 = (f32[1,144,256]{2,1,0:T(8,128)S(1)}, f32[1,144,256]{2,1,0:T(8,128)S(1)}, u32[]{:S(2)}, u32[]{:S(2)}) collective-permute-start(f32[1,144,256]{2,1,0:T(8,128)S(1)} %bitcast.179), channel_id=1, source_target_pairs={{0,2},{1,17},{2,0},{3,19},{4,6},{5,21},{6,4},{7,23},{8,10},{9,25},... | collective-permute-start | bytes 442376 | tf_op jit(solution)/shard_map/ppermute | solution.py:1016
  86.3 6.2 %collective-permute-start.20 = (f32[96,256]{1,0:T(8,128)S(1)}, f32[96,256]{1,0:T(8,128)S(1)}, u32[]{:S(2)}, u32[]{:S(2)}) collective-permute-start(f32[96,256]{1,0:T(8,128)S(1)} %pad_maximum_fusion.14), channel_id=1, source_target_pairs={{0,2},{1,3},{2,0},{3,1},{4,6},{5,7},{6,4},{7,5},{8,10},{9,11},{10,... | collective-permute-start | bytes 294920 | tf_op jit(solution)/shard_map/ppermute | solution.py:1016
  88.4 6.7 %collective-permute-start.25 = (f32[1,144,256]{2,1,0:T(8,128)S(1)}, f32[1,144,256]{2,1,0:T(8,128)S(1)}, u32[]{:S(2)}, u32[]{:S(2)}) collective-permute-start(f32[1,144,256]{2,1,0:T(8,128)S(1)} %get-tuple-element.122), channel_id=1, source_target_pairs={{0,8},{1,17},{2,10},{3,19},{4,12},{5,21},{6,14},{7,23},{8,0},{9,25... | collective-permute-start | bytes 442376 | tf_op jit(solution)/shard_map/ppermute | solution.py:1016
  92.6 7.6 %collective-permute-start.23 = (f32[176,256]{1,0:T(8,128)S(1)}, f32[176,256]{1,0:T(8,128)S(1)}, u32[]{:S(2)}, u32[]{:S(2)}) collective-permute-start(f32[176,256]{1,0:T(8,128)S(1)} %pad_maximum_fusion.12), channel_id=1, source_target_pairs={{0,8},{1,17},{2,10},{3,19},{4,12},{5,21},{6,14},{7,23},{8,0},{9,25... | collective-permute-start | bytes 540680 | tf_op jit(solution)/shard_map/ppermute | solution.py:1016
  93.6 6.7 %collective-permute-start.24 = (f32[2,144,256]{2,1,0:T(8,128)S(1)}, f32[2,144,256]{2,1,0:T(8,128)S(1)}, u32[]{:S(2)}, u32[]{:S(2)}) collective-permute-start(f32[2,144,256]{2,1,0:T(8,128)S(1)} %pad_maximum_fusion.9), channel_id=1, source_target_pairs={{0,16},{1,9},{2,18},{3,11},{4,20},{5,13},{6,22},{7,15},{8,24},{9,1... | collective-permute-start | bytes 884744 | tf_op jit(solution)/shard_map/ppermute | solution.py:1016
  95.1 9.5 %collective-permute-start.28 = (f32[2,144,256]{2,1,0:T(8,128)S(1)}, f32[2,144,256]{2,1,0:T(8,128)S(1)}, u32[]{:S(2)}, u32[]{:S(2)}) collective-permute-start(f32[2,144,256]{2,1,0:T(8,128)S(1)} %pad_maximum_fusion.10), channel_id=1, source_target_pairs={{0,2},{1,9},{2,0},{3,11},{4,6},{5,13},{6,4},{7,15},{8,10},{9,1},{1... | collective-permute-start | bytes 884744 | tf_op jit(solution)/shard_map/ppermute | solution.py:1016
  100.4 11.1 %collective-permute-start.27 = (f32[4,144,256]{2,1,0:T(8,128)S(1)}, f32[4,144,256]{2,1,0:T(8,128)S(1)}, u32[]{:S(2)}, u32[]{:S(2)}) collective-permute-start(f32[4,144,256]{2,1,0:T(8,128)S(1)} %pad_maximum_fusion.4), channel_id=1, source_target_pairs={{0,8},{1,3},{2,10},{3,1},{4,12},{5,7},{6,14},{7,5},{8,0},{9,11},{1... | collective-permute-start | bytes 1769480 | tf_op jit(solution)/shard_map/ppermute | solution.py:1016
  101.6 7.2 %collective-permute-start.26 = (f32[336,256]{1,0:T(8,128)S(1)}, f32[336,256]{1,0:T(8,128)S(1)}, u32[]{:S(2)}, u32[]{:S(2)}) collective-permute-start(f32[336,256]{1,0:T(8,128)S(1)} %pad_maximum_fusion.8), channel_id=1, source_target_pairs={{0,16},{1,9},{2,18},{3,11},{4,20},{5,13},{6,22},{7,15},{8,24},{9,1... | collective-permute-start | bytes 1032200 | tf_op jit(solution)/shard_map/ppermute | solution.py:1016
  104.6 10.5 %collective-permute-start.31 = (f32[4,144,256]{2,1,0:T(8,128)S(1)}, f32[4,144,256]{2,1,0:T(8,128)S(1)}, u32[]{:S(2)}, u32[]{:S(2)}) collective-permute-start(f32[4,144,256]{2,1,0:T(8,128)S(1)} %pad_maximum_fusion.5), channel_id=1, source_target_pairs={{0,16},{1,3},{2,18},{3,1},{4,20},{5,7},{6,22},{7,5},{8,24},{9,11},... | collective-permute-start | bytes 1769480 | tf_op jit(solution)/shard_map/ppermute | solution.py:1016
  111.6 7.3 %collective-permute-start.29 = (f32[8,144,256]{2,1,0:T(8,128)S(1)}, f32[8,144,256]{2,1,0:T(8,128)S(1)}, u32[]{:S(2)}, u32[]{:S(2)}) collective-permute-start(f32[8,144,256]{2,1,0:T(8,128)S(1)} %pad_maximum_fusion.1), channel_id=1, source_target_pairs={{0,1},{1,0},{2,3},{3,2},{4,5},{5,4},{6,7},{7,6},{8,9},{9,8},{10,11... | collective-permute-start | bytes 3538952 | tf_op jit(solution)/shard_map/ppermute | solution.py:1016
  115.2 3.7 %collective-permute-start.32 = (f32[8,144,256]{2,1,0:T(8,128)S(1)}, f32[8,144,256]{2,1,0:T(8,128)S(1)}, u32[]{:S(2)}, u32[]{:S(2)}) collective-permute-start(f32[8,144,256]{2,1,0:T(8,128)S(1)} %pad_maximum_fusion.3), channel_id=1, source_target_pairs={{0,1},{1,0},{2,3},{3,2},{4,5},{5,4},{6,7},{7,6},{8,9},{9,8},{10,11... | collective-permute-start | bytes 3538952 | tf_op jit(solution)/shard_map/ppermute | solution.py:1016
  115.3 3.5 %collective-permute-start.30 = (f32[8,64,256]{2,1,0:T(8,128)S(1)}, f32[8,64,256]{2,1,0:T(8,128)S(1)}, u32[]{:S(2)}, u32[]{:S(2)}) collective-permute-start(f32[8,64,256]{2,1,0:T(8,128)S(1)} %pad_maximum_fusion.7), channel_id=1, source_target_pairs={{0,1},{1,0},{2,3},{3,2},{4,5},{5,4},{6,7},{7,6},{8,9},{9,8},{10,11... | collective-permute-start | bytes 1572872 | tf_op jit(solution)/shard_map/ppermute | solution.py:1016
  (21 other events, 95.9 us)

commit v2 on v1

--- a/solution.py
+++ b/solution.py
@@ -1110,14 +1110,14 @@
                 chunk_c.extra = extra[:SUMS], extra[None, SUMS:]
             tie = chunk_a.step(tie)
             tie = chunk_c.step(tie)
-            tie = chunk_b.step(tie, late=home if k == 4 else None)
+            tie = chunk_b.step(tie, late=home if k == 5 else None)
             if n_bucket == 4:
-                if k == 1:
+                if k == 2:
                     hop = send(after(back[0], tie), by_core(x, y))
-                if k == 2:
+                if k == 3:
                     turn = after(jnp.where(notes[1:2] != 0.0, hop, back[1]), tie)
                     got = send(turn, by_core(y, x))
-                if k == 3:
+                if k == 4:
                     home = jnp.where(notes[2:3] != 0.0, hop, got)
                     grad = lax.dynamic_update_slice(grad, home[None], (WORK, 0, 0))
             elif k == 1:

time: 123 us -> 117 us (0.951)
  waiting for transfers between devices: 46.1 us -> 39.3 us
  starting transfers between devices: 33.1 us -> 34.4 us
    ppermute x33, waiting for transfers between devices: 46.1 us -> 39.3 us  [send(): return lax.ppermute(v, AXES, perm)]
    ppermute x33, starting transfers between devices: 33.1 us -> 34.4 us  [send(): return lax.ppermute(v, AXES, perm)]
  transfers between devices with their start and end apart: 33 -> 33, of which waited for: 18 -> 18; matrix products, arithmetic and copies ran while one was open for 3% -> 3% of each run, Pallas kernels for 18% -> 19%
where the time goes in v2:
time: 117 us
  waiting for transfers between devices  39.3 us (34%)
  Pallas kernels  35.1 us (30%)
  starting transfers between devices  34.4 us (29%)
  local copies, waits for them, and re-layouts  2.84 us (2%)
  between operations  2.82 us (2%)
  other arithmetic  2.44 us (2%)
    ppermute x33, waiting for transfers between devices, send(): return lax.ppermute(v, AXES, perm)  39.3 us
    ppermute x33, starting transfers between devices, send(): return lax.ppermute(v, AXES, perm)  34.4 us
    pallas_call x1, Pallas kernels, call_one(): pl.pallas_call(kernel_one, name='front_of_own_images', in_specs=[SMEM, HB...  10.4 us
    pallas_call x1, Pallas kernels, call_two(): pl.pallas_call(lambda *refs: kernel_two(n_bucket, *refs), name='front_of_...  8.99 us
    pallas_call x1, Pallas kernels, call_three(): pl.pallas_call(kernel_three, name='back_to_first_out', in_specs=[VMEM, AN...  5.8 us
    pallas_call x1, Pallas kernels, call_four(): pl.pallas_call(lambda *refs: kernel_four(n_bucket, *refs), name='back_to_...  4.08 us
    pallas_call x1, Pallas kernels, assemble(): pl.pallas_call(assemble_kernel, name='assemble', in_specs=[ANY] * 6, out_...  3.32 us
  transfers between devices with their start and end apart: 33, of which 18 were waited for; matrix products, arithmetic and copies ran while one was open for 3% of the time, Pallas kernels for 19%

profile of v2, /device:TPU:0, one launch (start us, length us, event | category | flops | bytes accessed | tf_op | source)
XLA Modules:
  0.0 117.0 jit_solution(7130180006993031738)
XLA Ops:
  2.0 1.3 %copy-done.2 = f32[1,1,5,256,256]{4,3,2,1,0:T(8,128)S(1)} copy-done((f32[1,1,5,256,256]{4,3,2,1,0:T(8,128)S(1)}, f32[1,1,5,256,256]{4,3,2,1,0:T(8,128)}, u32[]{:S(2)}) %copy-start.2) | copy-done | bytes 1310744
  4.7 4.0 %collective-permute-start.2 = (f32[264,256]{1,0:T(8,128)S(1)}, f32[264,256]{1,0:T(8,128)S(1)}, u32[]{:S(2)}, u32[]{:S(2)}) collective-permute-start(f32[264,256]{1,0:T(8,128)S(1)} %pack_spare.1), channel_id=1, source_target_pairs={{0,24},{1,25},{2,26},{3,27},{4,28},{5,29},{6,30},{7,31},{8,16},{9,... | collective-permute-start | bytes 811016 | tf_op jit(solution)/shard_map/ppermute | solution.py:1016
  9.4 10.4 %front_of_own_images.1 = (f32[4,256,256]{2,1,0:T(8,128)}, f32[4,256,256]{2,1,0:T(8,128)S(1)}, f32[4,256,256]{2,1,0:T(8,128)S(1)}, bf16[4,256,256]{2,1,0:T(8,128)...) custom-call(s32[1,1,5]{2,1,0:T(1,128)S(1)} %copy-done.19, ...), custom_call_target="tpu_custom_call" | custom-call | flops 20000000000 | bytes 1000000 | tf_op jit(solution)/shard_map/front_of_own_images/pallas_call | solution.py:796
  19.8 1.1 collective-permute-done.1.refs_6_
  21.2 9.0 %front_of_last_image.1 = (f32[4,256,256]{2,1,0:T(8,128)}, f32[4,256,256]{2,1,0:T(8,128)S(1)}, f32[4,256,256]{2,1,0:T(8,128)S(1)}, bf16[4,256,256]{2,1,0:T(8,128)...) custom-call(s32[1,1,5]{2,1,0:T(1,128)S(1)} %copy-done.19, ...), custom_call_target="tpu_custom_call", output_to_operand_aliasing={{0}: (29, {}), {1}: (27, {}), {2}: (30, {}), {3}: (31, {}),... | custom-call | flops 20000000000 | bytes 1000000 | tf_op jit(solution)/shard_map/front_of_last_image/pallas_call | solution.py:815
  30.8 5.8 %back_to_first_out.1 = (f32[8,9,16,256]{3,2,1,0:T(8,128)S(1)}, f32[8,9,16,256]{3,2,1,0:T(8,128)S(1)}, bf16[4,256,256]{2,1,0:T(8,128)(2,1)S(1)}, f32[16,256]{1,0:T(8,128)S(1)}, f32[8,256]{1,0:T(8,128)S(1)}) custom-call(f32[8,256]{1,0:T(8,128)S(1)} %get-tuple-element.89.notes, f32[4,256,256]{2,1,0:T(8,128)S(1)} %get-tuple-element.88.dmid_in.refs_4_, ...), custom_call_target="tpu_custom_call" | custom-call | tf_op jit(solution)/shard_map/back_to_first_out/pallas_call | solution.py:852
  37.1 1.6 %collective-permute-start.8 = (f32[2,2,144,256]{3,2,1,0:T(8,128)S(1)}, f32[2,2,144,256]{3,2,1,0:T(8,128)S(1)}, u32[]{:S(2)}, u32[]{:S(2)}) collective-permute-start(f32[2,2,144,256]{3,2,1,0:T(8,128)S(1)} %bitcast.207), channel_id=1, source_target_pairs={{0,8},{1,3},{2,10},{3,1},{4,12},{5,7},{6,14},{7,5},{8,0},{9,11},{1... | collective-permute-start | bytes 1769480 | tf_op jit(solution)/shard_map/ppermute | solution.py:1016
  39.8 1.5 %collective-permute-start.6 = (f32[2,2,144,256]{3,2,1,0:T(8,128)S(1)}, f32[2,2,144,256]{3,2,1,0:T(8,128)S(1)}, u32[]{:S(2)}, u32[]{:S(2)}) collective-permute-start(f32[2,2,144,256]{3,2,1,0:T(8,128)S(1)} %bitcast.208), channel_id=1, source_target_pairs={{0,16},{1,3},{2,18},{3,1},{4,20},{5,7},{6,22},{7,5},{8,24},{9,11},... | collective-permute-start | bytes 1769480 | tf_op jit(solution)/shard_map/ppermute | solution.py:1016
  41.3 4.1 %back_to_images.1 = (f32[5,256,256]{2,1,0:T(8,128)}, f32[2,256,256]{2,1,0:T(8,128)S(1)}, f32[24,256]{1,0:T(8,128)S(1)}) custom-call(s32[1,1]{1,0:T(1,128)S(6)} %copy.56.counts.refs_1_.refs_0_, s32[1,1]{1,0:T(1,128)S(6)} %copy.57.source.refs_2_.refs_1_, f32[5,256,256]{2,1,0:T(8,128)S(1)} %bitcast.145, f32[256,256]{1,0:T(8,128)S(1)} %get-tuple-element.87.refs_3_, ...), custom_call_target="tpu_custom_call" | custom-call | tf_op jit(solution)/shard_map/back_to_images/pallas_call | solution.py:871
  46.7 3.2 %collective-permute-done.8 = f32[2,2,144,256]{3,2,1,0:T(8,128)S(1)} collective-permute-done((f32[2,2,144,256]{3,2,1,0:T(8,128)S(1)}, f32[2,2,144,256]{3,2,1,0:T(8,128)S(1)}, u32[]{:S(2)}, u32[]{:S(2)}) %collective-permute-start.8) | collective-permute-done | bytes 589856 | tf_op jit(solution)/shard_map/ppermute | solution.py:1016
  50.0 1.5 %collective-permute-start.11 = (f32[2,144,256]{2,1,0:T(8,128)S(1)}, f32[2,144,256]{2,1,0:T(8,128)S(1)}, u32[]{:S(2)}, u32[]{:S(2)}) collective-permute-start(f32[2,144,256]{2,1,0:T(8,128)S(1)} %get-tuple-element.108), channel_id=1, source_target_pairs={{0,16},{1,9},{2,18},{3,11},{4,20},{5,13},{6,22},{7,15},{8,24},{9,1... | collective-permute-start | bytes 884744 | tf_op jit(solution)/shard_map/ppermute | solution.py:1016
  52.3 1.5 %collective-permute-start.9 = (f32[2,144,256]{2,1,0:T(8,128)S(1)}, f32[2,144,256]{2,1,0:T(8,128)S(1)}, u32[]{:S(2)}, u32[]{:S(2)}) collective-permute-start(f32[2,144,256]{2,1,0:T(8,128)S(1)} %get-tuple-element.110), channel_id=1, source_target_pairs={{0,2},{1,9},{2,0},{3,11},{4,6},{5,13},{6,4},{7,15},{8,10},{9,1},{1... | collective-permute-start | bytes 884744 | tf_op jit(solution)/shard_map/ppermute | solution.py:1016
  53.8 3.8 %collective-permute-done.10 = f32[2,64,256]{2,1,0:T(8,128)S(1)} collective-permute-done((f32[2,64,256]{2,1,0:T(8,128)S(1)}, f32[2,64,256]{2,1,0:T(8,128)S(1)}, u32[]{:S(2)}, u32[]{:S(2)}) %collective-permute-start.10) | collective-permute-done | bytes 131104 | tf_op jit(solution)/shard_map/ppermute | solution.py:1016
  58.5 1.2 %collective-permute-start.14 = (f32[64,256]{1,0:T(8,128)S(1)}, f32[64,256]{1,0:T(8,128)S(1)}, u32[]{:S(2)}, u32[]{:S(2)}) collective-permute-start(f32[64,256]{1,0:T(8,128)S(1)} %fusion.12), channel_id=1, source_target_pairs={{0,2},{1,3},{2,0},{3,1},{4,6},{5,7},{6,4},{7,5},{8,10},{9,11},{10,... | collective-permute-start | bytes 196616 | tf_op jit(solution)/shard_map/ppermute | solution.py:1016
  59.8 1.6 %collective-permute-start.13 = (f32[144,256]{1,0:T(8,128)S(1)}, f32[144,256]{1,0:T(8,128)S(1)}, u32[]{:S(2)}, u32[]{:S(2)}) collective-permute-start(f32[144,256]{1,0:T(8,128)S(1)} %fusion.7), channel_id=1, source_target_pairs={{0,8},{1,17},{2,10},{3,19},{4,12},{5,21},{6,14},{7,23},{8,0},{9,25... | collective-permute-start | bytes 442376 | tf_op jit(solution)/shard_map/ppermute | solution.py:1016
  61.9 1.6 %collective-permute-done.14 = f32[64,256]{1,0:T(8,128)S(1)} collective-permute-done((f32[64,256]{1,0:T(8,128)S(1)}, f32[64,256]{1,0:T(8,128)S(1)}, u32[]{:S(2)}, u32[]{:S(2)}) %collective-permute-start.14) | collective-permute-done | bytes 65568 | tf_op jit(solution)/shard_map/ppermute | solution.py:1016
  63.6 2.7 %collective-permute-start.19 = (f32[144,256]{1,0:T(8,128)S(1)}, f32[144,256]{1,0:T(8,128)S(1)}, u32[]{:S(2)}, u32[]{:S(2)}) collective-permute-start(f32[144,256]{1,0:T(8,128)S(1)} %fusion.3), channel_id=1, source_target_pairs={{0,4},{1,5},{2,6},{3,7},{4,0},{5,1},{6,2},{7,3},{8,12},{9,13},{10,... | collective-permute-start | bytes 442376 | tf_op jit(solution)/shard_map/ppermute | solution.py:1016
  66.6 2.7 %collective-permute-start.22 = (f32[144,256]{1,0:T(8,128)S(1)}, f32[144,256]{1,0:T(8,128)S(1)}, u32[]{:S(2)}, u32[]{:S(2)}) collective-permute-start(f32[144,256]{1,0:T(8,128)S(1)} %fusion.5), channel_id=1, source_target_pairs={{0,4},{1,5},{2,6},{3,7},{4,0},{5,1},{6,2},{7,3},{8,12},{9,13},{10,... | collective-permute-start | bytes 442376 | tf_op jit(solution)/shard_map/ppermute | solution.py:1016
  69.3 10.6 %collective-permute-done.18 = f32[88,256]{1,0:T(8,128)S(1)} collective-permute-done((f32[88,256]{1,0:T(8,128)S(1)}, f32[88,256]{1,0:T(8,128)S(1)}, u32[]{:S(2)}, u32[]{:S(2)}) %collective-permute-start.18) | collective-permute-done | bytes 90144 | tf_op jit(solution)/shard_map/ppermute | solution.py:1016
  80.8 2.0 %collective-permute-start.21 = (f32[1,144,256]{2,1,0:T(8,128)S(1)}, f32[1,144,256]{2,1,0:T(8,128)S(1)}, u32[]{:S(2)}, u32[]{:S(2)}) collective-permute-start(f32[1,144,256]{2,1,0:T(8,128)S(1)} %bitcast.177), channel_id=1, source_target_pairs={{0,2},{1,17},{2,0},{3,19},{4,6},{5,21},{6,4},{7,23},{8,10},{9,25},... | collective-permute-start | bytes 442376 | tf_op jit(solution)/shard_map/ppermute | solution.py:1016
  82.8 1.6 %collective-permute-start.25 = (f32[1,144,256]{2,1,0:T(8,128)S(1)}, f32[1,144,256]{2,1,0:T(8,128)S(1)}, u32[]{:S(2)}, u32[]{:S(2)}) collective-permute-start(f32[1,144,256]{2,1,0:T(8,128)S(1)} %bitcast.182), channel_id=1, source_target_pairs={{0,8},{1,17},{2,10},{3,19},{4,12},{5,21},{6,14},{7,23},{8,0},{9,25... | collective-permute-start | bytes 442376 | tf_op jit(solution)/shard_map/ppermute | solution.py:1016
  84.7 1.5 %collective-permute-done.21 = f32[1,144,256]{2,1,0:T(8,128)S(1)} collective-permute-done((f32[1,144,256]{2,1,0:T(8,128)S(1)}, f32[1,144,256]{2,1,0:T(8,128)S(1)}, u32[]{:S(2)}, u32[]{:S(2)}) %collective-permute-start.21) | collective-permute-done | bytes 147488 | tf_op jit(solution)/shard_map/ppermute | solution.py:1016
  86.2 1.2 collective-permute-start.24
  89.6 1.4 %collective-permute-start.28 = (f32[2,144,256]{2,1,0:T(8,128)S(1)}, f32[2,144,256]{2,1,0:T(8,128)S(1)}, u32[]{:S(2)}, u32[]{:S(2)}) collective-permute-start(f32[2,144,256]{2,1,0:T(8,128)S(1)} %maximum_add_fusion), channel_id=1, source_target_pairs={{0,2},{1,9},{2,0},{3,11},{4,6},{5,13},{6,4},{7,15},{8,10},{9,1},{1... | collective-permute-start | bytes 884744 | tf_op jit(solution)/shard_map/ppermute | solution.py:1016
  91.0 3.9 %collective-permute-done.23 = f32[176,256]{1,0:T(8,128)S(1)} collective-permute-done((f32[176,256]{1,0:T(8,128)S(1)}, f32[176,256]{1,0:T(8,128)S(1)}, u32[]{:S(2)}, u32[]{:S(2)}) %collective-permute-start.23) | collective-permute-done | bytes 180256 | tf_op jit(solution)/shard_map/ppermute | solution.py:1016
  96.1 1.1 collective-permute-start.26
  97.2 2.3 %collective-permute-done.28 = f32[2,144,256]{2,1,0:T(8,128)S(1)} collective-permute-done((f32[2,144,256]{2,1,0:T(8,128)S(1)}, f32[2,144,256]{2,1,0:T(8,128)S(1)}, u32[]{:S(2)}, u32[]{:S(2)}) %collective-permute-start.28) | collective-permute-done | bytes 294944 | tf_op jit(solution)/shard_map/ppermute | solution.py:1016
  100.4 2.9 %collective-permute-done.26 = f32[336,256]{1,0:T(8,128)S(1)} collective-permute-done((f32[336,256]{1,0:T(8,128)S(1)}, f32[336,256]{1,0:T(8,128)S(1)}, u32[]{:S(2)}, u32[]{:S(2)}) %collective-permute-start.26) | collective-permute-done | bytes 344096 | tf_op jit(solution)/shard_map/ppermute | solution.py:1016
  103.4 1.9 %collective-permute-done.27 = f32[4,144,256]{2,1,0:T(8,128)S(1)} collective-permute-done((f32[4,144,256]{2,1,0:T(8,128)S(1)}, f32[4,144,256]{2,1,0:T(8,128)S(1)}, u32[]{:S(2)}, u32[]{:S(2)}) %collective-permute-start.27) | collective-permute-done | bytes 589856 | tf_op jit(solution)/shard_map/ppermute | solution.py:1016
  105.5 4.2 %collective-permute-done.31 = f32[4,144,256]{2,1,0:T(8,128)S(1)} collective-permute-done((f32[4,144,256]{2,1,0:T(8,128)S(1)}, f32[4,144,256]{2,1,0:T(8,128)S(1)}, u32[]{:S(2)}, u32[]{:S(2)}) %collective-permute-start.31) | collective-permute-done | bytes 589856 | tf_op jit(solution)/shard_map/ppermute | solution.py:1016
  110.5 2.0 %embed_gradient.1 = f32[512,256]{1,0:T(8,128)} custom-call(f32[16,8,256]{2,1,0:T(8,128)S(1)} %fusion.9.refs_0_, f32[16,256]{1,0:T(8,128)S(1)} %slice_add_fusion.19.refs_1_), custom_call_target="tpu_custom_call" | custom-call | flops 1 | bytes 1 | tf_op jit(solution)/shard_map/embed_gradient/pallas_call | solution.py:966
  113.5 3.3 %assemble.1 = (f32[9,256,256]{2,1,0:T(8,128)}, f32[9,256,256]{2,1,0:T(8,128)}, f32[256,768]{1,0:T(8,128)}, f32[256,256]{1,0:T(8,128)}) custom-call(f32[8,9,16,256]{3,2,1,0:T(8,128)S(1)} %pad_maximum_fusion.refs_0_, f32[8,9,16,256]{3,2,1,0:T(8,128)S(1)} %bitcast.146, f32[8,4,16,256]{3,2,1,0:T(8,128)S(1)} %pad_maximum_fusion.6.refs_2_, ...), custom_call_target="tpu_custom_call" | custom-call | flops 1 | bytes 1 | tf_op jit(solution)/shard_map/assemble/pallas_call | solution.py:908
  (140 shorter events, 16.0 us)
Async XLA Ops:
  4.7 15.1 %collective-permute-start.2 = (f32[264,256]{1,0:T(8,128)S(1)}, f32[264,256]{1,0:T(8,128)S(1)}, u32[]{:S(2)}, u32[]{:S(2)}) collective-permute-start(f32[264,256]{1,0:T(8,128)S(1)} %pack_spare.1), channel_id=1, source_target_pairs={{0,24},{1,25},{2,26},{3,27},{4,28},{5,29},{6,30},{7,31},{8,16},{9,... | collective-permute-start | bytes 811016 | tf_op jit(solution)/shard_map/ppermute | solution.py:1016
  8.6 12.3 %collective-permute-start.1 = (f32[264,256]{1,0:T(8,128)S(1)}, f32[264,256]{1,0:T(8,128)S(1)}, u32[]{:S(2)}, u32[]{:S(2)}) collective-permute-start(f32[264,256]{1,0:T(8,128)S(1)} %pack_spare.1), channel_id=1, source_target_pairs={{0,16},{1,17},{2,18},{3,19},{4,20},{5,21},{6,22},{7,23},{8,24},{9,... | collective-permute-start | bytes 811016 | tf_op jit(solution)/shard_map/ppermute | solution.py:1016
  9.1 12.1 %collective-permute-start = (f32[264,256]{1,0:T(8,128)S(1)}, f32[264,256]{1,0:T(8,128)S(1)}, u32[]{:S(2)}, u32[]{:S(2)}) collective-permute-start(f32[264,256]{1,0:T(8,128)S(1)} %pack_spare.1), channel_id=1, source_target_pairs={{0,8},{1,9},{2,10},{3,11},{4,12},{5,13},{6,14},{7,15},{8,0},{9,1},... | collective-permute-start | bytes 811016 | tf_op jit(solution)/shard_map/ppermute | solution.py:1016
  30.2 6.7 %collective-permute-start.5 = (f32[8,9,16,256]{3,2,1,0:T(8,128)S(1)}, f32[8,9,16,256]{3,2,1,0:T(8,128)S(1)}, u32[]{:S(2)}, u32[]{:S(2)}) collective-permute-start(f32[8,9,16,256]{3,2,1,0:T(8,128)S(1)} %get-tuple-element.100), channel_id=1, source_target_pairs={{0,1},{1,0},{2,3},{3,2},{4,5},{5,4},{6,7},{7,6},{8,9},{9,8},{10,11... | collective-permute-start | bytes 3538952 | tf_op jit(solution)/shard_map/ppermute | solution.py:1016
  30.3 6.5 %collective-permute-start.4 = (f32[8,4,16,256]{3,2,1,0:T(8,128)S(1)}, f32[8,4,16,256]{3,2,1,0:T(8,128)S(1)}, u32[]{:S(2)}, u32[]{:S(2)}) collective-permute-start(f32[8,4,16,256]{3,2,1,0:T(8,128)S(1)} %get-tuple-element.98), channel_id=1, source_target_pairs={{0,1},{1,0},{2,3},{3,2},{4,5},{5,4},{6,7},{7,6},{8,9},{9,8},{10,11... | collective-permute-start | bytes 1572872 | tf_op jit(solution)/shard_map/ppermute | solution.py:1016
  36.6 2.9 %collective-permute-start.3 = (f32[8,9,16,256]{3,2,1,0:T(8,128)S(1)}, f32[8,9,16,256]{3,2,1,0:T(8,128)S(1)}, u32[]{:S(2)}, u32[]{:S(2)}) collective-permute-start(f32[8,9,16,256]{3,2,1,0:T(8,128)S(1)} %get-tuple-element.96), channel_id=1, source_target_pairs={{0,1},{1,0},{2,3},{3,2},{4,5},{5,4},{6,7},{7,6},{8,9},{9,8},{10,11... | collective-permute-start | bytes 3538952 | tf_op jit(solution)/shard_map/ppermute | solution.py:1016
  37.1 12.8 %collective-permute-start.8 = (f32[2,2,144,256]{3,2,1,0:T(8,128)S(1)}, f32[2,2,144,256]{3,2,1,0:T(8,128)S(1)}, u32[]{:S(2)}, u32[]{:S(2)}) collective-permute-start(f32[2,2,144,256]{3,2,1,0:T(8,128)S(1)} %bitcast.207), channel_id=1, source_target_pairs={{0,8},{1,3},{2,10},{3,1},{4,12},{5,7},{6,14},{7,5},{8,0},{9,11},{1... | collective-permute-start | bytes 1769480 | tf_op jit(solution)/shard_map/ppermute | solution.py:1016
  38.7 8.0 %collective-permute-start.7 = (f32[2,2,64,256]{3,2,1,0:T(8,128)S(1)}, f32[2,2,64,256]{3,2,1,0:T(8,128)S(1)}, u32[]{:S(2)}, u32[]{:S(2)}) collective-permute-start(f32[2,2,64,256]{3,2,1,0:T(8,128)S(1)} %bitcast.213), channel_id=1, source_target_pairs={{0,16},{1,9},{2,18},{3,11},{4,20},{5,13},{6,22},{7,15},{8,24},{9,1... | collective-permute-start | bytes 786440 | tf_op jit(solution)/shard_map/ppermute | solution.py:1016
  39.8 12.4 %collective-permute-start.6 = (f32[2,2,144,256]{3,2,1,0:T(8,128)S(1)}, f32[2,2,144,256]{3,2,1,0:T(8,128)S(1)}, u32[]{:S(2)}, u32[]{:S(2)}) collective-permute-start(f32[2,2,144,256]{3,2,1,0:T(8,128)S(1)} %bitcast.208), channel_id=1, source_target_pairs={{0,16},{1,3},{2,18},{3,1},{4,20},{5,7},{6,22},{7,5},{8,24},{9,11},... | collective-permute-start | bytes 1769480 | tf_op jit(solution)/shard_map/ppermute | solution.py:1016
  50.0 7.6 %collective-permute-start.11 = (f32[2,144,256]{2,1,0:T(8,128)S(1)}, f32[2,144,256]{2,1,0:T(8,128)S(1)}, u32[]{:S(2)}, u32[]{:S(2)}) collective-permute-start(f32[2,144,256]{2,1,0:T(8,128)S(1)} %get-tuple-element.108), channel_id=1, source_target_pairs={{0,16},{1,9},{2,18},{3,11},{4,20},{5,13},{6,22},{7,15},{8,24},{9,1... | collective-permute-start | bytes 884744 | tf_op jit(solution)/shard_map/ppermute | solution.py:1016
  51.5 6.1 %collective-permute-start.10 = (f32[2,64,256]{2,1,0:T(8,128)S(1)}, f32[2,64,256]{2,1,0:T(8,128)S(1)}, u32[]{:S(2)}, u32[]{:S(2)}) collective-permute-start(f32[2,64,256]{2,1,0:T(8,128)S(1)} %get-tuple-element.109), channel_id=1, source_target_pairs={{0,8},{1,17},{2,10},{3,19},{4,12},{5,21},{6,14},{7,23},{8,0},{9,25... | collective-permute-start | bytes 393224 | tf_op jit(solution)/shard_map/ppermute | solution.py:1016
  52.3 7.5 %collective-permute-start.9 = (f32[2,144,256]{2,1,0:T(8,128)S(1)}, f32[2,144,256]{2,1,0:T(8,128)S(1)}, u32[]{:S(2)}, u32[]{:S(2)}) collective-permute-start(f32[2,144,256]{2,1,0:T(8,128)S(1)} %get-tuple-element.110), channel_id=1, source_target_pairs={{0,2},{1,9},{2,0},{3,11},{4,6},{5,13},{6,4},{7,15},{8,10},{9,1},{1... | collective-permute-start | bytes 884744 | tf_op jit(solution)/shard_map/ppermute | solution.py:1016
  57.6 5.9 %collective-permute-start.16 = (f32[144,256]{1,0:T(8,128)S(1)}, f32[144,256]{1,0:T(8,128)S(1)}, u32[]{:S(2)}, u32[]{:S(2)}) collective-permute-start(f32[144,256]{1,0:T(8,128)S(1)} %fusion.6), channel_id=1, source_target_pairs={{0,2},{1,17},{2,0},{3,19},{4,6},{5,21},{6,4},{7,23},{8,10},{9,25},... | collective-permute-start | bytes 442376 | tf_op jit(solution)/shard_map/ppermute | solution.py:1016
  58.5 5.0 %collective-permute-start.14 = (f32[64,256]{1,0:T(8,128)S(1)}, f32[64,256]{1,0:T(8,128)S(1)}, u32[]{:S(2)}, u32[]{:S(2)}) collective-permute-start(f32[64,256]{1,0:T(8,128)S(1)} %fusion.12), channel_id=1, source_target_pairs={{0,2},{1,3},{2,0},{3,1},{4,6},{5,7},{6,4},{7,5},{8,10},{9,11},{10,... | collective-permute-start | bytes 196616 | tf_op jit(solution)/shard_map/ppermute | solution.py:1016
  59.8 6.8 %collective-permute-start.13 = (f32[144,256]{1,0:T(8,128)S(1)}, f32[144,256]{1,0:T(8,128)S(1)}, u32[]{:S(2)}, u32[]{:S(2)}) collective-permute-start(f32[144,256]{1,0:T(8,128)S(1)} %fusion.7), channel_id=1, source_target_pairs={{0,8},{1,17},{2,10},{3,19},{4,12},{5,21},{6,14},{7,23},{8,0},{9,25... | collective-permute-start | bytes 442376 | tf_op jit(solution)/shard_map/ppermute | solution.py:1016
  61.4 18.6 %collective-permute-start.12 = (f32[256,256]{1,0:T(8,128)S(1)}, f32[256,256]{1,0:T(8,128)S(1)}, u32[]{:S(2)}, u32[]{:S(2)}) collective-permute-start(f32[256,256]{1,0:T(8,128)S(1)} %slice_bitcast_fusion), channel_id=1, source_target_pairs={{0,8},{1,17},{2,10},{3,19},{4,12},{5,21},{6,14},{7,23},{8,0},{9,25... | collective-permute-start | bytes 786440 | tf_op jit(solution)/shard_map/ppermute | solution.py:1016
  63.6 16.3 %collective-permute-start.19 = (f32[144,256]{1,0:T(8,128)S(1)}, f32[144,256]{1,0:T(8,128)S(1)}, u32[]{:S(2)}, u32[]{:S(2)}) collective-permute-start(f32[144,256]{1,0:T(8,128)S(1)} %fusion.3), channel_id=1, source_target_pairs={{0,4},{1,5},{2,6},{3,7},{4,0},{5,1},{6,2},{7,3},{8,12},{9,13},{10,... | collective-permute-start | bytes 442376 | tf_op jit(solution)/shard_map/ppermute | solution.py:1016
  66.3 13.6 %collective-permute-start.18 = (f32[88,256]{1,0:T(8,128)S(1)}, f32[88,256]{1,0:T(8,128)S(1)}, u32[]{:S(2)}, u32[]{:S(2)}) collective-permute-start(f32[88,256]{1,0:T(8,128)S(1)} %pad_maximum_fusion.14), channel_id=1, source_target_pairs={{0,4},{1,5},{2,6},{3,7},{4,0},{5,1},{6,2},{7,3},{8,12},{9,13},{10,... | collective-permute-start | bytes 270344 | tf_op jit(solution)/shard_map/ppermute | solution.py:1016
  66.6 16.1 %collective-permute-start.22 = (f32[144,256]{1,0:T(8,128)S(1)}, f32[144,256]{1,0:T(8,128)S(1)}, u32[]{:S(2)}, u32[]{:S(2)}) collective-permute-start(f32[144,256]{1,0:T(8,128)S(1)} %fusion.5), channel_id=1, source_target_pairs={{0,4},{1,5},{2,6},{3,7},{4,0},{5,1},{6,2},{7,3},{8,12},{9,13},{10,... | collective-permute-start | bytes 442376 | tf_op jit(solution)/shard_map/ppermute | solution.py:1016
  80.0 4.7 %collective-permute-start.20 = (f32[96,256]{1,0:T(8,128)S(1)}, f32[96,256]{1,0:T(8,128)S(1)}, u32[]{:S(2)}, u32[]{:S(2)}) collective-permute-start(f32[96,256]{1,0:T(8,128)S(1)} %pad_maximum_fusion.13), channel_id=1, source_target_pairs={{0,2},{1,3},{2,0},{3,1},{4,6},{5,7},{6,4},{7,5},{8,10},{9,11},{10,... | collective-permute-start | bytes 294920 | tf_op jit(solution)/shard_map/ppermute | solution.py:1016
  80.1 8.3 %collective-permute-start.17 = (f32[256,256]{1,0:T(8,128)S(1)}, f32[256,256]{1,0:T(8,128)S(1)}, u32[]{:S(2)}, u32[]{:S(2)}) collective-permute-start(f32[256,256]{1,0:T(8,128)S(1)} %bitcast_select_fusion), channel_id=1, source_target_pairs={{0,16},{1,9},{2,18},{3,11},{4,20},{5,13},{6,22},{7,15},{8,24},{9,1... | collective-permute-start | bytes 786440 | tf_op jit(solution)/shard_map/ppermute | solution.py:1016
  80.8 5.5 %collective-permute-start.21 = (f32[1,144,256]{2,1,0:T(8,128)S(1)}, f32[1,144,256]{2,1,0:T(8,128)S(1)}, u32[]{:S(2)}, u32[]{:S(2)}) collective-permute-start(f32[1,144,256]{2,1,0:T(8,128)S(1)} %bitcast.177), channel_id=1, source_target_pairs={{0,2},{1,17},{2,0},{3,19},{4,6},{5,21},{6,4},{7,23},{8,10},{9,25},... | collective-permute-start | bytes 442376 | tf_op jit(solution)/shard_map/ppermute | solution.py:1016
  82.8 6.8 %collective-permute-start.25 = (f32[1,144,256]{2,1,0:T(8,128)S(1)}, f32[1,144,256]{2,1,0:T(8,128)S(1)}, u32[]{:S(2)}, u32[]{:S(2)}) collective-permute-start(f32[1,144,256]{2,1,0:T(8,128)S(1)} %bitcast.182), channel_id=1, source_target_pairs={{0,8},{1,17},{2,10},{3,19},{4,12},{5,21},{6,14},{7,23},{8,0},{9,25... | collective-permute-start | bytes 442376 | tf_op jit(solution)/shard_map/ppermute | solution.py:1016
  86.2 8.8 %collective-permute-start.24 = (f32[2,144,256]{2,1,0:T(8,128)S(1)}, f32[2,144,256]{2,1,0:T(8,128)S(1)}, u32[]{:S(2)}, u32[]{:S(2)}) collective-permute-start(f32[2,144,256]{2,1,0:T(8,128)S(1)} %pad_maximum_fusion.9), channel_id=1, source_target_pairs={{0,16},{1,9},{2,18},{3,11},{4,20},{5,13},{6,22},{7,15},{8,24},{9,1... | collective-permute-start | bytes 884744 | tf_op jit(solution)/shard_map/ppermute | solution.py:1016
  87.4 7.5 %collective-permute-start.23 = (f32[176,256]{1,0:T(8,128)S(1)}, f32[176,256]{1,0:T(8,128)S(1)}, u32[]{:S(2)}, u32[]{:S(2)}) collective-permute-start(f32[176,256]{1,0:T(8,128)S(1)} %pad_maximum_fusion.11), channel_id=1, source_target_pairs={{0,8},{1,17},{2,10},{3,19},{4,12},{5,21},{6,14},{7,23},{8,0},{9,25... | collective-permute-start | bytes 540680 | tf_op jit(solution)/shard_map/ppermute | solution.py:1016
  89.6 9.9 %collective-permute-start.28 = (f32[2,144,256]{2,1,0:T(8,128)S(1)}, f32[2,144,256]{2,1,0:T(8,128)S(1)}, u32[]{:S(2)}, u32[]{:S(2)}) collective-permute-start(f32[2,144,256]{2,1,0:T(8,128)S(1)} %maximum_add_fusion), channel_id=1, source_target_pairs={{0,2},{1,9},{2,0},{3,11},{4,6},{5,13},{6,4},{7,15},{8,10},{9,1},{1... | collective-permute-start | bytes 884744 | tf_op jit(solution)/shard_map/ppermute | solution.py:1016
  95.1 10.3 %collective-permute-start.27 = (f32[4,144,256]{2,1,0:T(8,128)S(1)}, f32[4,144,256]{2,1,0:T(8,128)S(1)}, u32[]{:S(2)}, u32[]{:S(2)}) collective-permute-start(f32[4,144,256]{2,1,0:T(8,128)S(1)} %pad_maximum_fusion.4), channel_id=1, source_target_pairs={{0,8},{1,3},{2,10},{3,1},{4,12},{5,7},{6,14},{7,5},{8,0},{9,11},{1... | collective-permute-start | bytes 1769480 | tf_op jit(solution)/shard_map/ppermute | solution.py:1016
  96.1 7.2 %collective-permute-start.26 = (f32[336,256]{1,0:T(8,128)S(1)}, f32[336,256]{1,0:T(8,128)S(1)}, u32[]{:S(2)}, u32[]{:S(2)}) collective-permute-start(f32[336,256]{1,0:T(8,128)S(1)} %pad_maximum_fusion.8), channel_id=1, source_target_pairs={{0,16},{1,9},{2,18},{3,11},{4,20},{5,13},{6,22},{7,15},{8,24},{9,1... | collective-permute-start | bytes 1032200 | tf_op jit(solution)/shard_map/ppermute | solution.py:1016
  99.6 10.1 %collective-permute-start.31 = (f32[4,144,256]{2,1,0:T(8,128)S(1)}, f32[4,144,256]{2,1,0:T(8,128)S(1)}, u32[]{:S(2)}, u32[]{:S(2)}) collective-permute-start(f32[4,144,256]{2,1,0:T(8,128)S(1)} %pad_maximum_fusion.5), channel_id=1, source_target_pairs={{0,16},{1,3},{2,18},{3,1},{4,20},{5,7},{6,22},{7,5},{8,24},{9,11},... | collective-permute-start | bytes 1769480 | tf_op jit(solution)/shard_map/ppermute | solution.py:1016
  105.5 8.0 %collective-permute-start.29 = (f32[8,144,256]{2,1,0:T(8,128)S(1)}, f32[8,144,256]{2,1,0:T(8,128)S(1)}, u32[]{:S(2)}, u32[]{:S(2)}) collective-permute-start(f32[8,144,256]{2,1,0:T(8,128)S(1)} %pad_maximum_fusion.1), channel_id=1, source_target_pairs={{0,1},{1,0},{2,3},{3,2},{4,5},{5,4},{6,7},{7,6},{8,9},{9,8},{10,11... | collective-permute-start | bytes 3538952 | tf_op jit(solution)/shard_map/ppermute | solution.py:1016
  109.8 3.7 %collective-permute-start.32 = (f32[8,144,256]{2,1,0:T(8,128)S(1)}, f32[8,144,256]{2,1,0:T(8,128)S(1)}, u32[]{:S(2)}, u32[]{:S(2)}) collective-permute-start(f32[8,144,256]{2,1,0:T(8,128)S(1)} %pad_maximum_fusion.3), channel_id=1, source_target_pairs={{0,1},{1,0},{2,3},{3,2},{4,5},{5,4},{6,7},{7,6},{8,9},{9,8},{10,11... | collective-permute-start | bytes 3538952 | tf_op jit(solution)/shard_map/ppermute | solution.py:1016
  109.9 3.5 %collective-permute-start.30 = (f32[8,64,256]{2,1,0:T(8,128)S(1)}, f32[8,64,256]{2,1,0:T(8,128)S(1)}, u32[]{:S(2)}, u32[]{:S(2)}) collective-permute-start(f32[8,64,256]{2,1,0:T(8,128)S(1)} %pad_maximum_fusion.7), channel_id=1, source_target_pairs={{0,1},{1,0},{2,3},{3,2},{4,5},{5,4},{6,7},{7,6},{8,9},{9,8},{10,11... | collective-permute-start | bytes 1572872 | tf_op jit(solution)/shard_map/ppermute | solution.py:1016
  (21 other events, 95.9 us)

commit v3 on v2

--- a/solution.py
+++ b/solution.py
@@ -435,7 +435,7 @@
     copies.finish()
 
 
-ORDERS = (("xyz", "zxy"), ("yzx", "zxy"), ("yxz", "xyz"))
+ORDERS = (("xyz", "zxy"), ("yzx", "zxy"), ("yxz", "yzx"))
 CHUNK_A, CHUNK_B, CHUNK_C = ORDERS[0], ORDERS[1], ORDERS[2]
 
 
@@ -883,11 +883,14 @@
     )(counts, source, images, last, dmid, low, stats, sums, rows, w[W_FIRST_CONV], w[W_FIRST_GAIN], w[W_FIRST_SHIFT])
 
 
-def assemble_kernel(*refs):
-    first, second, triple, out = refs[6:10]
+def assemble_kernel(orders, *refs):
+    outs = list(refs[2 * len(orders) : -1])
     copies = Copies(refs[-1])
-    for n, order in enumerate((CHUNK_A, CHUNK_C, CHUNK_B)):
+    for n, order in enumerate(orders):
         core, even, odd = owner_codes(order)
+        target = outs.pop(0)
+        units = refs[2 * n].shape[1]
+        beside = outs.pop(0) if units == 4 else None
         for half in range(2):
             src = refs[2 * n + half]
             holder = core if half == 0 else 1 - core
@@ -895,23 +898,26 @@
             for low in range(8):
                 block = holder * 8 + (low ^ code)
                 rows = pl.ds(pl.multiple_of(block * 16, 16), 16)
-                if n != 1:
-                    copies.start((n, half, low), src.at[low], (second if n == 0 else first).at[:, rows, :])
+                if units == 9:
+                    copies.start((n, half, low), src.at[low], target.at[:, rows, :])
                     continue
                 for p in range(3):
-                    copies.start((n, half, low, p), src.at[low, p], triple.at[rows, p * C : (p + 1) * C])
-                copies.start((n, half, low), src.at[low, 3], out.at[rows, :])
+                    copies.start((n, half, low, p), src.at[low, p], target.at[rows, p * C : (p + 1) * C])
+                copies.start((n, half, low), src.at[low, 3], beside.at[rows, :])
     copies.finish()
 
 
-def assemble(*halves):
+def assemble(orders, *halves):
+    out_shape = []
+    for own in halves[::2]:
+        out_shape += [shape((9, C, C))] if own.shape[1] == 9 else [shape((C, 3 * C)), shape((C, C))]
     return pl.pallas_call(
-        assemble_kernel,
+        lambda *refs: assemble_kernel(orders, *refs),
         name="assemble",
-        in_specs=[ANY] * 6,
-        out_specs=[ANY] * 4,
-        out_shape=[shape((9, C, C)), shape((9, C, C)), shape((C, 3 * C)), shape((C, C))],
-        scratch_shapes=[pltpu.SemaphoreType.DMA((16 + 16 + 16 * 4,))],
+        in_specs=[ANY] * len(halves),
+        out_specs=[ANY] * len(out_shape),
+        out_shape=out_shape,
+        scratch_shapes=[pltpu.SemaphoreType.DMA((16 + 16 * 4,))],
         cost_estimate=pl.CostEstimate(flops=1, bytes_accessed=1, transcendentals=0),
         compiler_params=params(2),
     )(*halves)
@@ -1125,12 +1131,13 @@
                 for n in range(2, n_bucket):
                     home = home + send(back[n - 1], bucket_perms[n - 1])
                 grad = lax.dynamic_update_slice(grad, home[None], (WORK, 0, 0))
+        tie = chunk_c.step(tie)
         tie = chunk_a.step(tie)
-        tie = chunk_c.step(tie)
-        tie = chunk_b.step(tie)
         sums, rows = chunk_c.extra
         g_embed = embed_gradient(devices, CHUNK_C, rows, sums)
-        g_first, g_second, g_triple, g_out = assemble(*chunk_a.halves(), *chunk_c.halves(), *chunk_b.halves())
+        tie = chunk_b.step(tie, late=g_embed)
+        (g_second,) = assemble((CHUNK_A,), *chunk_a.halves())
+        g_triple, g_out, g_first = assemble((CHUNK_C, CHUNK_B), *chunk_c.halves(), *chunk_b.halves())
 
         def vec(r):
             return sums[r]

time: 117 us -> 116 us (level)
  starting transfers between devices: 34.4 us -> 32.7 us
  waiting for transfers between devices: 39.3 us -> 37.9 us
  Pallas kernels: 35.1 us -> 36.3 us
    ppermute x33, starting transfers between devices: 34.4 us -> 32.7 us  [send(): return lax.ppermute(v, AXES, perm)]
    ppermute x33, waiting for transfers between devices: 39.3 us -> 37.9 us  [send(): return lax.ppermute(v, AXES, perm)]
    pallas_call x1 -> x2, Pallas kernels: 3.32 us -> 4.57 us  [assemble(): pl.pallas_call(lambda *refs: assemble_kernel(orders, *refs), name='assemb...]
  transfers between devices with their start and end apart: 33 -> 33, of which waited for: 18 -> 20; matrix products, arithmetic and copies ran while one was open for 3% -> 3% of each run, Pallas kernels for 19% -> 21%
where the time goes in v3:
time: 116 us
  waiting for transfers between devices  37.9 us (33%)
  Pallas kernels  36.3 us (31%)
  starting transfers between devices  32.7 us (28%)
  other arithmetic  3.14 us (3%)
  local copies, waits for them, and re-layouts  2.84 us (2%)
  between operations  2.81 us (2%)
    ppermute x33, waiting for transfers between devices, send(): return lax.ppermute(v, AXES, perm)  37.9 us
    ppermute x33, starting transfers between devices, send(): return lax.ppermute(v, AXES, perm)  32.7 us
    pallas_call x1, Pallas kernels, call_one(): pl.pallas_call(kernel_one, name='front_of_own_images', in_specs=[SMEM, HB...  10.4 us
    pallas_call x1, Pallas kernels, call_two(): pl.pallas_call(lambda *refs: kernel_two(n_bucket, *refs), name='front_of_...  8.99 us
    pallas_call x1, Pallas kernels, call_three(): pl.pallas_call(kernel_three, name='back_to_first_out', in_specs=[VMEM, AN...  5.8 us
    pallas_call x2, Pallas kernels, assemble(): pl.pallas_call(lambda *refs: assemble_kernel(orders, *refs), name='assemb...  4.57 us
    pallas_call x1, Pallas kernels, call_four(): pl.pallas_call(lambda *refs: kernel_four(n_bucket, *refs), name='back_to_...  4.07 us
  transfers between devices with their start and end apart: 33, of which 20 were waited for; matrix products, arithmetic and copies ran while one was open for 3% of the time, Pallas kernels for 21%

profile of v3, /device:TPU:0, one launch (start us, length us, event | category | flops | bytes accessed | tf_op | source)
XLA Modules:
  0.0 115.7 jit_solution(9066911350591964497)
XLA Ops:
  2.0 1.3 %copy-done.2 = f32[1,1,5,256,256]{4,3,2,1,0:T(8,128)S(1)} copy-done((f32[1,1,5,256,256]{4,3,2,1,0:T(8,128)S(1)}, f32[1,1,5,256,256]{4,3,2,1,0:T(8,128)}, u32[]{:S(2)}) %copy-start.2) | copy-done | bytes 1310744
  4.7 4.0 %collective-permute-start.2 = (f32[264,256]{1,0:T(8,128)S(1)}, f32[264,256]{1,0:T(8,128)S(1)}, u32[]{:S(2)}, u32[]{:S(2)}) collective-permute-start(f32[264,256]{1,0:T(8,128)S(1)} %pack_spare.1), channel_id=1, source_target_pairs={{0,24},{1,25},{2,26},{3,27},{4,28},{5,29},{6,30},{7,31},{8,16},{9,... | collective-permute-start | bytes 811016 | tf_op jit(solution)/shard_map/ppermute | solution.py:1022
  9.4 10.4 %front_of_own_images.1 = (f32[4,256,256]{2,1,0:T(8,128)}, f32[4,256,256]{2,1,0:T(8,128)S(1)}, f32[4,256,256]{2,1,0:T(8,128)S(1)}, bf16[4,256,256]{2,1,0:T(8,128)...) custom-call(s32[1,1,5]{2,1,0:T(1,128)S(1)} %copy-done.19, ...), custom_call_target="tpu_custom_call" | custom-call | flops 20000000000 | bytes 1000000 | tf_op jit(solution)/shard_map/front_of_own_images/pallas_call | solution.py:796
  19.8 1.1 collective-permute-done.1.refs_6_
  21.2 9.0 %front_of_last_image.1 = (f32[4,256,256]{2,1,0:T(8,128)}, f32[4,256,256]{2,1,0:T(8,128)S(1)}, f32[4,256,256]{2,1,0:T(8,128)S(1)}, bf16[4,256,256]{2,1,0:T(8,128)...) custom-call(s32[1,1,5]{2,1,0:T(1,128)S(1)} %copy-done.19, ...), custom_call_target="tpu_custom_call", output_to_operand_aliasing={{0}: (29, {}), {1}: (27, {}), {2}: (30, {}), {3}: (31, {}),... | custom-call | flops 20000000000 | bytes 1000000 | tf_op jit(solution)/shard_map/front_of_last_image/pallas_call | solution.py:815
  30.8 5.8 %back_to_first_out.1 = (f32[8,9,16,256]{3,2,1,0:T(8,128)S(1)}, f32[8,9,16,256]{3,2,1,0:T(8,128)S(1)}, bf16[4,256,256]{2,1,0:T(8,128)(2,1)S(1)}, f32[16,256]{1,0:T(8,128)S(1)}, f32[8,256]{1,0:T(8,128)S(1)}) custom-call(f32[8,256]{1,0:T(8,128)S(1)} %get-tuple-element.88.notes, f32[4,256,256]{2,1,0:T(8,128)S(1)} %get-tuple-element.87.dmid_in.refs_4_, ...), custom_call_target="tpu_custom_call" | custom-call | tf_op jit(solution)/shard_map/back_to_first_out/pallas_call | solution.py:852
  37.1 1.6 %collective-permute-start.8 = (f32[2,2,144,256]{3,2,1,0:T(8,128)S(1)}, f32[2,2,144,256]{3,2,1,0:T(8,128)S(1)}, u32[]{:S(2)}, u32[]{:S(2)}) collective-permute-start(f32[2,2,144,256]{3,2,1,0:T(8,128)S(1)} %bitcast.209), channel_id=1, source_target_pairs={{0,8},{1,3},{2,10},{3,1},{4,12},{5,7},{6,14},{7,5},{8,0},{9,11},{1... | collective-permute-start | bytes 1769480 | tf_op jit(solution)/shard_map/ppermute | solution.py:1022
  39.8 1.5 %collective-permute-start.6 = (f32[2,2,144,256]{3,2,1,0:T(8,128)S(1)}, f32[2,2,144,256]{3,2,1,0:T(8,128)S(1)}, u32[]{:S(2)}, u32[]{:S(2)}) collective-permute-start(f32[2,2,144,256]{3,2,1,0:T(8,128)S(1)} %bitcast.210), channel_id=1, source_target_pairs={{0,16},{1,3},{2,18},{3,1},{4,20},{5,7},{6,22},{7,5},{8,24},{9,11},... | collective-permute-start | bytes 1769480 | tf_op jit(solution)/shard_map/ppermute | solution.py:1022
  41.3 4.1 %back_to_images.1 = (f32[5,256,256]{2,1,0:T(8,128)}, f32[2,256,256]{2,1,0:T(8,128)S(1)}, f32[24,256]{1,0:T(8,128)S(1)}) custom-call(s32[1,1]{1,0:T(1,128)S(6)} %copy.56.counts.refs_1_.refs_0_, s32[1,1]{1,0:T(1,128)S(6)} %copy.57.source.refs_2_.refs_1_, f32[5,256,256]{2,1,0:T(8,128)S(1)} %bitcast.146, f32[256,256]{1,0:T(8,128)S(1)} %get-tuple-element.86.refs_3_, ...), custom_call_target="tpu_custom_call" | custom-call | tf_op jit(solution)/shard_map/back_to_images/pallas_call | solution.py:871
  47.3 1.4 %collective-permute-start.11 = (f32[2,144,256]{2,1,0:T(8,128)S(1)}, f32[2,144,256]{2,1,0:T(8,128)S(1)}, u32[]{:S(2)}, u32[]{:S(2)}) collective-permute-start(f32[2,144,256]{2,1,0:T(8,128)S(1)} %get-tuple-element.107), channel_id=1, source_target_pairs={{0,16},{1,9},{2,18},{3,11},{4,20},{5,13},{6,22},{7,15},{8,24},{9,1... | collective-permute-start | bytes 884744 | tf_op jit(solution)/shard_map/ppermute | solution.py:1022
  49.6 3.9 %collective-permute-done.6 = f32[2,2,144,256]{3,2,1,0:T(8,128)S(1)} collective-permute-done((f32[2,2,144,256]{3,2,1,0:T(8,128)S(1)}, f32[2,2,144,256]{3,2,1,0:T(8,128)S(1)}, u32[]{:S(2)}, u32[]{:S(2)}) %collective-permute-start.6) | collective-permute-done | bytes 589856 | tf_op jit(solution)/shard_map/ppermute | solution.py:1022
  54.4 2.2 %collective-permute-done.11 = f32[2,144,256]{2,1,0:T(8,128)S(1)} collective-permute-done((f32[2,144,256]{2,1,0:T(8,128)S(1)}, f32[2,144,256]{2,1,0:T(8,128)S(1)}, u32[]{:S(2)}, u32[]{:S(2)}) %collective-permute-start.11) | collective-permute-done | bytes 294944 | tf_op jit(solution)/shard_map/ppermute | solution.py:1022
  57.2 1.6 %collective-permute-start.14 = (f32[64,256]{1,0:T(8,128)S(1)}, f32[64,256]{1,0:T(8,128)S(1)}, u32[]{:S(2)}, u32[]{:S(2)}) collective-permute-start(f32[64,256]{1,0:T(8,128)S(1)} %fusion.12), channel_id=1, source_target_pairs={{0,2},{1,9},{2,0},{3,11},{4,6},{5,13},{6,4},{7,15},{8,10},{9,1},{1... | collective-permute-start | bytes 196616 | tf_op jit(solution)/shard_map/ppermute | solution.py:1022
  58.7 1.6 %collective-permute-done.9 = f32[2,144,256]{2,1,0:T(8,128)S(1)} collective-permute-done((f32[2,144,256]{2,1,0:T(8,128)S(1)}, f32[2,144,256]{2,1,0:T(8,128)S(1)}, u32[]{:S(2)}, u32[]{:S(2)}) %collective-permute-start.9) | collective-permute-done | bytes 294944 | tf_op jit(solution)/shard_map/ppermute | solution.py:1022
  60.4 1.3 %collective-permute-start.13 = (f32[144,256]{1,0:T(8,128)S(1)}, f32[144,256]{1,0:T(8,128)S(1)}, u32[]{:S(2)}, u32[]{:S(2)}) collective-permute-start(f32[144,256]{1,0:T(8,128)S(1)} %fusion.7), channel_id=1, source_target_pairs={{0,8},{1,17},{2,10},{3,19},{4,12},{5,21},{6,14},{7,23},{8,0},{9,25... | collective-permute-start | bytes 442376 | tf_op jit(solution)/shard_map/ppermute | solution.py:1022
  62.7 2.7 %collective-permute-start.19 = (f32[144,256]{1,0:T(8,128)S(1)}, f32[144,256]{1,0:T(8,128)S(1)}, u32[]{:S(2)}, u32[]{:S(2)}) collective-permute-start(f32[144,256]{1,0:T(8,128)S(1)} %fusion.3), channel_id=1, source_target_pairs={{0,4},{1,5},{2,6},{3,7},{4,0},{5,1},{6,2},{7,3},{8,12},{9,13},{10,... | collective-permute-start | bytes 442376 | tf_op jit(solution)/shard_map/ppermute | solution.py:1022
  65.7 2.7 %collective-permute-start.22 = (f32[144,256]{1,0:T(8,128)S(1)}, f32[144,256]{1,0:T(8,128)S(1)}, u32[]{:S(2)}, u32[]{:S(2)}) collective-permute-start(f32[144,256]{1,0:T(8,128)S(1)} %fusion.5), channel_id=1, source_target_pairs={{0,4},{1,5},{2,6},{3,7},{4,0},{5,1},{6,2},{7,3},{8,12},{9,13},{10,... | collective-permute-start | bytes 442376 | tf_op jit(solution)/shard_map/ppermute | solution.py:1022
  68.4 10.6 %collective-permute-done.18 = f32[88,256]{1,0:T(8,128)S(1)} collective-permute-done((f32[88,256]{1,0:T(8,128)S(1)}, f32[88,256]{1,0:T(8,128)S(1)}, u32[]{:S(2)}, u32[]{:S(2)}) %collective-permute-start.18) | collective-permute-done | bytes 90144 | tf_op jit(solution)/shard_map/ppermute | solution.py:1022
  79.2 1.5 %collective-permute-start.17 = (f32[256,256]{1,0:T(8,128)S(1)}, f32[256,256]{1,0:T(8,128)S(1)}, u32[]{:S(2)}, u32[]{:S(2)}) collective-permute-start(f32[256,256]{1,0:T(8,128)S(1)} %bitcast_select_fusion), channel_id=1, source_target_pairs={{0,16},{1,9},{2,18},{3,11},{4,20},{5,13},{6,22},{7,15},{8,24},{9,1... | collective-permute-start | bytes 786440 | tf_op jit(solution)/shard_map/ppermute | solution.py:1022
  80.7 2.0 %collective-permute-start.21 = (f32[1,144,256]{2,1,0:T(8,128)S(1)}, f32[1,144,256]{2,1,0:T(8,128)S(1)}, u32[]{:S(2)}, u32[]{:S(2)}) collective-permute-start(f32[1,144,256]{2,1,0:T(8,128)S(1)} %bitcast.178), channel_id=1, source_target_pairs={{0,2},{1,17},{2,0},{3,19},{4,6},{5,21},{6,4},{7,23},{8,10},{9,25},... | collective-permute-start | bytes 442376 | tf_op jit(solution)/shard_map/ppermute | solution.py:1022
  83.8 2.0 %collective-permute-done.21 = f32[1,144,256]{2,1,0:T(8,128)S(1)} collective-permute-done((f32[1,144,256]{2,1,0:T(8,128)S(1)}, f32[1,144,256]{2,1,0:T(8,128)S(1)}, u32[]{:S(2)}, u32[]{:S(2)}) %collective-permute-start.21) | collective-permute-done | bytes 147488 | tf_op jit(solution)/shard_map/ppermute | solution.py:1022
  86.8 1.1 collective-permute-start.23
  89.6 1.2 collective-permute-start.27
  90.7 3.6 %collective-permute-done.23 = f32[176,256]{1,0:T(8,128)S(1)} collective-permute-done((f32[176,256]{1,0:T(8,128)S(1)}, f32[176,256]{1,0:T(8,128)S(1)}, u32[]{:S(2)}, u32[]{:S(2)}) %collective-permute-start.23) | collective-permute-done | bytes 180256 | tf_op jit(solution)/shard_map/ppermute | solution.py:1022
  94.5 1.2 %collective-permute-start.26 = (f32[336,256]{1,0:T(8,128)S(1)}, f32[336,256]{1,0:T(8,128)S(1)}, u32[]{:S(2)}, u32[]{:S(2)}) collective-permute-start(f32[336,256]{1,0:T(8,128)S(1)} %pad_maximum_fusion.7), channel_id=1, source_target_pairs={{0,16},{1,17},{2,18},{3,19},{4,20},{5,21},{6,22},{7,23},{8,24},{9,... | collective-permute-start | bytes 1032200 | tf_op jit(solution)/shard_map/ppermute | solution.py:1022
  96.5 2.8 %collective-permute-done.27 = f32[2,144,256]{2,1,0:T(8,128)S(1)} collective-permute-done((f32[2,144,256]{2,1,0:T(8,128)S(1)}, f32[2,144,256]{2,1,0:T(8,128)S(1)}, u32[]{:S(2)}, u32[]{:S(2)}) %collective-permute-start.27) | collective-permute-done | bytes 294944 | tf_op jit(solution)/shard_map/ppermute | solution.py:1022
  100.0 1.8 %collective-permute-done.26 = f32[336,256]{1,0:T(8,128)S(1)} collective-permute-done((f32[336,256]{1,0:T(8,128)S(1)}, f32[336,256]{1,0:T(8,128)S(1)}, u32[]{:S(2)}, u32[]{:S(2)}) %collective-permute-start.26) | collective-permute-done | bytes 344096 | tf_op jit(solution)/shard_map/ppermute | solution.py:1022
  101.8 2.0 %embed_gradient.1 = f32[512,256]{1,0:T(8,128)} custom-call(f32[16,8,256]{2,1,0:T(8,128)S(1)} %fusion.9.refs_0_, f32[16,256]{1,0:T(8,128)S(1)} %slice_add_fusion.19.refs_1_), custom_call_target="tpu_custom_call" | custom-call | flops 1 | bytes 1 | tf_op jit(solution)/shard_map/embed_gradient/pallas_call | solution.py:972
  104.5 1.0 collective-permute-done.30
  105.7 3.6 %collective-permute-done.29 = f32[4,144,256]{2,1,0:T(8,128)S(1)} collective-permute-done((f32[4,144,256]{2,1,0:T(8,128)S(1)}, f32[4,144,256]{2,1,0:T(8,128)S(1)}, u32[]{:S(2)}, u32[]{:S(2)}) %collective-permute-start.29) | collective-permute-done | bytes 589856 | tf_op jit(solution)/shard_map/ppermute | solution.py:1022
  110.8 2.1 %assemble.3 = f32[9,256,256]{2,1,0:T(8,128)} custom-call(f32[8,9,16,256]{3,2,1,0:T(8,128)S(1)} %pad_maximum_fusion.2.refs_0_, f32[8,9,16,256]{3,2,1,0:T(8,128)S(1)} %bitcast.148), custom_call_target="tpu_custom_call" | custom-call | flops 1 | bytes 1 | tf_op jit(solution)/shard_map/assemble/pallas_call | solution.py:914
  113.1 2.4 %assemble.2 = (f32[256,768]{1,0:T(8,128)}, f32[256,256]{1,0:T(8,128)}, f32[9,256,256]{2,1,0:T(8,128)}) custom-call(f32[8,4,16,256]{3,2,1,0:T(8,128)S(1)} %pad_maximum_fusion.5.refs_0_, f32[8,4,16,256]{3,2,1,0:T(8,128)S(1)} %bitcast.149, f32[8,9,16,256]{3,2,1,0:T(8,128)S(1)} %pad_maximum_fusion.refs_2_, f32[8,9,16,256]{3,2,1,0:T(8,128)S(1)} %bitcast.147), custom_call_target="tpu_custom_call" | custom-call | flops 1 | bytes 1 | tf_op jit(solution)/shard_map/assemble/pallas_call | solution.py:914
  (142 shorter events, 18.2 us)
Async XLA Ops:
  4.7 15.1 %collective-permute-start.2 = (f32[264,256]{1,0:T(8,128)S(1)}, f32[264,256]{1,0:T(8,128)S(1)}, u32[]{:S(2)}, u32[]{:S(2)}) collective-permute-start(f32[264,256]{1,0:T(8,128)S(1)} %pack_spare.1), channel_id=1, source_target_pairs={{0,24},{1,25},{2,26},{3,27},{4,28},{5,29},{6,30},{7,31},{8,16},{9,... | collective-permute-start | bytes 811016 | tf_op jit(solution)/shard_map/ppermute | solution.py:1022
  8.6 12.3 %collective-permute-start.1 = (f32[264,256]{1,0:T(8,128)S(1)}, f32[264,256]{1,0:T(8,128)S(1)}, u32[]{:S(2)}, u32[]{:S(2)}) collective-permute-start(f32[264,256]{1,0:T(8,128)S(1)} %pack_spare.1), channel_id=1, source_target_pairs={{0,16},{1,17},{2,18},{3,19},{4,20},{5,21},{6,22},{7,23},{8,24},{9,... | collective-permute-start | bytes 811016 | tf_op jit(solution)/shard_map/ppermute | solution.py:1022
  9.1 12.1 %collective-permute-start = (f32[264,256]{1,0:T(8,128)S(1)}, f32[264,256]{1,0:T(8,128)S(1)}, u32[]{:S(2)}, u32[]{:S(2)}) collective-permute-start(f32[264,256]{1,0:T(8,128)S(1)} %pack_spare.1), channel_id=1, source_target_pairs={{0,8},{1,9},{2,10},{3,11},{4,12},{5,13},{6,14},{7,15},{8,0},{9,1},... | collective-permute-start | bytes 811016 | tf_op jit(solution)/shard_map/ppermute | solution.py:1022
  30.2 6.7 %collective-permute-start.5 = (f32[8,9,16,256]{3,2,1,0:T(8,128)S(1)}, f32[8,9,16,256]{3,2,1,0:T(8,128)S(1)}, u32[]{:S(2)}, u32[]{:S(2)}) collective-permute-start(f32[8,9,16,256]{3,2,1,0:T(8,128)S(1)} %get-tuple-element.99), channel_id=1, source_target_pairs={{0,1},{1,0},{2,3},{3,2},{4,5},{5,4},{6,7},{7,6},{8,9},{9,8},{10,11... | collective-permute-start | bytes 3538952 | tf_op jit(solution)/shard_map/ppermute | solution.py:1022
  30.3 6.5 %collective-permute-start.4 = (f32[8,4,16,256]{3,2,1,0:T(8,128)S(1)}, f32[8,4,16,256]{3,2,1,0:T(8,128)S(1)}, u32[]{:S(2)}, u32[]{:S(2)}) collective-permute-start(f32[8,4,16,256]{3,2,1,0:T(8,128)S(1)} %get-tuple-element.97), channel_id=1, source_target_pairs={{0,1},{1,0},{2,3},{3,2},{4,5},{5,4},{6,7},{7,6},{8,9},{9,8},{10,11... | collective-permute-start | bytes 1572872 | tf_op jit(solution)/shard_map/ppermute | solution.py:1022
  36.6 2.9 %collective-permute-start.3 = (f32[8,9,16,256]{3,2,1,0:T(8,128)S(1)}, f32[8,9,16,256]{3,2,1,0:T(8,128)S(1)}, u32[]{:S(2)}, u32[]{:S(2)}) collective-permute-start(f32[8,9,16,256]{3,2,1,0:T(8,128)S(1)} %get-tuple-element.95), channel_id=1, source_target_pairs={{0,1},{1,0},{2,3},{3,2},{4,5},{5,4},{6,7},{7,6},{8,9},{9,8},{10,11... | collective-permute-start | bytes 3538952 | tf_op jit(solution)/shard_map/ppermute | solution.py:1022
  37.1 10.0 %collective-permute-start.8 = (f32[2,2,144,256]{3,2,1,0:T(8,128)S(1)}, f32[2,2,144,256]{3,2,1,0:T(8,128)S(1)}, u32[]{:S(2)}, u32[]{:S(2)}) collective-permute-start(f32[2,2,144,256]{3,2,1,0:T(8,128)S(1)} %bitcast.209), channel_id=1, source_target_pairs={{0,8},{1,3},{2,10},{3,1},{4,12},{5,7},{6,14},{7,5},{8,0},{9,11},{1... | collective-permute-start | bytes 1769480 | tf_op jit(solution)/shard_map/ppermute | solution.py:1022
  38.7 8.4 %collective-permute-start.7 = (f32[2,2,64,256]{3,2,1,0:T(8,128)S(1)}, f32[2,2,64,256]{3,2,1,0:T(8,128)S(1)}, u32[]{:S(2)}, u32[]{:S(2)}) collective-permute-start(f32[2,2,64,256]{3,2,1,0:T(8,128)S(1)} %bitcast.215), channel_id=1, source_target_pairs={{0,16},{1,17},{2,18},{3,19},{4,20},{5,21},{6,22},{7,23},{8,24},{9,... | collective-permute-start | bytes 786440 | tf_op jit(solution)/shard_map/ppermute | solution.py:1022
  39.8 13.7 %collective-permute-start.6 = (f32[2,2,144,256]{3,2,1,0:T(8,128)S(1)}, f32[2,2,144,256]{3,2,1,0:T(8,128)S(1)}, u32[]{:S(2)}, u32[]{:S(2)}) collective-permute-start(f32[2,2,144,256]{3,2,1,0:T(8,128)S(1)} %bitcast.210), channel_id=1, source_target_pairs={{0,16},{1,3},{2,18},{3,1},{4,20},{5,7},{6,22},{7,5},{8,24},{9,11},... | collective-permute-start | bytes 1769480 | tf_op jit(solution)/shard_map/ppermute | solution.py:1022
  47.3 9.3 %collective-permute-start.11 = (f32[2,144,256]{2,1,0:T(8,128)S(1)}, f32[2,144,256]{2,1,0:T(8,128)S(1)}, u32[]{:S(2)}, u32[]{:S(2)}) collective-permute-start(f32[2,144,256]{2,1,0:T(8,128)S(1)} %get-tuple-element.107), channel_id=1, source_target_pairs={{0,16},{1,9},{2,18},{3,11},{4,20},{5,13},{6,22},{7,15},{8,24},{9,1... | collective-permute-start | bytes 884744 | tf_op jit(solution)/shard_map/ppermute | solution.py:1022
  48.7 5.7 %collective-permute-start.10 = (f32[2,64,256]{2,1,0:T(8,128)S(1)}, f32[2,64,256]{2,1,0:T(8,128)S(1)}, u32[]{:S(2)}, u32[]{:S(2)}) collective-permute-start(f32[2,64,256]{2,1,0:T(8,128)S(1)} %get-tuple-element.108), channel_id=1, source_target_pairs={{0,8},{1,3},{2,10},{3,1},{4,12},{5,7},{6,14},{7,5},{8,0},{9,11},{1... | collective-permute-start | bytes 393224 | tf_op jit(solution)/shard_map/ppermute | solution.py:1022
  53.6 6.8 %collective-permute-start.9 = (f32[2,144,256]{2,1,0:T(8,128)S(1)}, f32[2,144,256]{2,1,0:T(8,128)S(1)}, u32[]{:S(2)}, u32[]{:S(2)}) collective-permute-start(f32[2,144,256]{2,1,0:T(8,128)S(1)} %get-tuple-element.109), channel_id=1, source_target_pairs={{0,2},{1,9},{2,0},{3,11},{4,6},{5,13},{6,4},{7,15},{8,10},{9,1},{1... | collective-permute-start | bytes 884744 | tf_op jit(solution)/shard_map/ppermute | solution.py:1022
  56.6 6.0 %collective-permute-start.16 = (f32[144,256]{1,0:T(8,128)S(1)}, f32[144,256]{1,0:T(8,128)S(1)}, u32[]{:S(2)}, u32[]{:S(2)}) collective-permute-start(f32[144,256]{1,0:T(8,128)S(1)} %fusion.6), channel_id=1, source_target_pairs={{0,2},{1,17},{2,0},{3,19},{4,6},{5,21},{6,4},{7,23},{8,10},{9,25},... | collective-permute-start | bytes 442376 | tf_op jit(solution)/shard_map/ppermute | solution.py:1022
  57.2 5.5 %collective-permute-start.14 = (f32[64,256]{1,0:T(8,128)S(1)}, f32[64,256]{1,0:T(8,128)S(1)}, u32[]{:S(2)}, u32[]{:S(2)}) collective-permute-start(f32[64,256]{1,0:T(8,128)S(1)} %fusion.12), channel_id=1, source_target_pairs={{0,2},{1,9},{2,0},{3,11},{4,6},{5,13},{6,4},{7,15},{8,10},{9,1},{1... | collective-permute-start | bytes 196616 | tf_op jit(solution)/shard_map/ppermute | solution.py:1022
  60.4 5.3 %collective-permute-start.13 = (f32[144,256]{1,0:T(8,128)S(1)}, f32[144,256]{1,0:T(8,128)S(1)}, u32[]{:S(2)}, u32[]{:S(2)}) collective-permute-start(f32[144,256]{1,0:T(8,128)S(1)} %fusion.7), channel_id=1, source_target_pairs={{0,8},{1,17},{2,10},{3,19},{4,12},{5,21},{6,14},{7,23},{8,0},{9,25... | collective-permute-start | bytes 442376 | tf_op jit(solution)/shard_map/ppermute | solution.py:1022
  61.7 17.4 %collective-permute-start.12 = (f32[256,256]{1,0:T(8,128)S(1)}, f32[256,256]{1,0:T(8,128)S(1)}, u32[]{:S(2)}, u32[]{:S(2)}) collective-permute-start(f32[256,256]{1,0:T(8,128)S(1)} %slice_bitcast_fusion), channel_id=1, source_target_pairs={{0,8},{1,17},{2,10},{3,19},{4,12},{5,21},{6,14},{7,23},{8,0},{9,25... | collective-permute-start | bytes 786440 | tf_op jit(solution)/shard_map/ppermute | solution.py:1022
  62.7 16.3 %collective-permute-start.19 = (f32[144,256]{1,0:T(8,128)S(1)}, f32[144,256]{1,0:T(8,128)S(1)}, u32[]{:S(2)}, u32[]{:S(2)}) collective-permute-start(f32[144,256]{1,0:T(8,128)S(1)} %fusion.3), channel_id=1, source_target_pairs={{0,4},{1,5},{2,6},{3,7},{4,0},{5,1},{6,2},{7,3},{8,12},{9,13},{10,... | collective-permute-start | bytes 442376 | tf_op jit(solution)/shard_map/ppermute | solution.py:1022
  65.4 13.6 %collective-permute-start.18 = (f32[88,256]{1,0:T(8,128)S(1)}, f32[88,256]{1,0:T(8,128)S(1)}, u32[]{:S(2)}, u32[]{:S(2)}) collective-permute-start(f32[88,256]{1,0:T(8,128)S(1)} %pad_maximum_fusion.13), channel_id=1, source_target_pairs={{0,4},{1,5},{2,6},{3,7},{4,0},{5,1},{6,2},{7,3},{8,12},{9,13},{10,... | collective-permute-start | bytes 270344 | tf_op jit(solution)/shard_map/ppermute | solution.py:1022
  65.7 16.9 %collective-permute-start.22 = (f32[144,256]{1,0:T(8,128)S(1)}, f32[144,256]{1,0:T(8,128)S(1)}, u32[]{:S(2)}, u32[]{:S(2)}) collective-permute-start(f32[144,256]{1,0:T(8,128)S(1)} %fusion.5), channel_id=1, source_target_pairs={{0,4},{1,5},{2,6},{3,7},{4,0},{5,1},{6,2},{7,3},{8,12},{9,13},{10,... | collective-permute-start | bytes 442376 | tf_op jit(solution)/shard_map/ppermute | solution.py:1022
  79.0 4.7 %collective-permute-start.20 = (f32[96,256]{1,0:T(8,128)S(1)}, f32[96,256]{1,0:T(8,128)S(1)}, u32[]{:S(2)}, u32[]{:S(2)}) collective-permute-start(f32[96,256]{1,0:T(8,128)S(1)} %pad_maximum_fusion.12), channel_id=1, source_target_pairs={{0,2},{1,9},{2,0},{3,11},{4,6},{5,13},{6,4},{7,15},{8,10},{9,1},{1... | collective-permute-start | bytes 294920 | tf_op jit(solution)/shard_map/ppermute | solution.py:1022
  79.2 8.7 %collective-permute-start.17 = (f32[256,256]{1,0:T(8,128)S(1)}, f32[256,256]{1,0:T(8,128)S(1)}, u32[]{:S(2)}, u32[]{:S(2)}) collective-permute-start(f32[256,256]{1,0:T(8,128)S(1)} %bitcast_select_fusion), channel_id=1, source_target_pairs={{0,16},{1,9},{2,18},{3,11},{4,20},{5,13},{6,22},{7,15},{8,24},{9,1... | collective-permute-start | bytes 786440 | tf_op jit(solution)/shard_map/ppermute | solution.py:1022
  80.7 5.1 %collective-permute-start.21 = (f32[1,144,256]{2,1,0:T(8,128)S(1)}, f32[1,144,256]{2,1,0:T(8,128)S(1)}, u32[]{:S(2)}, u32[]{:S(2)}) collective-permute-start(f32[1,144,256]{2,1,0:T(8,128)S(1)} %bitcast.178), channel_id=1, source_target_pairs={{0,2},{1,17},{2,0},{3,19},{4,6},{5,21},{6,4},{7,23},{8,10},{9,25},... | collective-permute-start | bytes 442376 | tf_op jit(solution)/shard_map/ppermute | solution.py:1022
  82.7 6.9 %collective-permute-start.25 = (f32[1,144,256]{2,1,0:T(8,128)S(1)}, f32[1,144,256]{2,1,0:T(8,128)S(1)}, u32[]{:S(2)}, u32[]{:S(2)}) collective-permute-start(f32[1,144,256]{2,1,0:T(8,128)S(1)} %bitcast.183), channel_id=1, source_target_pairs={{0,8},{1,17},{2,10},{3,19},{4,12},{5,21},{6,14},{7,23},{8,0},{9,25... | collective-permute-start | bytes 442376 | tf_op jit(solution)/shard_map/ppermute | solution.py:1022
  85.8 8.6 %collective-permute-start.24 = (f32[2,144,256]{2,1,0:T(8,128)S(1)}, f32[2,144,256]{2,1,0:T(8,128)S(1)}, u32[]{:S(2)}, u32[]{:S(2)}) collective-permute-start(f32[2,144,256]{2,1,0:T(8,128)S(1)} %pad_maximum_fusion.8), channel_id=1, source_target_pairs={{0,16},{1,9},{2,18},{3,11},{4,20},{5,13},{6,22},{7,15},{8,24},{9,1... | collective-permute-start | bytes 884744 | tf_op jit(solution)/shard_map/ppermute | solution.py:1022
  86.8 7.5 %collective-permute-start.23 = (f32[176,256]{1,0:T(8,128)S(1)}, f32[176,256]{1,0:T(8,128)S(1)}, u32[]{:S(2)}, u32[]{:S(2)}) collective-permute-start(f32[176,256]{1,0:T(8,128)S(1)} %pad_maximum_fusion.10), channel_id=1, source_target_pairs={{0,8},{1,3},{2,10},{3,1},{4,12},{5,7},{6,14},{7,5},{8,0},{9,11},{1... | collective-permute-start | bytes 540680 | tf_op jit(solution)/shard_map/ppermute | solution.py:1022
  89.6 9.8 %collective-permute-start.27 = (f32[2,144,256]{2,1,0:T(8,128)S(1)}, f32[2,144,256]{2,1,0:T(8,128)S(1)}, u32[]{:S(2)}, u32[]{:S(2)}) collective-permute-start(f32[2,144,256]{2,1,0:T(8,128)S(1)} %maximum_add_fusion.1), channel_id=1, source_target_pairs={{0,2},{1,9},{2,0},{3,11},{4,6},{5,13},{6,4},{7,15},{8,10},{9,1},{1... | collective-permute-start | bytes 884744 | tf_op jit(solution)/shard_map/ppermute | solution.py:1022
  94.5 7.3 %collective-permute-start.26 = (f32[336,256]{1,0:T(8,128)S(1)}, f32[336,256]{1,0:T(8,128)S(1)}, u32[]{:S(2)}, u32[]{:S(2)}) collective-permute-start(f32[336,256]{1,0:T(8,128)S(1)} %pad_maximum_fusion.7), channel_id=1, source_target_pairs={{0,16},{1,17},{2,18},{3,19},{4,20},{5,21},{6,22},{7,23},{8,24},{9,... | collective-permute-start | bytes 1032200 | tf_op jit(solution)/shard_map/ppermute | solution.py:1022
  95.7 9.9 %collective-permute-start.30 = (f32[4,144,256]{2,1,0:T(8,128)S(1)}, f32[4,144,256]{2,1,0:T(8,128)S(1)}, u32[]{:S(2)}, u32[]{:S(2)}) collective-permute-start(f32[4,144,256]{2,1,0:T(8,128)S(1)} %pad_maximum_fusion.3), channel_id=1, source_target_pairs={{0,8},{1,3},{2,10},{3,1},{4,12},{5,7},{6,14},{7,5},{8,0},{9,11},{1... | collective-permute-start | bytes 1769480 | tf_op jit(solution)/shard_map/ppermute | solution.py:1022
  99.4 9.9 %collective-permute-start.29 = (f32[4,144,256]{2,1,0:T(8,128)S(1)}, f32[4,144,256]{2,1,0:T(8,128)S(1)}, u32[]{:S(2)}, u32[]{:S(2)}) collective-permute-start(f32[4,144,256]{2,1,0:T(8,128)S(1)} %pad_maximum_fusion.4), channel_id=1, source_target_pairs={{0,16},{1,3},{2,18},{3,1},{4,20},{5,7},{6,22},{7,5},{8,24},{9,11},... | collective-permute-start | bytes 1769480 | tf_op jit(solution)/shard_map/ppermute | solution.py:1022
  105.6 5.2 %collective-permute-start.32 = (f32[8,144,256]{2,1,0:T(8,128)S(1)}, f32[8,144,256]{2,1,0:T(8,128)S(1)}, u32[]{:S(2)}, u32[]{:S(2)}) collective-permute-start(f32[8,144,256]{2,1,0:T(8,128)S(1)} %pad_maximum_fusion.1), channel_id=1, source_target_pairs={{0,1},{1,0},{2,3},{3,2},{4,5},{5,4},{6,7},{7,6},{8,9},{9,8},{10,11... | collective-permute-start | bytes 3538952 | tf_op jit(solution)/shard_map/ppermute | solution.py:1022
  109.4 3.7 %collective-permute-start.31 = (f32[8,144,256]{2,1,0:T(8,128)S(1)}, f32[8,144,256]{2,1,0:T(8,128)S(1)}, u32[]{:S(2)}, u32[]{:S(2)}) collective-permute-start(f32[8,144,256]{2,1,0:T(8,128)S(1)} %maximum_add_fusion), channel_id=1, source_target_pairs={{0,1},{1,0},{2,3},{3,2},{4,5},{5,4},{6,7},{7,6},{8,9},{9,8},{10,11... | collective-permute-start | bytes 3538952 | tf_op jit(solution)/shard_map/ppermute | solution.py:1022
  109.5 3.6 %collective-permute-start.28 = (f32[8,64,256]{2,1,0:T(8,128)S(1)}, f32[8,64,256]{2,1,0:T(8,128)S(1)}, u32[]{:S(2)}, u32[]{:S(2)}) collective-permute-start(f32[8,64,256]{2,1,0:T(8,128)S(1)} %pad_maximum_fusion.6), channel_id=1, source_target_pairs={{0,1},{1,0},{2,3},{3,2},{4,5},{5,4},{6,7},{7,6},{8,9},{9,8},{10,11... | collective-permute-start | bytes 1572872 | tf_op jit(solution)/shard_map/ppermute | solution.py:1022
  (21 other events, 95.9 us)

commit v4 on v3

--- a/solution.py
+++ b/solution.py
@@ -653,14 +653,11 @@
     )
     copies.start((TO, LOW), v_low, low)
 
-    def tap(di, carry):
-        rows = pl.ds(pl.multiple_of(SIDE * (2 - di), SIDE), TOK)
-        g = dot(act1[...].reshape(WORK * TOK, C), shifted[:, rows, :].reshape(WORK * TOK, 3 * C), TN)
+    act = act1[...].reshape(WORK * TOK, C)
+    for di in range(3):
+        g = dot(act, window(shifted, WORK, 2 - di), TN)
         for dj in range(3):
             scatter_unit(blocks, di * 3 + dj, g[:, dj * C : (dj + 1) * C], codes)
-        return carry
-
-    lax.fori_loop(0, 3, tap, 0)
     copies.start((TO, GIVE), blocks.at[8:16], give)
     copies.start((TO, KEEP), blocks.at[0:8], keep)
     sums[...] = sums_in[...]

time: 116 us -> 116 us (level)
  no operation moved by 1% of the time
where the time goes in v4:
time: 116 us
  waiting for transfers between devices  37.7 us (33%)
  Pallas kernels  36.4 us (31%)
  starting transfers between devices  32.7 us (28%)
  other arithmetic  3.14 us (3%)
  local copies, waits for them, and re-layouts  2.84 us (2%)
  between operations  2.81 us (2%)
    ppermute x33, waiting for transfers between devices, send(): return lax.ppermute(v, AXES, perm)  37.7 us
    ppermute x33, starting transfers between devices, send(): return lax.ppermute(v, AXES, perm)  32.7 us
    pallas_call x1, Pallas kernels, call_one(): pl.pallas_call(kernel_one, name='front_of_own_images', in_specs=[SMEM, HB...  10.4 us
    pallas_call x1, Pallas kernels, call_two(): pl.pallas_call(lambda *refs: kernel_two(n_bucket, *refs), name='front_of_...  8.99 us
    pallas_call x1, Pallas kernels, call_three(): pl.pallas_call(kernel_three, name='back_to_first_out', in_specs=[VMEM, AN...  5.66 us
    pallas_call x2, Pallas kernels, assemble(): pl.pallas_call(lambda *refs: assemble_kernel(orders, *refs), name='assemb...  4.57 us
    pallas_call x1, Pallas kernels, call_four(): pl.pallas_call(lambda *refs: kernel_four(n_bucket, *refs), name='back_to_...  4.24 us
  transfers between devices with their start and end apart: 33, of which 20 were waited for; matrix products, arithmetic and copies ran while one was open for 3% of the time, Pallas kernels for 21%

profile of v4, /device:TPU:0, one launch (start us, length us, event | category | flops | bytes accessed | tf_op | source)
XLA Modules:
  0.0 115.6 jit_solution(634334555479331121)
XLA Ops:
  2.0 1.3 %copy-done.2 = f32[1,1,5,256,256]{4,3,2,1,0:T(8,128)S(1)} copy-done((f32[1,1,5,256,256]{4,3,2,1,0:T(8,128)S(1)}, f32[1,1,5,256,256]{4,3,2,1,0:T(8,128)}, u32[]{:S(2)}) %copy-start.2) | copy-done | bytes 1310744
  4.7 4.0 %collective-permute-start.2 = (f32[264,256]{1,0:T(8,128)S(1)}, f32[264,256]{1,0:T(8,128)S(1)}, u32[]{:S(2)}, u32[]{:S(2)}) collective-permute-start(f32[264,256]{1,0:T(8,128)S(1)} %pack_spare.1), channel_id=1, source_target_pairs={{0,24},{1,25},{2,26},{3,27},{4,28},{5,29},{6,30},{7,31},{8,16},{9,... | collective-permute-start | bytes 811016 | tf_op jit(solution)/shard_map/ppermute | solution.py:1019
  9.4 10.4 %front_of_own_images.1 = (f32[4,256,256]{2,1,0:T(8,128)}, f32[4,256,256]{2,1,0:T(8,128)S(1)}, f32[4,256,256]{2,1,0:T(8,128)S(1)}, bf16[4,256,256]{2,1,0:T(8,128)...) custom-call(s32[1,1,5]{2,1,0:T(1,128)S(1)} %copy-done.19, ...), custom_call_target="tpu_custom_call" | custom-call | flops 20000000000 | bytes 1000000 | tf_op jit(solution)/shard_map/front_of_own_images/pallas_call | solution.py:793
  19.8 1.1 collective-permute-done.1.refs_6_
  21.2 9.0 %front_of_last_image.1 = (f32[4,256,256]{2,1,0:T(8,128)}, f32[4,256,256]{2,1,0:T(8,128)S(1)}, f32[4,256,256]{2,1,0:T(8,128)S(1)}, bf16[4,256,256]{2,1,0:T(8,128)...) custom-call(s32[1,1,5]{2,1,0:T(1,128)S(1)} %copy-done.19, ...), custom_call_target="tpu_custom_call", output_to_operand_aliasing={{0}: (29, {}), {1}: (27, {}), {2}: (30, {}), {3}: (31, {}),... | custom-call | flops 20000000000 | bytes 1000000 | tf_op jit(solution)/shard_map/front_of_last_image/pallas_call | solution.py:812
  30.8 5.7 %back_to_first_out.1 = (f32[8,9,16,256]{3,2,1,0:T(8,128)S(1)}, f32[8,9,16,256]{3,2,1,0:T(8,128)S(1)}, bf16[4,256,256]{2,1,0:T(8,128)(2,1)S(1)}, f32[16,256]{1,0:T(8,128)S(1)}, f32[8,256]{1,0:T(8,128)S(1)}) custom-call(f32[8,256]{1,0:T(8,128)S(1)} %get-tuple-element.88.notes, f32[4,256,256]{2,1,0:T(8,128)S(1)} %get-tuple-element.87.dmid_in.refs_4_, ...), custom_call_target="tpu_custom_call" | custom-call | tf_op jit(solution)/shard_map/back_to_first_out/pallas_call | solution.py:849
  37.0 1.6 %collective-permute-start.8 = (f32[2,2,144,256]{3,2,1,0:T(8,128)S(1)}, f32[2,2,144,256]{3,2,1,0:T(8,128)S(1)}, u32[]{:S(2)}, u32[]{:S(2)}) collective-permute-start(f32[2,2,144,256]{3,2,1,0:T(8,128)S(1)} %bitcast.209), channel_id=1, source_target_pairs={{0,8},{1,3},{2,10},{3,1},{4,12},{5,7},{6,14},{7,5},{8,0},{9,11},{1... | collective-permute-start | bytes 1769480 | tf_op jit(solution)/shard_map/ppermute | solution.py:1019
  39.7 1.5 %collective-permute-start.6 = (f32[2,2,144,256]{3,2,1,0:T(8,128)S(1)}, f32[2,2,144,256]{3,2,1,0:T(8,128)S(1)}, u32[]{:S(2)}, u32[]{:S(2)}) collective-permute-start(f32[2,2,144,256]{3,2,1,0:T(8,128)S(1)} %bitcast.210), channel_id=1, source_target_pairs={{0,16},{1,3},{2,18},{3,1},{4,20},{5,7},{6,22},{7,5},{8,24},{9,11},... | collective-permute-start | bytes 1769480 | tf_op jit(solution)/shard_map/ppermute | solution.py:1019
  41.1 4.2 %back_to_images.1 = (f32[5,256,256]{2,1,0:T(8,128)}, f32[2,256,256]{2,1,0:T(8,128)S(1)}, f32[24,256]{1,0:T(8,128)S(1)}) custom-call(s32[1,1]{1,0:T(1,128)S(6)} %copy.56.counts.refs_1_.refs_0_, s32[1,1]{1,0:T(1,128)S(6)} %copy.57.source.refs_2_.refs_1_, f32[5,256,256]{2,1,0:T(8,128)S(1)} %bitcast.146, f32[256,256]{1,0:T(8,128)S(1)} %get-tuple-element.86.refs_3_, ...), custom_call_target="tpu_custom_call" | custom-call | tf_op jit(solution)/shard_map/back_to_images/pallas_call | solution.py:868
  47.2 1.4 %collective-permute-start.11 = (f32[2,144,256]{2,1,0:T(8,128)S(1)}, f32[2,144,256]{2,1,0:T(8,128)S(1)}, u32[]{:S(2)}, u32[]{:S(2)}) collective-permute-start(f32[2,144,256]{2,1,0:T(8,128)S(1)} %get-tuple-element.107), channel_id=1, source_target_pairs={{0,16},{1,9},{2,18},{3,11},{4,20},{5,13},{6,22},{7,15},{8,24},{9,1... | collective-permute-start | bytes 884744 | tf_op jit(solution)/shard_map/ppermute | solution.py:1019
  49.4 3.9 %collective-permute-done.6 = f32[2,2,144,256]{3,2,1,0:T(8,128)S(1)} collective-permute-done((f32[2,2,144,256]{3,2,1,0:T(8,128)S(1)}, f32[2,2,144,256]{3,2,1,0:T(8,128)S(1)}, u32[]{:S(2)}, u32[]{:S(2)}) %collective-permute-start.6) | collective-permute-done | bytes 589856 | tf_op jit(solution)/shard_map/ppermute | solution.py:1019
  54.3 2.2 %collective-permute-done.11 = f32[2,144,256]{2,1,0:T(8,128)S(1)} collective-permute-done((f32[2,144,256]{2,1,0:T(8,128)S(1)}, f32[2,144,256]{2,1,0:T(8,128)S(1)}, u32[]{:S(2)}, u32[]{:S(2)}) %collective-permute-start.11) | collective-permute-done | bytes 294944 | tf_op jit(solution)/shard_map/ppermute | solution.py:1019
  57.0 1.6 %collective-permute-start.14 = (f32[64,256]{1,0:T(8,128)S(1)}, f32[64,256]{1,0:T(8,128)S(1)}, u32[]{:S(2)}, u32[]{:S(2)}) collective-permute-start(f32[64,256]{1,0:T(8,128)S(1)} %fusion.12), channel_id=1, source_target_pairs={{0,2},{1,9},{2,0},{3,11},{4,6},{5,13},{6,4},{7,15},{8,10},{9,1},{1... | collective-permute-start | bytes 196616 | tf_op jit(solution)/shard_map/ppermute | solution.py:1019
  58.6 1.6 %collective-permute-done.9 = f32[2,144,256]{2,1,0:T(8,128)S(1)} collective-permute-done((f32[2,144,256]{2,1,0:T(8,128)S(1)}, f32[2,144,256]{2,1,0:T(8,128)S(1)}, u32[]{:S(2)}, u32[]{:S(2)}) %collective-permute-start.9) | collective-permute-done | bytes 294944 | tf_op jit(solution)/shard_map/ppermute | solution.py:1019
  60.2 1.3 %collective-permute-start.13 = (f32[144,256]{1,0:T(8,128)S(1)}, f32[144,256]{1,0:T(8,128)S(1)}, u32[]{:S(2)}, u32[]{:S(2)}) collective-permute-start(f32[144,256]{1,0:T(8,128)S(1)} %fusion.7), channel_id=1, source_target_pairs={{0,8},{1,17},{2,10},{3,19},{4,12},{5,21},{6,14},{7,23},{8,0},{9,25... | collective-permute-start | bytes 442376 | tf_op jit(solution)/shard_map/ppermute | solution.py:1019
  62.6 2.7 %collective-permute-start.19 = (f32[144,256]{1,0:T(8,128)S(1)}, f32[144,256]{1,0:T(8,128)S(1)}, u32[]{:S(2)}, u32[]{:S(2)}) collective-permute-start(f32[144,256]{1,0:T(8,128)S(1)} %fusion.3), channel_id=1, source_target_pairs={{0,4},{1,5},{2,6},{3,7},{4,0},{5,1},{6,2},{7,3},{8,12},{9,13},{10,... | collective-permute-start | bytes 442376 | tf_op jit(solution)/shard_map/ppermute | solution.py:1019
  65.6 2.7 %collective-permute-start.22 = (f32[144,256]{1,0:T(8,128)S(1)}, f32[144,256]{1,0:T(8,128)S(1)}, u32[]{:S(2)}, u32[]{:S(2)}) collective-permute-start(f32[144,256]{1,0:T(8,128)S(1)} %fusion.5), channel_id=1, source_target_pairs={{0,4},{1,5},{2,6},{3,7},{4,0},{5,1},{6,2},{7,3},{8,12},{9,13},{10,... | collective-permute-start | bytes 442376 | tf_op jit(solution)/shard_map/ppermute | solution.py:1019
  68.3 10.6 %collective-permute-done.18 = f32[88,256]{1,0:T(8,128)S(1)} collective-permute-done((f32[88,256]{1,0:T(8,128)S(1)}, f32[88,256]{1,0:T(8,128)S(1)}, u32[]{:S(2)}, u32[]{:S(2)}) %collective-permute-start.18) | collective-permute-done | bytes 90144 | tf_op jit(solution)/shard_map/ppermute | solution.py:1019
  79.0 1.5 %collective-permute-start.17 = (f32[256,256]{1,0:T(8,128)S(1)}, f32[256,256]{1,0:T(8,128)S(1)}, u32[]{:S(2)}, u32[]{:S(2)}) collective-permute-start(f32[256,256]{1,0:T(8,128)S(1)} %bitcast_select_fusion), channel_id=1, source_target_pairs={{0,16},{1,9},{2,18},{3,11},{4,20},{5,13},{6,22},{7,15},{8,24},{9,1... | collective-permute-start | bytes 786440 | tf_op jit(solution)/shard_map/ppermute | solution.py:1019
  80.5 2.0 %collective-permute-start.21 = (f32[1,144,256]{2,1,0:T(8,128)S(1)}, f32[1,144,256]{2,1,0:T(8,128)S(1)}, u32[]{:S(2)}, u32[]{:S(2)}) collective-permute-start(f32[1,144,256]{2,1,0:T(8,128)S(1)} %bitcast.178), channel_id=1, source_target_pairs={{0,2},{1,17},{2,0},{3,19},{4,6},{5,21},{6,4},{7,23},{8,10},{9,25},... | collective-permute-start | bytes 442376 | tf_op jit(solution)/shard_map/ppermute | solution.py:1019
  83.7 2.0 %collective-permute-done.21 = f32[1,144,256]{2,1,0:T(8,128)S(1)} collective-permute-done((f32[1,144,256]{2,1,0:T(8,128)S(1)}, f32[1,144,256]{2,1,0:T(8,128)S(1)}, u32[]{:S(2)}, u32[]{:S(2)}) %collective-permute-start.21) | collective-permute-done | bytes 147488 | tf_op jit(solution)/shard_map/ppermute | solution.py:1019
  86.7 1.1 collective-permute-start.23
  89.4 1.2 %collective-permute-start.27 = (f32[2,144,256]{2,1,0:T(8,128)S(1)}, f32[2,144,256]{2,1,0:T(8,128)S(1)}, u32[]{:S(2)}, u32[]{:S(2)}) collective-permute-start(f32[2,144,256]{2,1,0:T(8,128)S(1)} %maximum_add_fusion.1), channel_id=1, source_target_pairs={{0,2},{1,9},{2,0},{3,11},{4,6},{5,13},{6,4},{7,15},{8,10},{9,1},{1... | collective-permute-start | bytes 884744 | tf_op jit(solution)/shard_map/ppermute | solution.py:1019
  90.6 3.6 %collective-permute-done.23 = f32[176,256]{1,0:T(8,128)S(1)} collective-permute-done((f32[176,256]{1,0:T(8,128)S(1)}, f32[176,256]{1,0:T(8,128)S(1)}, u32[]{:S(2)}, u32[]{:S(2)}) %collective-permute-start.23) | collective-permute-done | bytes 180256 | tf_op jit(solution)/shard_map/ppermute | solution.py:1019
  94.3 1.2 %collective-permute-start.26 = (f32[336,256]{1,0:T(8,128)S(1)}, f32[336,256]{1,0:T(8,128)S(1)}, u32[]{:S(2)}, u32[]{:S(2)}) collective-permute-start(f32[336,256]{1,0:T(8,128)S(1)} %pad_maximum_fusion.7), channel_id=1, source_target_pairs={{0,16},{1,17},{2,18},{3,19},{4,20},{5,21},{6,22},{7,23},{8,24},{9,... | collective-permute-start | bytes 1032200 | tf_op jit(solution)/shard_map/ppermute | solution.py:1019
  96.4 2.8 %collective-permute-done.27 = f32[2,144,256]{2,1,0:T(8,128)S(1)} collective-permute-done((f32[2,144,256]{2,1,0:T(8,128)S(1)}, f32[2,144,256]{2,1,0:T(8,128)S(1)}, u32[]{:S(2)}, u32[]{:S(2)}) %collective-permute-start.27) | collective-permute-done | bytes 294944 | tf_op jit(solution)/shard_map/ppermute | solution.py:1019
  99.9 1.8 %collective-permute-done.26 = f32[336,256]{1,0:T(8,128)S(1)} collective-permute-done((f32[336,256]{1,0:T(8,128)S(1)}, f32[336,256]{1,0:T(8,128)S(1)}, u32[]{:S(2)}, u32[]{:S(2)}) %collective-permute-start.26) | collective-permute-done | bytes 344096 | tf_op jit(solution)/shard_map/ppermute | solution.py:1019
  101.7 2.0 %embed_gradient.1 = f32[512,256]{1,0:T(8,128)} custom-call(f32[16,8,256]{2,1,0:T(8,128)S(1)} %fusion.9.refs_0_, f32[16,256]{1,0:T(8,128)S(1)} %slice_add_fusion.19.refs_1_), custom_call_target="tpu_custom_call" | custom-call | flops 1 | bytes 1 | tf_op jit(solution)/shard_map/embed_gradient/pallas_call | solution.py:969
  104.4 1.0 collective-permute-done.30
  105.6 3.6 %collective-permute-done.29 = f32[4,144,256]{2,1,0:T(8,128)S(1)} collective-permute-done((f32[4,144,256]{2,1,0:T(8,128)S(1)}, f32[4,144,256]{2,1,0:T(8,128)S(1)}, u32[]{:S(2)}, u32[]{:S(2)}) %collective-permute-start.29) | collective-permute-done | bytes 589856 | tf_op jit(solution)/shard_map/ppermute | solution.py:1019
  110.7 2.1 %assemble.3 = f32[9,256,256]{2,1,0:T(8,128)} custom-call(f32[8,9,16,256]{3,2,1,0:T(8,128)S(1)} %pad_maximum_fusion.2.refs_0_, f32[8,9,16,256]{3,2,1,0:T(8,128)S(1)} %bitcast.148), custom_call_target="tpu_custom_call" | custom-call | flops 1 | bytes 1 | tf_op jit(solution)/shard_map/assemble/pallas_call | solution.py:911
  112.9 2.4 %assemble.2 = (f32[256,768]{1,0:T(8,128)}, f32[256,256]{1,0:T(8,128)}, f32[9,256,256]{2,1,0:T(8,128)}) custom-call(f32[8,4,16,256]{3,2,1,0:T(8,128)S(1)} %pad_maximum_fusion.5.refs_0_, f32[8,4,16,256]{3,2,1,0:T(8,128)S(1)} %bitcast.149, f32[8,9,16,256]{3,2,1,0:T(8,128)S(1)} %pad_maximum_fusion.refs_2_, f32[8,9,16,256]{3,2,1,0:T(8,128)S(1)} %bitcast.147), custom_call_target="tpu_custom_call" | custom-call | flops 1 | bytes 1 | tf_op jit(solution)/shard_map/assemble/pallas_call | solution.py:911
  (142 shorter events, 18.0 us)
Async XLA Ops:
  4.7 15.1 %collective-permute-start.2 = (f32[264,256]{1,0:T(8,128)S(1)}, f32[264,256]{1,0:T(8,128)S(1)}, u32[]{:S(2)}, u32[]{:S(2)}) collective-permute-start(f32[264,256]{1,0:T(8,128)S(1)} %pack_spare.1), channel_id=1, source_target_pairs={{0,24},{1,25},{2,26},{3,27},{4,28},{5,29},{6,30},{7,31},{8,16},{9,... | collective-permute-start | bytes 811016 | tf_op jit(solution)/shard_map/ppermute | solution.py:1019
  8.6 12.3 %collective-permute-start.1 = (f32[264,256]{1,0:T(8,128)S(1)}, f32[264,256]{1,0:T(8,128)S(1)}, u32[]{:S(2)}, u32[]{:S(2)}) collective-permute-start(f32[264,256]{1,0:T(8,128)S(1)} %pack_spare.1), channel_id=1, source_target_pairs={{0,16},{1,17},{2,18},{3,19},{4,20},{5,21},{6,22},{7,23},{8,24},{9,... | collective-permute-start | bytes 811016 | tf_op jit(solution)/shard_map/ppermute | solution.py:1019
  9.1 12.1 %collective-permute-start = (f32[264,256]{1,0:T(8,128)S(1)}, f32[264,256]{1,0:T(8,128)S(1)}, u32[]{:S(2)}, u32[]{:S(2)}) collective-permute-start(f32[264,256]{1,0:T(8,128)S(1)} %pack_spare.1), channel_id=1, source_target_pairs={{0,8},{1,9},{2,10},{3,11},{4,12},{5,13},{6,14},{7,15},{8,0},{9,1},... | collective-permute-start | bytes 811016 | tf_op jit(solution)/shard_map/ppermute | solution.py:1019
  30.2 6.5 %collective-permute-start.5 = (f32[8,9,16,256]{3,2,1,0:T(8,128)S(1)}, f32[8,9,16,256]{3,2,1,0:T(8,128)S(1)}, u32[]{:S(2)}, u32[]{:S(2)}) collective-permute-start(f32[8,9,16,256]{3,2,1,0:T(8,128)S(1)} %get-tuple-element.99), channel_id=1, source_target_pairs={{0,1},{1,0},{2,3},{3,2},{4,5},{5,4},{6,7},{7,6},{8,9},{9,8},{10,11... | collective-permute-start | bytes 3538952 | tf_op jit(solution)/shard_map/ppermute | solution.py:1019
  30.3 6.3 %collective-permute-start.4 = (f32[8,4,16,256]{3,2,1,0:T(8,128)S(1)}, f32[8,4,16,256]{3,2,1,0:T(8,128)S(1)}, u32[]{:S(2)}, u32[]{:S(2)}) collective-permute-start(f32[8,4,16,256]{3,2,1,0:T(8,128)S(1)} %get-tuple-element.97), channel_id=1, source_target_pairs={{0,1},{1,0},{2,3},{3,2},{4,5},{5,4},{6,7},{7,6},{8,9},{9,8},{10,11... | collective-permute-start | bytes 1572872 | tf_op jit(solution)/shard_map/ppermute | solution.py:1019
  36.4 2.9 %collective-permute-start.3 = (f32[8,9,16,256]{3,2,1,0:T(8,128)S(1)}, f32[8,9,16,256]{3,2,1,0:T(8,128)S(1)}, u32[]{:S(2)}, u32[]{:S(2)}) collective-permute-start(f32[8,9,16,256]{3,2,1,0:T(8,128)S(1)} %get-tuple-element.95), channel_id=1, source_target_pairs={{0,1},{1,0},{2,3},{3,2},{4,5},{5,4},{6,7},{7,6},{8,9},{9,8},{10,11... | collective-permute-start | bytes 3538952 | tf_op jit(solution)/shard_map/ppermute | solution.py:1019
  37.0 10.0 %collective-permute-start.8 = (f32[2,2,144,256]{3,2,1,0:T(8,128)S(1)}, f32[2,2,144,256]{3,2,1,0:T(8,128)S(1)}, u32[]{:S(2)}, u32[]{:S(2)}) collective-permute-start(f32[2,2,144,256]{3,2,1,0:T(8,128)S(1)} %bitcast.209), channel_id=1, source_target_pairs={{0,8},{1,3},{2,10},{3,1},{4,12},{5,7},{6,14},{7,5},{8,0},{9,11},{1... | collective-permute-start | bytes 1769480 | tf_op jit(solution)/shard_map/ppermute | solution.py:1019
  38.6 8.4 %collective-permute-start.7 = (f32[2,2,64,256]{3,2,1,0:T(8,128)S(1)}, f32[2,2,64,256]{3,2,1,0:T(8,128)S(1)}, u32[]{:S(2)}, u32[]{:S(2)}) collective-permute-start(f32[2,2,64,256]{3,2,1,0:T(8,128)S(1)} %bitcast.215), channel_id=1, source_target_pairs={{0,16},{1,17},{2,18},{3,19},{4,20},{5,21},{6,22},{7,23},{8,24},{9,... | collective-permute-start | bytes 786440 | tf_op jit(solution)/shard_map/ppermute | solution.py:1019
  39.7 13.7 %collective-permute-start.6 = (f32[2,2,144,256]{3,2,1,0:T(8,128)S(1)}, f32[2,2,144,256]{3,2,1,0:T(8,128)S(1)}, u32[]{:S(2)}, u32[]{:S(2)}) collective-permute-start(f32[2,2,144,256]{3,2,1,0:T(8,128)S(1)} %bitcast.210), channel_id=1, source_target_pairs={{0,16},{1,3},{2,18},{3,1},{4,20},{5,7},{6,22},{7,5},{8,24},{9,11},... | collective-permute-start | bytes 1769480 | tf_op jit(solution)/shard_map/ppermute | solution.py:1019
  47.2 9.3 %collective-permute-start.11 = (f32[2,144,256]{2,1,0:T(8,128)S(1)}, f32[2,144,256]{2,1,0:T(8,128)S(1)}, u32[]{:S(2)}, u32[]{:S(2)}) collective-permute-start(f32[2,144,256]{2,1,0:T(8,128)S(1)} %get-tuple-element.107), channel_id=1, source_target_pairs={{0,16},{1,9},{2,18},{3,11},{4,20},{5,13},{6,22},{7,15},{8,24},{9,1... | collective-permute-start | bytes 884744 | tf_op jit(solution)/shard_map/ppermute | solution.py:1019
  48.5 5.7 %collective-permute-start.10 = (f32[2,64,256]{2,1,0:T(8,128)S(1)}, f32[2,64,256]{2,1,0:T(8,128)S(1)}, u32[]{:S(2)}, u32[]{:S(2)}) collective-permute-start(f32[2,64,256]{2,1,0:T(8,128)S(1)} %get-tuple-element.108), channel_id=1, source_target_pairs={{0,8},{1,3},{2,10},{3,1},{4,12},{5,7},{6,14},{7,5},{8,0},{9,11},{1... | collective-permute-start | bytes 393224 | tf_op jit(solution)/shard_map/ppermute | solution.py:1019
  53.4 6.8 %collective-permute-start.9 = (f32[2,144,256]{2,1,0:T(8,128)S(1)}, f32[2,144,256]{2,1,0:T(8,128)S(1)}, u32[]{:S(2)}, u32[]{:S(2)}) collective-permute-start(f32[2,144,256]{2,1,0:T(8,128)S(1)} %get-tuple-element.109), channel_id=1, source_target_pairs={{0,2},{1,9},{2,0},{3,11},{4,6},{5,13},{6,4},{7,15},{8,10},{9,1},{1... | collective-permute-start | bytes 884744 | tf_op jit(solution)/shard_map/ppermute | solution.py:1019
  56.5 6.0 %collective-permute-start.16 = (f32[144,256]{1,0:T(8,128)S(1)}, f32[144,256]{1,0:T(8,128)S(1)}, u32[]{:S(2)}, u32[]{:S(2)}) collective-permute-start(f32[144,256]{1,0:T(8,128)S(1)} %fusion.6), channel_id=1, source_target_pairs={{0,2},{1,17},{2,0},{3,19},{4,6},{5,21},{6,4},{7,23},{8,10},{9,25},... | collective-permute-start | bytes 442376 | tf_op jit(solution)/shard_map/ppermute | solution.py:1019
  57.0 5.5 %collective-permute-start.14 = (f32[64,256]{1,0:T(8,128)S(1)}, f32[64,256]{1,0:T(8,128)S(1)}, u32[]{:S(2)}, u32[]{:S(2)}) collective-permute-start(f32[64,256]{1,0:T(8,128)S(1)} %fusion.12), channel_id=1, source_target_pairs={{0,2},{1,9},{2,0},{3,11},{4,6},{5,13},{6,4},{7,15},{8,10},{9,1},{1... | collective-permute-start | bytes 196616 | tf_op jit(solution)/shard_map/ppermute | solution.py:1019
  60.2 5.3 %collective-permute-start.13 = (f32[144,256]{1,0:T(8,128)S(1)}, f32[144,256]{1,0:T(8,128)S(1)}, u32[]{:S(2)}, u32[]{:S(2)}) collective-permute-start(f32[144,256]{1,0:T(8,128)S(1)} %fusion.7), channel_id=1, source_target_pairs={{0,8},{1,17},{2,10},{3,19},{4,12},{5,21},{6,14},{7,23},{8,0},{9,25... | collective-permute-start | bytes 442376 | tf_op jit(solution)/shard_map/ppermute | solution.py:1019
  61.6 17.4 %collective-permute-start.12 = (f32[256,256]{1,0:T(8,128)S(1)}, f32[256,256]{1,0:T(8,128)S(1)}, u32[]{:S(2)}, u32[]{:S(2)}) collective-permute-start(f32[256,256]{1,0:T(8,128)S(1)} %slice_bitcast_fusion), channel_id=1, source_target_pairs={{0,8},{1,17},{2,10},{3,19},{4,12},{5,21},{6,14},{7,23},{8,0},{9,25... | collective-permute-start | bytes 786440 | tf_op jit(solution)/shard_map/ppermute | solution.py:1019
  62.6 16.3 %collective-permute-start.19 = (f32[144,256]{1,0:T(8,128)S(1)}, f32[144,256]{1,0:T(8,128)S(1)}, u32[]{:S(2)}, u32[]{:S(2)}) collective-permute-start(f32[144,256]{1,0:T(8,128)S(1)} %fusion.3), channel_id=1, source_target_pairs={{0,4},{1,5},{2,6},{3,7},{4,0},{5,1},{6,2},{7,3},{8,12},{9,13},{10,... | collective-permute-start | bytes 442376 | tf_op jit(solution)/shard_map/ppermute | solution.py:1019
  65.2 13.6 %collective-permute-start.18 = (f32[88,256]{1,0:T(8,128)S(1)}, f32[88,256]{1,0:T(8,128)S(1)}, u32[]{:S(2)}, u32[]{:S(2)}) collective-permute-start(f32[88,256]{1,0:T(8,128)S(1)} %pad_maximum_fusion.13), channel_id=1, source_target_pairs={{0,4},{1,5},{2,6},{3,7},{4,0},{5,1},{6,2},{7,3},{8,12},{9,13},{10,... | collective-permute-start | bytes 270344 | tf_op jit(solution)/shard_map/ppermute | solution.py:1019
  65.6 16.9 %collective-permute-start.22 = (f32[144,256]{1,0:T(8,128)S(1)}, f32[144,256]{1,0:T(8,128)S(1)}, u32[]{:S(2)}, u32[]{:S(2)}) collective-permute-start(f32[144,256]{1,0:T(8,128)S(1)} %fusion.5), channel_id=1, source_target_pairs={{0,4},{1,5},{2,6},{3,7},{4,0},{5,1},{6,2},{7,3},{8,12},{9,13},{10,... | collective-permute-start | bytes 442376 | tf_op jit(solution)/shard_map/ppermute | solution.py:1019
  78.9 4.7 %collective-permute-start.20 = (f32[96,256]{1,0:T(8,128)S(1)}, f32[96,256]{1,0:T(8,128)S(1)}, u32[]{:S(2)}, u32[]{:S(2)}) collective-permute-start(f32[96,256]{1,0:T(8,128)S(1)} %pad_maximum_fusion.12), channel_id=1, source_target_pairs={{0,2},{1,9},{2,0},{3,11},{4,6},{5,13},{6,4},{7,15},{8,10},{9,1},{1... | collective-permute-start | bytes 294920 | tf_op jit(solution)/shard_map/ppermute | solution.py:1019
  79.0 8.7 %collective-permute-start.17 = (f32[256,256]{1,0:T(8,128)S(1)}, f32[256,256]{1,0:T(8,128)S(1)}, u32[]{:S(2)}, u32[]{:S(2)}) collective-permute-start(f32[256,256]{1,0:T(8,128)S(1)} %bitcast_select_fusion), channel_id=1, source_target_pairs={{0,16},{1,9},{2,18},{3,11},{4,20},{5,13},{6,22},{7,15},{8,24},{9,1... | collective-permute-start | bytes 786440 | tf_op jit(solution)/shard_map/ppermute | solution.py:1019
  80.5 5.1 %collective-permute-start.21 = (f32[1,144,256]{2,1,0:T(8,128)S(1)}, f32[1,144,256]{2,1,0:T(8,128)S(1)}, u32[]{:S(2)}, u32[]{:S(2)}) collective-permute-start(f32[1,144,256]{2,1,0:T(8,128)S(1)} %bitcast.178), channel_id=1, source_target_pairs={{0,2},{1,17},{2,0},{3,19},{4,6},{5,21},{6,4},{7,23},{8,10},{9,25},... | collective-permute-start | bytes 442376 | tf_op jit(solution)/shard_map/ppermute | solution.py:1019
  82.6 6.8 %collective-permute-start.25 = (f32[1,144,256]{2,1,0:T(8,128)S(1)}, f32[1,144,256]{2,1,0:T(8,128)S(1)}, u32[]{:S(2)}, u32[]{:S(2)}) collective-permute-start(f32[1,144,256]{2,1,0:T(8,128)S(1)} %bitcast.183), channel_id=1, source_target_pairs={{0,8},{1,17},{2,10},{3,19},{4,12},{5,21},{6,14},{7,23},{8,0},{9,25... | collective-permute-start | bytes 442376 | tf_op jit(solution)/shard_map/ppermute | solution.py:1019
  85.7 8.6 %collective-permute-start.24 = (f32[2,144,256]{2,1,0:T(8,128)S(1)}, f32[2,144,256]{2,1,0:T(8,128)S(1)}, u32[]{:S(2)}, u32[]{:S(2)}) collective-permute-start(f32[2,144,256]{2,1,0:T(8,128)S(1)} %pad_maximum_fusion.8), channel_id=1, source_target_pairs={{0,16},{1,9},{2,18},{3,11},{4,20},{5,13},{6,22},{7,15},{8,24},{9,1... | collective-permute-start | bytes 884744 | tf_op jit(solution)/shard_map/ppermute | solution.py:1019
  86.7 7.5 %collective-permute-start.23 = (f32[176,256]{1,0:T(8,128)S(1)}, f32[176,256]{1,0:T(8,128)S(1)}, u32[]{:S(2)}, u32[]{:S(2)}) collective-permute-start(f32[176,256]{1,0:T(8,128)S(1)} %pad_maximum_fusion.10), channel_id=1, source_target_pairs={{0,8},{1,3},{2,10},{3,1},{4,12},{5,7},{6,14},{7,5},{8,0},{9,11},{1... | collective-permute-start | bytes 540680 | tf_op jit(solution)/shard_map/ppermute | solution.py:1019
  89.4 9.8 %collective-permute-start.27 = (f32[2,144,256]{2,1,0:T(8,128)S(1)}, f32[2,144,256]{2,1,0:T(8,128)S(1)}, u32[]{:S(2)}, u32[]{:S(2)}) collective-permute-start(f32[2,144,256]{2,1,0:T(8,128)S(1)} %maximum_add_fusion.1), channel_id=1, source_target_pairs={{0,2},{1,9},{2,0},{3,11},{4,6},{5,13},{6,4},{7,15},{8,10},{9,1},{1... | collective-permute-start | bytes 884744 | tf_op jit(solution)/shard_map/ppermute | solution.py:1019
  94.3 7.3 %collective-permute-start.26 = (f32[336,256]{1,0:T(8,128)S(1)}, f32[336,256]{1,0:T(8,128)S(1)}, u32[]{:S(2)}, u32[]{:S(2)}) collective-permute-start(f32[336,256]{1,0:T(8,128)S(1)} %pad_maximum_fusion.7), channel_id=1, source_target_pairs={{0,16},{1,17},{2,18},{3,19},{4,20},{5,21},{6,22},{7,23},{8,24},{9,... | collective-permute-start | bytes 1032200 | tf_op jit(solution)/shard_map/ppermute | solution.py:1019
  95.5 9.9 %collective-permute-start.30 = (f32[4,144,256]{2,1,0:T(8,128)S(1)}, f32[4,144,256]{2,1,0:T(8,128)S(1)}, u32[]{:S(2)}, u32[]{:S(2)}) collective-permute-start(f32[4,144,256]{2,1,0:T(8,128)S(1)} %pad_maximum_fusion.3), channel_id=1, source_target_pairs={{0,8},{1,3},{2,10},{3,1},{4,12},{5,7},{6,14},{7,5},{8,0},{9,11},{1... | collective-permute-start | bytes 1769480 | tf_op jit(solution)/shard_map/ppermute | solution.py:1019
  99.2 9.9 %collective-permute-start.29 = (f32[4,144,256]{2,1,0:T(8,128)S(1)}, f32[4,144,256]{2,1,0:T(8,128)S(1)}, u32[]{:S(2)}, u32[]{:S(2)}) collective-permute-start(f32[4,144,256]{2,1,0:T(8,128)S(1)} %pad_maximum_fusion.4), channel_id=1, source_target_pairs={{0,16},{1,3},{2,18},{3,1},{4,20},{5,7},{6,22},{7,5},{8,24},{9,11},... | collective-permute-start | bytes 1769480 | tf_op jit(solution)/shard_map/ppermute | solution.py:1019
  105.5 5.2 %collective-permute-start.32 = (f32[8,144,256]{2,1,0:T(8,128)S(1)}, f32[8,144,256]{2,1,0:T(8,128)S(1)}, u32[]{:S(2)}, u32[]{:S(2)}) collective-permute-start(f32[8,144,256]{2,1,0:T(8,128)S(1)} %pad_maximum_fusion.1), channel_id=1, source_target_pairs={{0,1},{1,0},{2,3},{3,2},{4,5},{5,4},{6,7},{7,6},{8,9},{9,8},{10,11... | collective-permute-start | bytes 3538952 | tf_op jit(solution)/shard_map/ppermute | solution.py:1019
  109.3 3.7 %collective-permute-start.31 = (f32[8,144,256]{2,1,0:T(8,128)S(1)}, f32[8,144,256]{2,1,0:T(8,128)S(1)}, u32[]{:S(2)}, u32[]{:S(2)}) collective-permute-start(f32[8,144,256]{2,1,0:T(8,128)S(1)} %maximum_add_fusion), channel_id=1, source_target_pairs={{0,1},{1,0},{2,3},{3,2},{4,5},{5,4},{6,7},{7,6},{8,9},{9,8},{10,11... | collective-permute-start | bytes 3538952 | tf_op jit(solution)/shard_map/ppermute | solution.py:1019
  109.4 3.6 %collective-permute-start.28 = (f32[8,64,256]{2,1,0:T(8,128)S(1)}, f32[8,64,256]{2,1,0:T(8,128)S(1)}, u32[]{:S(2)}, u32[]{:S(2)}) collective-permute-start(f32[8,64,256]{2,1,0:T(8,128)S(1)} %pad_maximum_fusion.6), channel_id=1, source_target_pairs={{0,1},{1,0},{2,3},{3,2},{4,5},{5,4},{6,7},{7,6},{8,9},{9,8},{10,11... | collective-permute-start | bytes 1572872 | tf_op jit(solution)/shard_map/ppermute | solution.py:1019
  (21 other events, 95.9 us)
